TPU v7x, 32 devices: a whole 2x2x4 slice. The times are simulated.
32 devices in a mesh: grp: 2 (over y), blk: 4 (over x, core), head: 4 (over z).
Axes of the slice: x: 2, y: 2, z: 4, core: 2. Of those that a mesh axis runs over, the one named last changes fastest.
Arguments:
- query_rows: bfloat16 [4096, 8192], P(('grp', 'blk', 'head')), parts along dimension 0, may hold values from -144 to 144
- key_rows: bfloat16 [4096, 1024], P(('grp', 'blk', 'head')), parts along dimension 0, may hold values from -6 to 6
- value_rows: bfloat16 [4096, 1024], P(('grp', 'blk', 'head')), parts along dimension 0, may hold values from -6 to 6
- placement: int32 [8], P('grp'), parts along dimension 0, may hold values from 0 to 3, as said below
- lengths: int32 [4], P('grp'), parts along dimension 0, may hold values from 1 to 512, as said below
Outputs:
- attended: bfloat16 [4096, 8192], P(('grp', 'blk', 'head')), parts along dimension 0
There are 2 independent parts, one for each index of `grp`. A program takes and returns all parts, laid end to end along the dimension named above; each array names one. Nothing has to cross between parts.
Inputs may be any that keep to these rules, and one draw needn't show every extreme that they name: `placement`: a permutation of 0 to 3. `lengths`: exactly one response has the full length 512; the others are shorter.
All inputs are finite; a program needn't handle non-finite values.
Results may differ from a plain program's by a relative error of at most 0.0033.
Values may be sent and summed in bfloat16 or wider, within the bound.
No kernel may reach another device: no remote copies, remote signals or barrier semaphores. Data moves between devices by JAX's collectives and lax.ppermute only.
A program may use at most 64 MiB of HBM per device.

v0:
```python
import math

import jax
import jax.numpy as jnp
from jax import lax
from jax.sharding import PartitionSpec as P

HD = 128


def from_behind(x, axis, by):
    count = lax.axis_size(axis)
    return lax.ppermute(x, axis, [(i, (i + by) % count) for i in range(count)])


def shards(query_rows, key_rows, value_rows, placement, lengths):
    cycle_size = lax.axis_size("blk")
    prompt_count = cycle_size // 2
    score_scale = 1.0 / math.sqrt(HD)
    query_heads, key_heads, value_heads = (
        lax.all_to_all(query_rows, "head", split_axis=1, concat_axis=0, tiled=True),
        lax.all_to_all(key_rows, "head", split_axis=1, concat_axis=0, tiled=True),
        lax.all_to_all(value_rows, "head", split_axis=1, concat_axis=0, tiled=True),
    )
    row_count = query_heads.shape[0]
    local_q = query_heads.shape[1] // HD
    local_kv = key_heads.shape[1] // HD
    head_group = local_q // local_kv
    query_stack = query_heads.reshape(row_count, local_q, HD).transpose(1, 0, 2)
    kv_stack = jnp.stack([key_heads, value_heads])
    my_index = lax.axis_index("blk")
    block_id = placement[my_index]
    is_resp = block_id >= prompt_count
    resp_slot = jnp.clip(block_id - prompt_count, 0, prompt_count - 1)
    resp_len = jnp.where(is_resp, lengths[resp_slot], row_count)
    offsets = jnp.arange(row_count, dtype=jnp.int32)
    query_pos = block_id * row_count + offsets

    def attend(carry_state, kv_block, key_id):
        key_resp = key_id >= prompt_count
        key_slot = jnp.clip(key_id - prompt_count, 0, prompt_count - 1)
        key_len = jnp.where(key_resp, lengths[key_slot], row_count)
        needed = True & jnp.where(key_resp, key_id == block_id, is_resp | (key_id <= block_id))

        def fold_block(old_state):
            key_pos = key_id * row_count + offsets
            prompt_vis = is_resp | (key_pos[None, :] <= query_pos[:, None])
            resp_vis = (
                (key_id == block_id)
                & (offsets[None, :] <= offsets[:, None])
                & (offsets[None, :] < key_len)
            )
            visible = jnp.where(key_resp, resp_vis, prompt_vis)
            key_part = kv_block[0].reshape(row_count, local_kv, HD)
            value_part = kv_block[1].reshape(row_count, local_kv, HD)

            def one_head(head_items):
                query_one, run_max, run_sum, run_acc, head_pos = head_items
                kv_index = head_pos // head_group
                key_one = lax.dynamic_index_in_dim(key_part, kv_index, 1, keepdims=False)
                value_one = lax.dynamic_index_in_dim(value_part, kv_index, 1, keepdims=False)
                scores = (
                    jnp.einsum("qd,kd->qk", query_one, key_one, preferred_element_type=jnp.float32)
                    * score_scale
                )
                scores = jnp.where(visible, scores, -jnp.inf)
                new_max = jnp.maximum(run_max, jnp.max(scores, axis=1))
                weights = jnp.exp(scores - new_max[:, None])
                factor = jnp.exp(run_max - new_max)
                new_sum = run_sum * factor + jnp.sum(weights, axis=1)
                new_acc = run_acc * factor[:, None] + jnp.dot(
                    weights.astype(jnp.bfloat16), value_one, preferred_element_type=jnp.float32
                )
                return (new_max, new_sum, new_acc)

            return lax.map(
                one_head,
                (query_stack, old_state[0], old_state[1], old_state[2], jnp.arange(local_q)),
            )

        return lax.cond(needed, fold_block, lambda old_state: old_state, carry_state)

    carry_state = (
        jnp.full((local_q, row_count), -1e30, jnp.float32),
        jnp.zeros((local_q, row_count), jnp.float32),
        jnp.zeros((local_q, row_count, HD), jnp.float32),
    )
    carry_state = attend(carry_state, kv_stack, block_id)

    def cycle_step(loop_step, carry_pair):
        kv_block, old_state = carry_pair
        kv_block = from_behind(kv_block, "blk", 1)
        source_index = (my_index - loop_step) % cycle_size
        return (kv_block, attend(old_state, kv_block, placement[source_index]))

    carry_pair = lax.fori_loop(1, cycle_size, cycle_step, (kv_stack, carry_state))
    carry_state = carry_pair[1]
    result = carry_state[2] / carry_state[1][:, :, None]
    keep_rows = jnp.logical_not(is_resp) | (offsets < resp_len)
    result = result * keep_rows[None, :, None]
    merged = result.transpose(1, 0, 2).reshape(row_count, local_q * HD).astype(jnp.bfloat16)
    return lax.all_to_all(merged, "head", split_axis=0, concat_axis=1, tiled=True)


def solution(mesh):
    placed = (
        P(("grp", "blk", "head"), None),
        P(("grp", "blk", "head"), None),
        P(("grp", "blk", "head"), None),
        P("grp"),
        P("grp"),
    )
    return jax.shard_map(
        shards,
        mesh=mesh,
        in_specs=placed,
        out_specs=P(("grp", "blk", "head"), None),
        check_vma=False,
    )
```

profile of v0, /device:TPU:3, one launch (start us, length us, event | category | flops | bytes accessed | tf_op | source)
XLA Modules:
  0.0 609.0 jit_solution(7693475962121212589)
XLA Ops:
  1.7 4.6 all-to-all-start
  7.9 5.9 all-to-all-done
  13.8 3.4 all-to-all-start.1
  17.3 3.2 copy.39
  20.4 2.4 all-to-all-done.1
  22.9 3.6 all-to-all-start.2
  31.7 42.5 %all-to-all-done.2 = bf16[128,4,2048]{2,0,1:T(8,128)(2,1)S(1)} async-done(((bf16[128,4,2048]{2,0,1:T(8,128)(2,1)}), bf16[128,4,2048]{2,0,1:T(8,128)(2,1)S(1)}, u32[]{:S(2)}, u32[]{:S(2)}) %all-to-all-start.2) | async-done | bytes 2097184 | tf_op jit(solution)/shard_map/all_to_all | solution.py:21
  76.6 94.2 %while.69 = (s32[]{:T(128)}, f32[16,512]{1,0:T(8,128)S(1)}, f32[16,512]{1,0:T(8,128)S(1)}, f32[16,512,128]{2,1,0:T(8,128)}, bf16[16,512,128]{2,1,0:T(8,128)(2,1)...) while((s32[]{:T(128)}, f32[16,512]{1,0:T(8,128)S(1)}, ...), condition=%wide.region_3.4_spmd.clone, body=%wide.region_0.3_spmd.clone.sunk | while | flops 137431056 | bytes 3838321 | solution.py:76
  170.9 394.6 %while.70 = (s32[]{:T(128)}, bf16[2,512,256]{1,2,0:T(8,128)(2,1)S(1)}, f32[16,512]{1,0:T(8,128)S(1)}, f32[16,512]{1,0:T(8,128)S(1)}, f32[16,512,128]{2,1,0:T(8,1...) while((s32[]{:T(128)}, ...), condition=%wide.region_11.12_spmd.clone.clone, body=%wide.region_4.11_spmd.clone.clone.sunk | while | flops 137760288 | bytes 16845656 | solution.py:96
  176.1 2.6 collective-permute-done
  178.7 125.6 %conditional.4 = ((f32[16,512]{1,0:T(8,128)S(1)}, f32[16,512]{1,0:T(8,128)S(1)}, f32[16,512,128]{2,1,0:T(8,128)})) conditional(s32[]{:T(128)} %convert_element_type.61, (f32[16,512]{1,0:T(8,128)S(1)}, f32[16,512]{1,0:T(8,128)S(1)}, f32[16,512,128]{2,1,0:T(8,128)}) %tuple.139, (bf16[2,512,256]{1,2,0:T(8,128)(2,1)S(1)}, pred[]{:T(512)}, s32[]{:T(128)}, ...), branch_computations={%region_5.5_spmd, %region_6.10_spmd} | conditional | flops 137760272 | bytes 13697335 | solution.py:81
  182.5 117.2 %while.68 = (s32[]{:T(128)}, f32[16,512]{1,0:T(8,128)S(1)}, f32[16,512]{1,0:T(8,128)S(1)}, f32[16,512,128]{2,1,0:T(8,128)}, f32[16,512]{1,0:T(8,128)S(1)}, /*ind...) while((s32[]{:T(128)}, f32[16,512]{1,0:T(8,128)S(1)}, ...), condition=%wide.region_10.9_spmd.clone, body=%wide.region_7.8_spmd.clone.sunk | while | flops 137758736 | bytes 4117937 | solution.py:76
  202.1 2.0 fusion.63
  224.1 2.0 fusion.63
  290.0 2.0 fusion.63
  297.3 2.0 fusion.63
  299.7 4.5 copy.65
  307.9 2.6 collective-permute-done
  310.5 2.5 collective-permute-start
  316.6 123.3 %collective-permute-done = bf16[2,512,256]{1,2,0:T(8,128)(2,1)S(1)} collective-permute-done((bf16[2,512,256]{1,2,0:T(8,128)(2,1)S(1)}, bf16[2,512,256]{1,2,0:T(8,128)(2,1)S(1)}, u32[]{:S(2)}, u32[]{:S(2)}) %collective-permute-start) | collective-permute-done | bytes 524320 | tf_op jit(solution)/shard_map/while/body/eval_jaxpr/ppermute | solution.py:13
  439.9 125.6 %conditional.4 = ((f32[16,512]{1,0:T(8,128)S(1)}, f32[16,512]{1,0:T(8,128)S(1)}, f32[16,512,128]{2,1,0:T(8,128)})) conditional(s32[]{:T(128)} %convert_element_type.61, (f32[16,512]{1,0:T(8,128)S(1)}, f32[16,512]{1,0:T(8,128)S(1)}, f32[16,512,128]{2,1,0:T(8,128)}) %tuple.139, (bf16[2,512,256]{1,2,0:T(8,128)(2,1)S(1)}, pred[]{:T(512)}, s32[]{:T(128)}, ...), branch_computations={%region_5.5_spmd, %region_6.10_spmd} | conditional | flops 137760272 | bytes 13697335 | solution.py:81
  443.7 117.2 %while.68 = (s32[]{:T(128)}, f32[16,512]{1,0:T(8,128)S(1)}, f32[16,512]{1,0:T(8,128)S(1)}, f32[16,512,128]{2,1,0:T(8,128)}, f32[16,512]{1,0:T(8,128)S(1)}, /*ind...) while((s32[]{:T(128)}, f32[16,512]{1,0:T(8,128)S(1)}, ...), condition=%wide.region_10.9_spmd.clone, body=%wide.region_7.8_spmd.clone.sunk | while | flops 137758736 | bytes 4117937 | solution.py:76
  463.3 2.0 fusion.63
  485.3 2.0 fusion.63
  551.2 2.0 fusion.63
  558.5 2.0 fusion.63
  560.9 4.5 copy.65
  565.5 3.7 fusion.40
  570.6 2.3 convert_element_type.44
  572.9 29.6 %all_to_all.64 = bf16[4,128,2048]{2,1,0:T(8,128)(2,1)S(1)} all-to-all(bf16[4,128,2048]{2,1,0:T(8,128)(2,1)} %convert_element_type.44), channel_id=1, replica_groups=mesh['grp'=2,'blk'=4,'head'=4] {'head'}, dimensions={0} | all-to-all | bytes 4194304 | tf_op jit(solution)/shard_map/all_to_all | solution.py:102
  602.4 2.5 copy.26
  604.9 4.1 copy.27
  (466 shorter events, 197.4 us)
Async XLA Ops:
  1.7 12.2 %all-to-all-start = ((bf16[128,4,256]{2,0,1:T(8,128)(2,1)}), bf16[128,4,256]{2,0,1:T(8,128)(2,1)S(1)}, u32[]{:S(2)}, u32[]{:S(2)}) async-start(bf16[128,4,256]{2,0,1:T(8,128)(2,1)} %bitcast.80), calls=%async_computation | async-start | bytes 524288 | tf_op jit(solution)/shard_map/all_to_all | solution.py:22
  13.8 9.0 %all-to-all-start.1 = ((bf16[128,4,256]{2,0,1:T(8,128)(2,1)}), bf16[128,4,256]{2,0,1:T(8,128)(2,1)S(1)}, u32[]{:S(2)}, u32[]{:S(2)}) async-start(bf16[128,4,256]{2,0,1:T(8,128)(2,1)} %bitcast.79), calls=%async_computation.1 | async-start | bytes 524288 | tf_op jit(solution)/shard_map/all_to_all | solution.py:23
  17.2 9.3 %copy-start.1 = (s32[4]{0:T(128)S(1)}, s32[4]{0:T(128)}, u32[]{:S(2)}) copy-start(s32[4]{0:T(128)} %param.16) | copy-start | bytes 52
  17.3 11.8 %copy-start.2 = (s32[2]{0:T(128)S(1)}, s32[2]{0:T(128)}, u32[]{:S(2)}) copy-start(s32[2]{0:T(128)} %param.17) | copy-start | bytes 28
  22.9 51.3 %all-to-all-start.2 = ((bf16[128,4,2048]{2,0,1:T(8,128)(2,1)}), bf16[128,4,2048]{2,0,1:T(8,128)(2,1)S(1)}, u32[]{:S(2)}, u32[]{:S(2)}) async-start(bf16[128,4,2048]{2,0,1:T(8,128)(2,1)} %bitcast.78), calls=%async_computation.2 | async-start | bytes 4194304 | tf_op jit(solution)/shard_map/all_to_all | solution.py:21
  76.6 94.3 %copy-start = (bf16[2,512,256]{1,2,0:T(8,128)(2,1)S(1)}, bf16[2,512,256]{1,2,0:T(8,128)(2,1)}, u32[]{:S(2)}) copy-start(bf16[2,512,256]{1,2,0:T(8,128)(2,1)} %pad_maximum_fusion) | copy-start | bytes 1572868
  170.9 7.8 %collective-permute-start = (bf16[2,512,256]{1,2,0:T(8,128)(2,1)S(1)}, bf16[2,512,256]{1,2,0:T(8,128)(2,1)S(1)}, u32[]{:S(2)}, u32[]{:S(2)}) collective-permute-start(bf16[2,512,256]{1,2,0:T(8,128)(2,1)S(1)} %get-tuple-element.1480), channel_id=1, source_target_pairs={{0,4},{4,8},{8,12},{12,0},{1,5},{5,9},{9,13},{13,1},{2,6},{6,10},{... | collective-permute-start | bytes 1572872 | tf_op jit(solution)/shard_map/while/body/eval_jaxpr/ppermute | solution.py:13
  304.3 6.2 %collective-permute-start = (bf16[2,512,256]{1,2,0:T(8,128)(2,1)S(1)}, bf16[2,512,256]{1,2,0:T(8,128)(2,1)S(1)}, u32[]{:S(2)}, u32[]{:S(2)}) collective-permute-start(bf16[2,512,256]{1,2,0:T(8,128)(2,1)S(1)} %get-tuple-element.1480), channel_id=1, source_target_pairs={{0,4},{4,8},{8,12},{12,0},{1,5},{5,9},{9,13},{13,1},{2,6},{6,10},{... | collective-permute-start | bytes 1572872 | tf_op jit(solution)/shard_map/while/body/eval_jaxpr/ppermute | solution.py:13
  310.5 129.4 %collective-permute-start = (bf16[2,512,256]{1,2,0:T(8,128)(2,1)S(1)}, bf16[2,512,256]{1,2,0:T(8,128)(2,1)S(1)}, u32[]{:S(2)}, u32[]{:S(2)}) collective-permute-start(bf16[2,512,256]{1,2,0:T(8,128)(2,1)S(1)} %get-tuple-element.1480), channel_id=1, source_target_pairs={{0,4},{4,8},{8,12},{12,0},{1,5},{5,9},{9,13},{13,1},{2,6},{6,10},{... | collective-permute-start | bytes 1572872 | tf_op jit(solution)/shard_map/while/body/eval_jaxpr/ppermute | solution.py:13
where the time goes:
time: 621 us; the launch traced here: 609 us
  waiting for transfers between devices  179 us (29%)
  matrix products  151 us (24%)
  loops' own time  145 us (23%)
  local copies, waits for them, and re-layouts  70.1 us (11%)
  blocking collectives  29.6 us (5%)
  starting transfers between devices  15.8 us (3%)
  other arithmetic  15.2 us (2%)
    another operation x3, loops' own time, fold_block(): lax.map(one_head, (query_stack, old_state[0], old_state[1], old_state[2],...  130 us
    ppermute x3, waiting for transfers between devices, from_behind(): return lax.ppermute(x, axis, [(i, (i + by) % count) for i in range(count)])  128 us
    dot_general x48, matrix products, one_head(): jnp.dot(weights.astype(jnp.bfloat16), value_one, preferred_element_type=j...  81.1 us
    dot_general x48, matrix products, one_head(): jnp.einsum('qd,kd->qk', query_one, key_one, preferred_element_type=jnp.fl...  70.3 us
    all_to_all x1, waiting for transfers between devices, shards(): lax.all_to_all(query_rows, 'head', split_axis=1, concat_axis=0, tiled=True)  42.5 us
    dynamic_slice x80, local copies, waits for them, and re-layouts, fold_block(): lax.map(one_head, (query_stack, old_state[0], old_state[1], old_state[2],...  30.8 us
    all_to_all x1, blocking collectives, shards(): lax.all_to_all(merged, 'head', split_axis=0, concat_axis=1, tiled=True)  29.6 us
  transfers between devices with their start and end apart: 6, of which 6 were waited for; matrix products, arithmetic and copies ran while one was open for 2% of the time, Pallas kernels for 0%

commit v1 on v0

v1 whole, which is shorter than its diff:
```python
import functools
import math

import jax
import jax.numpy as jnp
from jax import lax
from jax.experimental import pallas as pl
from jax.experimental.pallas import tpu as pltpu
from jax.sharding import PartitionSpec as P

HD = 128
CHUNKS = 2
EXP2_SCALE = math.log2(math.e) / math.sqrt(HD)


def attend_kernel(prompt_count, group, heads_per_tile, info, query, *refs):
    key_refs = refs[: prompt_count + 1]
    value_refs = refs[prompt_count + 1 : 2 * prompt_count + 2]
    out, bias = refs[-2:]
    tokens = query.shape[0]
    block_rows = key_refs[0].shape[0]
    block_id, first_offset, keep_len = info[prompt_count + 1], info[prompt_count + 2], info[prompt_count + 3]

    @pl.when(pl.program_id(0) == 0)
    def _():
        own_offset = first_offset + lax.broadcasted_iota(jnp.int32, (tokens, block_rows), 0)
        key_offset = lax.broadcasted_iota(jnp.int32, (tokens, block_rows), 1)
        bias[...] = jnp.where(key_offset <= own_offset, 0.0, -jnp.inf)

    kept = first_offset + lax.broadcasted_iota(jnp.int32, (tokens, 1), 0) < keep_len
    hidden = [jnp.where(block_id > j, 0.0, jnp.inf).astype(jnp.float32) for j in range(prompt_count)]
    rows = heads_per_tile * tokens
    for tile in range(group // heads_per_tile):
        heads = range(tile * heads_per_tile, (tile + 1) * heads_per_tile)
        query_tile = jnp.concatenate([query[:, h * HD : (h + 1) * HD] for h in heads], axis=0)
        scores = [
            lax.dot_general(query_tile, k[...], (((1,), (1,)), ((), ())), preferred_element_type=jnp.float32)
            for k in key_refs
        ]
        own = scores[prompt_count].reshape(heads_per_tile, tokens, block_rows) + bias[...][None]
        scores[prompt_count] = own.reshape(rows, block_rows)
        row_max = jnp.max(scores[prompt_count], axis=1, keepdims=True)
        for j in range(prompt_count):
            row_max = jnp.maximum(row_max, jnp.max(scores[j], axis=1, keepdims=True) - hidden[j])
        total = jnp.zeros((rows, 1), jnp.float32)
        summed = jnp.zeros((rows, HD), jnp.float32)
        for j in range(prompt_count + 1):
            shift = row_max if j == prompt_count else row_max + hidden[j]
            weights = jnp.exp2((scores[j] - shift) * EXP2_SCALE)
            total += jnp.sum(weights, axis=1, keepdims=True)
            summed += jnp.dot(weights.astype(jnp.bfloat16), value_refs[j][...], preferred_element_type=jnp.float32)
        result = summed / total
        for i, h in enumerate(heads):
            one = jnp.where(kept, result[i * tokens : (i + 1) * tokens], 0.0)
            out[:, h * HD : (h + 1) * HD] = one.astype(out.dtype)


def attend(info, query_rows, kv, chunk, chunks, prompt_count, previous):
    tokens, width = query_rows.shape
    kv_heads = kv.shape[1] // (2 * HD)
    group = width // HD // (kv_heads * chunks)
    block_rows = kv.shape[0] // (2 * prompt_count)

    def kv_spec(place, first):
        return pl.BlockSpec((block_rows, HD), lambda g, info: (info[place], first + g))

    own_spec = pl.BlockSpec((tokens, group * HD), lambda g, info: (0, chunk * kv_heads + g))
    kv_specs = [kv_spec(j, first) for first in (0, kv_heads) for j in range(prompt_count + 1)]
    in_specs, args, aliases = [own_spec, *kv_specs], [info, query_rows] + [kv] * len(kv_specs), {}
    body = functools.partial(attend_kernel, prompt_count, group, 4)
    if previous is not None:
        aliases = {len(args): 0}
        in_specs.append(pl.BlockSpec(memory_space=pl.ANY))
        args.append(previous)
    work = tokens * group * kv_heads * block_rows * (prompt_count + 1)
    return pl.pallas_call(
        body,
        grid_spec=pltpu.PrefetchScalarGridSpec(
            num_scalar_prefetch=1,
            grid=(kv_heads,),
            in_specs=in_specs,
            out_specs=own_spec,
            scratch_shapes=[pltpu.VMEM((tokens, block_rows), jnp.float32)],
        ),
        out_shape=jax.ShapeDtypeStruct(query_rows.shape, query_rows.dtype),
        input_output_aliases=aliases,
        cost_estimate=pl.CostEstimate(flops=4 * work * HD, bytes_accessed=8 << 20, transcendentals=work),
        compiler_params=pltpu.CompilerParams(vmem_limit_bytes=48 << 20),
    )(*args)


def shards(query_rows, key_rows, value_rows, placement, lengths):
    block_count = lax.axis_size("blk")
    prompt_count = block_count // 2
    tokens = query_rows.shape[0]
    my_index = lax.axis_index("blk")
    block_id = placement[my_index]
    slot = jnp.clip(block_id - prompt_count, 0, prompt_count - 1)
    block_rows = tokens * lax.axis_size("head")
    keep_len = jnp.where(block_id >= prompt_count, lengths[slot], block_rows)
    inverse = jnp.sum(
        jnp.where(placement[None, :] == jnp.arange(prompt_count)[:, None], jnp.arange(block_count)[None, :], 0), axis=1
    )
    first_offset = lax.axis_index("head") * tokens
    info = jnp.concatenate([inverse, jnp.stack([my_index, block_id, first_offset, keep_len])]).astype(jnp.int32)

    width = key_rows.shape[1] // CHUNKS
    gathered = []
    for c in range(CHUNKS):
        columns = slice(c * width, (c + 1) * width)
        packed = jnp.concatenate([key_rows[:, columns], value_rows[:, columns]], axis=1)
        gathered.append(lax.all_gather(packed, ("blk", "head"), axis=0, tiled=True))
    out = None
    for c in range(CHUNKS):
        out = attend(info, query_rows, gathered[c], c, CHUNKS, prompt_count, out)
    return out


def solution(mesh):
    rows = P(("grp", "blk", "head"), None)
    return jax.shard_map(
        shards,
        mesh=mesh,
        in_specs=(rows, rows, rows, P("grp"), P("grp")),
        out_specs=rows,
        check_vma=False,
    )
```

time: 621 us -> 136 us (0.22)
  the two profiles are of different devices: /device:TPU:3 before, /device:TPU:0 now
where the time goes in v1:
time: 136 us
  waiting for transfers between devices  86.6 us (64%)
  Pallas kernels  29.5 us (22%)
  between operations  15.2 us (11%)
  local copies, waits for them, and re-layouts  3.16 us (2%)
  other arithmetic  1.6 us (1%)
    all_gather x2, waiting for transfers between devices, shards(): gathered.append(lax.all_gather(packed, ('blk', 'head'), axis=0, tiled=True))  86.5 us
    pallas_call x2, Pallas kernels, attend(): pl.pallas_call(body, grid_spec=pltpu.PrefetchScalarGridSpec(num_scalar_pr...  29.5 us
  transfers between devices with their start and end apart: 2, of which 2 were waited for; matrix products, arithmetic and copies ran while one was open for 2% of the time, Pallas kernels for 11%

profile of v1, /device:TPU:0, one launch (start us, length us, event | category | flops | bytes accessed | tf_op | source)
XLA Modules:
  0.0 136.0 jit_solution(13764693474519609245)
XLA Ops:
  6.5 0.0 copy-start.2
  6.5 0.0 copy-start.1
  6.5 0.0 copy-start
  6.5 0.0 all-gather.5.cloned.1.call-start
  6.5 1.3 fusion.1
  7.8 0.7 pad_maximum_fusion.1
  8.6 0.0 all-gather.5.cloned.1.call-update
  8.6 0.0 all-gather.3.cloned.1.call-start
  8.6 0.8 pad_maximum_fusion
  9.4 0.0 all-gather.3.cloned.1.call-update
  9.4 0.0 copy-done.2
  9.4 0.6 dynamic_slice.6
  11.1 0.0 copy-done.1
  11.1 0.7 dynamic_slice.7
  12.4 0.1 fusion
  12.6 0.6 concatenate.9.info
  13.2 49.8 %all-gather.5.cloned.1.call-done.refs_0_.refs_1_.refs_2_.refs_3_.refs_4_.refs_5_ = bf16[2048,1024]{1,0:T(8,128)(2,1)} async-done(((bf16[128,1024]{1,0:T(8,128)(2,1)}), bf16[2048,1024]{1,0:T(8,128)(2,1)}) %all-gather.5.cloned.1.call-update) | async-done | bytes 4194320 | tf_op jit(solution)/shard_map/all_gather | solution.py:112
  63.0 0.0 copy-done
  63.0 14.7 %shard_map.55.refs_6_ = bf16[128,8192]{1,0:T(8,128)(2,1)} custom-call(s32[6]{0:T(128)S(1)} %concatenate.9.info, bf16[128,8192]{1,0:T(8,128)(2,1)S(1)} %copy-done, bf16[2048,1024]{1,0:T(8,128)(2,1)} %all-gather.5.cloned.1.call-done.refs_0_.refs_1_.refs_2_.refs_3_.refs_4_.refs_5_, ...), custom_call_target="tpu_custom_call" | custom-call | flops 3221225472 | bytes 8388608 | tf_op jit(solution)/shard_map/pallas_call | solution.py:76
  77.8 36.7 %all-gather.3.cloned.1.call-done.refs_0_.refs_1_.refs_2_.refs_3_.refs_4_.refs_5_ = bf16[2048,1024]{1,0:T(8,128)(2,1)} async-done(((bf16[128,1024]{1,0:T(8,128)(2,1)}), bf16[2048,1024]{1,0:T(8,128)(2,1)}) %all-gather.3.cloned.1.call-update) | async-done | bytes 4194320 | tf_op jit(solution)/shard_map/all_gather | solution.py:112
  114.5 14.7 %shard_map.56 = bf16[128,8192]{1,0:T(8,128)(2,1)} custom-call(s32[6]{0:T(128)S(1)} %concatenate.9.info, bf16[128,8192]{1,0:T(8,128)(2,1)S(1)} %copy-done, bf16[2048,1024]{1,0:T(8,128)(2,1)} %all-gather.3.cloned.1.call-done.refs_0_.refs_1_.refs_2_.refs_3_.refs_4_.refs_5_, ...), custom_call_target="tpu_custom_call", output_to_operand_aliasing={{}: (8, {})} | custom-call | flops 3221225472 | bytes 8388608 | tf_op jit(solution)/shard_map/pallas_call | solution.py:76
Async XLA Ops:
  6.5 2.9 %copy-start.2 = (s32[4]{0:T(128)S(1)}, s32[4]{0:T(128)}, u32[]{:S(2)}) copy-start(s32[4]{0:T(128)} %param.8) | copy-start | bytes 52
  6.5 4.6 %copy-start.1 = (s32[2]{0:T(128)S(1)}, s32[2]{0:T(128)}, u32[]{:S(2)}) copy-start(s32[2]{0:T(128)} %param.9) | copy-start | bytes 28
  6.5 56.5 %copy-start = (bf16[128,8192]{1,0:T(8,128)(2,1)S(1)}, bf16[128,8192]{1,0:T(8,128)(2,1)}, u32[]{:S(2)}) copy-start(bf16[128,8192]{1,0:T(8,128)(2,1)} %query.3) | copy-start | bytes 6291460
  6.5 56.5 %all-gather.5.cloned.1.call-start = ((), (), s32[]{:S(2)}) async-start(), calls=%async_computation.1 | async-start | bytes 4456448 | tf_op jit(solution)/shard_map/all_gather | solution.py:112
  8.6 105.9 %all-gather.3.cloned.1.call-start = ((), (), s32[]{:S(2)}) async-start(), calls=%async_computation | async-start | bytes 4456448 | tf_op jit(solution)/shard_map/all_gather | solution.py:112
Sparse Core Ops, SparseCore 0:
  9.6 53.3 all-gather.4
  65.2 49.1 all-gather.2

commit v2 on v1

v2 whole, which is shorter than its diff:
```python
import functools
import math

import jax
import jax.numpy as jnp
from jax import lax
from jax.experimental import pallas as pl
from jax.experimental.pallas import tpu as pltpu
from jax.sharding import PartitionSpec as P

HD = 128
CHUNKS = 2
CORES = 2
EXP2_SCALE = math.log2(math.e) / math.sqrt(HD)


def attend_kernel(sizes, info, query, *refs):
    prompt_count, chips, ring, group, heads_per_tile = sizes
    slots = prompt_count + 1
    pieces, (out, held, bias, sems) = refs[: chips * CORES * ring], refs[-4:]
    tokens = query.shape[0]
    block_rows = ring * tokens
    width = held.shape[2] // 2
    block_id, first_offset, keep_len = info[0], info[1], info[2]
    kv_head = pl.program_id(0)

    def place(piece, slot, hop):
        row = pl.multiple_of(info[3 + slots + hop], tokens)
        return pltpu.make_async_copy(piece, held.at[slot, pl.ds(row, tokens)], sems.at[slot, hop])

    @pl.when(kv_head == 0)
    def _():
        for slot in range(slots):
            for source in range(chips * CORES):

                @pl.when(info[3 + slot] == source)
                def _():
                    for hop in range(ring):
                        place(pieces[source * ring + hop], slot, hop).start()

        own_offset = first_offset + lax.broadcasted_iota(jnp.int32, (tokens, block_rows), 0)
        key_offset = lax.broadcasted_iota(jnp.int32, (tokens, block_rows), 1)
        bias[...] = jnp.where(key_offset <= own_offset, 0.0, -jnp.inf)
        for slot in range(slots):
            for hop in range(ring):
                place(pieces[0], slot, hop).wait()

    kept = first_offset + lax.broadcasted_iota(jnp.int32, (tokens, 1), 0) < keep_len
    hidden = [jnp.where(block_id > j, 0.0, jnp.inf).astype(jnp.float32) for j in range(prompt_count)]
    rows = heads_per_tile * tokens
    column = pl.multiple_of(kv_head * HD, HD)
    keys = [held[j, :, pl.ds(column, HD)] for j in range(slots)]
    values = [held[j, :, pl.ds(pl.multiple_of(width + column, HD), HD)] for j in range(slots)]
    for tile in range(group // heads_per_tile):
        heads = range(tile * heads_per_tile, (tile + 1) * heads_per_tile)
        query_tile = jnp.concatenate([query[:, h * HD : (h + 1) * HD] for h in heads], axis=0)
        scores = [
            lax.dot_general(query_tile, k, (((1,), (1,)), ((), ())), preferred_element_type=jnp.float32) for k in keys
        ]
        own = scores[prompt_count].reshape(heads_per_tile, tokens, block_rows) + bias[...][None]
        scores[prompt_count] = own.reshape(rows, block_rows)
        row_max = jnp.max(scores[prompt_count], axis=1, keepdims=True)
        for j in range(prompt_count):
            row_max = jnp.maximum(row_max, jnp.max(scores[j], axis=1, keepdims=True) - hidden[j])
        total = jnp.zeros((rows, 1), jnp.float32)
        summed = jnp.zeros((rows, HD), jnp.float32)
        for j in range(slots):
            shift = row_max if j == prompt_count else row_max + hidden[j]
            weights = jnp.exp2((scores[j] - shift) * EXP2_SCALE)
            total += jnp.sum(weights, axis=1, keepdims=True)
            summed += jnp.dot(weights.astype(jnp.bfloat16), values[j], preferred_element_type=jnp.float32)
        result = summed / total
        for i, h in enumerate(heads):
            one = jnp.where(kept, result[i * tokens : (i + 1) * tokens], 0.0)
            out[:, h * HD : (h + 1) * HD] = one.astype(out.dtype)


def attend(info, query_rows, pieces, chunk, sizes, previous):
    prompt_count, chips, ring, group, _ = sizes
    tokens, width = query_rows.shape
    piece_width = pieces[0].shape[1]
    kv_heads = piece_width // (2 * HD)
    slots = prompt_count + 1
    own_spec = pl.BlockSpec((tokens, group * HD), lambda g, info: (0, chunk * kv_heads + g))
    whole = pl.BlockSpec(memory_space=pl.ANY)
    in_specs, args, aliases = [own_spec] + [whole] * len(pieces), [info, query_rows, *pieces], {}
    if previous is not None:
        aliases = {len(args): 0}
        in_specs.append(whole)
        args.append(previous)
    work = tokens * group * kv_heads * ring * tokens * slots
    return pl.pallas_call(
        functools.partial(attend_kernel, sizes),
        grid_spec=pltpu.PrefetchScalarGridSpec(
            num_scalar_prefetch=1,
            grid=(kv_heads,),
            in_specs=in_specs,
            out_specs=own_spec,
            scratch_shapes=[
                pltpu.VMEM((slots, ring * tokens, piece_width), jnp.bfloat16),
                pltpu.VMEM((tokens, ring * tokens), jnp.float32),
                pltpu.SemaphoreType.DMA((slots, ring)),
            ],
        ),
        out_shape=jax.ShapeDtypeStruct(query_rows.shape, query_rows.dtype),
        input_output_aliases=aliases,
        cost_estimate=pl.CostEstimate(flops=4 * work * HD, bytes_accessed=8 << 20, transcendentals=work),
        compiler_params=pltpu.CompilerParams(vmem_limit_bytes=48 << 20),
    )(*args)


def gather_pieces(own, chips):
    ring, blocks = lax.axis_size("head"), chips * CORES
    column = [own]
    for _ in range(ring - 1):
        column.append(lax.ppermute(column[-1], "head", [(i, (i + 1) % ring) for i in range(ring)]))
    planes = [column]
    for _ in range(chips - 1):
        planes.append(
            [lax.ppermute(x, "blk", [(i, (i + CORES) % blocks) for i in range(blocks)]) for x in planes[-1]]
        )
    pieces = []
    for plane in planes:
        pieces += plane
        pieces += [lax.ppermute(x, "blk", [(i, i ^ 1) for i in range(blocks)]) for x in plane]
    return pieces


def shards(query_rows, key_rows, value_rows, placement, lengths):
    block_count = lax.axis_size("blk")
    ring = lax.axis_size("head")
    prompt_count = block_count // 2
    chips = block_count // CORES
    tokens = query_rows.shape[0]
    my_index = lax.axis_index("blk")
    my_head = lax.axis_index("head")
    block_id = placement[my_index]
    slot = jnp.clip(block_id - prompt_count, 0, prompt_count - 1)
    keep_len = jnp.where(block_id >= prompt_count, lengths[slot], ring * tokens)
    inverse = jnp.sum(
        jnp.where(placement[None, :] == jnp.arange(prompt_count)[:, None], jnp.arange(block_count)[None, :], 0), axis=1
    )
    chips_back = (my_index // CORES - inverse // CORES) % chips
    source = chips_back * CORES + (my_index + inverse) % CORES
    rows = (my_head - jnp.arange(ring)) % ring * tokens
    fixed = jnp.stack([block_id, my_head * tokens, keep_len])
    info = jnp.concatenate([fixed, source, jnp.zeros((1,), jnp.int32), rows]).astype(jnp.int32)

    group = query_rows.shape[1] // key_rows.shape[1]
    sizes = (prompt_count, chips, ring, group, 4)
    width = key_rows.shape[1] // CHUNKS
    pieces = []
    for c in range(CHUNKS):
        columns = slice(c * width, (c + 1) * width)
        packed = jnp.concatenate([key_rows[:, columns], value_rows[:, columns]], axis=1)
        pieces.append(gather_pieces(packed, chips))
    out = None
    for c in range(CHUNKS):
        out = attend(info, query_rows, pieces[c], c, sizes, out)
    return out


def solution(mesh):
    rows = P(("grp", "blk", "head"), None)
    return jax.shard_map(
        shards,
        mesh=mesh,
        in_specs=(rows, rows, rows, P("grp"), P("grp")),
        out_specs=rows,
        check_vma=False,
    )
```

time: 136 us -> 91.1 us (0.67)
  waiting for transfers between devices: 86.6 us -> 29 us
  starting transfers between devices: 0.04 us -> 21.2 us
  between operations: 15.2 us -> 2.04 us
  local copies, waits for them, and re-layouts: 3.16 us -> 7.14 us
  Pallas kernels: 29.5 us -> 31.3 us
  other arithmetic: 1.6 us -> 0.18 us
    all_gather x2 -> x0, waiting for transfers between devices: 86.5 us -> none  [shards(): gathered.append(lax.all_gather(packed, ('blk', 'head'), axis=0, tiled=True))]
    ppermute x0 -> x30, waiting for transfers between devices: none -> 29 us  [the longest x6 20.3 us: gather_pieces(): lax.ppermute(column[-1], 'head', [(i, (i + 1) % ring) for i in range(ring)])]
    ppermute x0 -> x30, starting transfers between devices: none -> 21.2 us  [the longest x8 10.4 us: gather_pieces(): lax.ppermute(x, 'blk', [(i, (i + CORES) % blocks) for i in range(blocks)])]
    unnamed x6 -> x16, local copies, waits for them, and re-layouts: 0.01 us -> 4.01 us
    pallas_call x2, Pallas kernels: 29.5 us -> 31.3 us  [attend(): pl.pallas_call(functools.partial(attend_kernel, sizes), grid_spec=pltpu.P...]
    concatenate x2, other arithmetic: 1.48 us -> 0.04 us  [shards(): jnp.concatenate([key_rows[:, columns], value_rows[:, columns]], axis=1)]
  transfers between devices with their start and end apart: 2 -> 30, of which waited for: 2 -> 12; matrix products, arithmetic and copies ran while one was open for 2% -> 2% of each run, Pallas kernels for 11% -> 17%
where the time goes in v2:
time: 91.1 us; the launch traced here: 90.8 us
  Pallas kernels  31.3 us (34%)
  waiting for transfers between devices  29 us (32%)
  starting transfers between devices  21.2 us (23%)
  local copies, waits for them, and re-layouts  7.14 us (8%)
  between operations  2.04 us (2%)
    pallas_call x2, Pallas kernels, attend(): pl.pallas_call(functools.partial(attend_kernel, sizes), grid_spec=pltpu.P...  31.3 us
    ppermute x6, waiting for transfers between devices, gather_pieces(): lax.ppermute(column[-1], 'head', [(i, (i + 1) % ring) for i in range(ring)])  20.3 us
    ppermute x8, starting transfers between devices, gather_pieces(): lax.ppermute(x, 'blk', [(i, (i + CORES) % blocks) for i in range(blocks)])  10.4 us
    ppermute x8, waiting for transfers between devices, gather_pieces(): lax.ppermute(x, 'blk', [(i, (i + CORES) % blocks) for i in range(blocks)])  8.59 us
    ppermute x6, starting transfers between devices, gather_pieces(): lax.ppermute(column[-1], 'head', [(i, (i + 1) % ring) for i in range(ring)])  8.08 us
    unnamed x16, local copies, waits for them, and re-layouts  4.01 us
    ppermute x16, starting transfers between devices, gather_pieces(): lax.ppermute(x, 'blk', [(i, i ^ 1) for i in range(blocks)])  2.73 us
  transfers between devices with their start and end apart: 30, of which 12 were waited for; matrix products, arithmetic and copies ran while one was open for 2% of the time, Pallas kernels for 17%

profile of v2, /device:TPU:0, one launch (start us, length us, event | category | flops | bytes accessed | tf_op | source)
XLA Modules:
  0.0 90.8 jit_solution(10552558159640138216)
XLA Ops:
  0.0 1.2 %fusion.7 = (bf16[128,512]{1,0:T(8,128)(2,1)S(1)}, bf16[128,512]{1,0:T(8,128)(2,1)S(1)}, bf16[128,512]{1,0:T(8,128)(2,1)S(1)}, bf16[128,512]{1,0:T(8,128)(2,1)S(1)}) fusion(bf16[128,1024]{1,0:T(8,128)(2,1)} %param.6, bf16[128,1024]{1,0:T(8,128)(2,1)} %param.7), kind=kLoop, calls=%fused_computation.23 | loop fusion | bytes 1048576 | tf_op jit(solution)/shard_map/slice | solution.py:155
  1.2 3.1 %collective-permute-start.15 = (bf16[128,1024]{1,0:T(8,128)(2,1)S(1)}, bf16[128,1024]{1,0:T(8,128)(2,1)S(1)}, u32[]{:S(2)}, u32[]{:S(2)}) collective-permute-start(bf16[128,1024]{1,0:T(8,128)(2,1)S(1)} %pad_maximum_fusion.1.refs_0_), channel_id=1, source_target_pairs={{0,1},{1,2},{2,3},{3,0},{4,5},{5,6},{6,7},{7,4},{8,9},{9,10},{10,1... | collective-permute-start | bytes 786440 | tf_op jit(solution)/shard_map/ppermute | solution.py:116
  4.3 1.5 %collective-permute-start.22 = (bf16[128,1024]{1,0:T(8,128)(2,1)S(1)}, bf16[128,1024]{1,0:T(8,128)(2,1)S(1)}, u32[]{:S(2)}, u32[]{:S(2)}) collective-permute-start(bf16[128,1024]{1,0:T(8,128)(2,1)S(1)} %pad_maximum_fusion.1.refs_0_), channel_id=1, source_target_pairs={{0,8},{4,12},{8,0},{12,4},{1,9},{5,13},{9,1},{13,5},{2,10},{6,14},... | collective-permute-start | bytes 786440 | tf_op jit(solution)/shard_map/ppermute | solution.py:120
  5.8 1.6 %collective-permute-start = (bf16[128,1024]{1,0:T(8,128)(2,1)S(1)}, bf16[128,1024]{1,0:T(8,128)(2,1)S(1)}, u32[]{:S(2)}, u32[]{:S(2)}) collective-permute-start(bf16[128,1024]{1,0:T(8,128)(2,1)S(1)} %pad_maximum_fusion.refs_0_), channel_id=1, source_target_pairs={{0,1},{1,2},{2,3},{3,0},{4,5},{5,6},{6,7},{7,4},{8,9},{9,10},{10,1... | collective-permute-start | bytes 786440 | tf_op jit(solution)/shard_map/ppermute | solution.py:116
  7.4 0.5 collective-permute-start.7
  8.0 5.5 %collective-permute-done.15.refs_1_ = bf16[128,1024]{1,0:T(8,128)(2,1)S(1)} collective-permute-done((bf16[128,1024]{1,0:T(8,128)(2,1)S(1)}, bf16[128,1024]{1,0:T(8,128)(2,1)S(1)}, u32[]{:S(2)}, u32[]{:S(2)}) %collective-permute-start.15) | collective-permute-done | bytes 262176 | tf_op jit(solution)/shard_map/ppermute | solution.py:116
  13.5 1.6 %collective-permute-start.16 = (bf16[128,1024]{1,0:T(8,128)(2,1)S(1)}, bf16[128,1024]{1,0:T(8,128)(2,1)S(1)}, u32[]{:S(2)}, u32[]{:S(2)}) collective-permute-start(bf16[128,1024]{1,0:T(8,128)(2,1)S(1)} %collective-permute-done.15.refs_1_), channel_id=1, source_target_pairs={{0,1},{1,2},{2,3},{3,0},{4,5},{5,6},{6,7},{7,4},{8,9},{9,10},{10,1... | collective-permute-start | bytes 786440 | tf_op jit(solution)/shard_map/ppermute | solution.py:116
  15.1 1.5 %collective-permute-start.23 = (bf16[128,1024]{1,0:T(8,128)(2,1)S(1)}, bf16[128,1024]{1,0:T(8,128)(2,1)S(1)}, u32[]{:S(2)}, u32[]{:S(2)}) collective-permute-start(bf16[128,1024]{1,0:T(8,128)(2,1)S(1)} %collective-permute-done.15.refs_1_), channel_id=1, source_target_pairs={{0,8},{4,12},{8,0},{12,4},{1,9},{5,13},{9,1},{13,5},{2,10},{6,14},... | collective-permute-start | bytes 786440 | tf_op jit(solution)/shard_map/ppermute | solution.py:120
  16.6 1.6 %collective-permute-done.refs_1_ = bf16[128,1024]{1,0:T(8,128)(2,1)S(1)} collective-permute-done((bf16[128,1024]{1,0:T(8,128)(2,1)S(1)}, bf16[128,1024]{1,0:T(8,128)(2,1)S(1)}, u32[]{:S(2)}, u32[]{:S(2)}) %collective-permute-start) | collective-permute-done | bytes 262176 | tf_op jit(solution)/shard_map/ppermute | solution.py:116
  18.7 1.8 %collective-permute-start.1 = (bf16[128,1024]{1,0:T(8,128)(2,1)S(1)}, bf16[128,1024]{1,0:T(8,128)(2,1)S(1)}, u32[]{:S(2)}, u32[]{:S(2)}) collective-permute-start(bf16[128,1024]{1,0:T(8,128)(2,1)S(1)} %collective-permute-done.refs_1_), channel_id=1, source_target_pairs={{0,1},{1,2},{2,3},{3,0},{4,5},{5,6},{6,7},{7,4},{8,9},{9,10},{10,1... | collective-permute-start | bytes 786440 | tf_op jit(solution)/shard_map/ppermute | solution.py:116
  20.5 3.8 %collective-permute-done.16.refs_2_ = bf16[128,1024]{1,0:T(8,128)(2,1)S(1)} collective-permute-done((bf16[128,1024]{1,0:T(8,128)(2,1)S(1)}, bf16[128,1024]{1,0:T(8,128)(2,1)S(1)}, u32[]{:S(2)}, u32[]{:S(2)}) %collective-permute-start.16) | collective-permute-done | bytes 262176 | tf_op jit(solution)/shard_map/ppermute | solution.py:116
  24.3 1.8 %collective-permute-start.8 = (bf16[128,1024]{1,0:T(8,128)(2,1)S(1)}, bf16[128,1024]{1,0:T(8,128)(2,1)S(1)}, u32[]{:S(2)}, u32[]{:S(2)}) collective-permute-start(bf16[128,1024]{1,0:T(8,128)(2,1)S(1)} %collective-permute-done.refs_1_), channel_id=1, source_target_pairs={{0,8},{4,12},{8,0},{12,4},{1,9},{5,13},{9,1},{13,5},{2,10},{6,14},... | collective-permute-start | bytes 786440 | tf_op jit(solution)/shard_map/ppermute | solution.py:120
  26.1 0.7 copy-done
  27.3 0.7 copy-done.4
  28.0 1.6 %collective-permute-done.1.refs_2_ = bf16[128,1024]{1,0:T(8,128)(2,1)S(1)} collective-permute-done((bf16[128,1024]{1,0:T(8,128)(2,1)S(1)}, bf16[128,1024]{1,0:T(8,128)(2,1)S(1)}, u32[]{:S(2)}, u32[]{:S(2)}) %collective-permute-start.1) | collective-permute-done | bytes 262176 | tf_op jit(solution)/shard_map/ppermute | solution.py:116
  29.6 1.7 %collective-permute-start.24 = (bf16[128,1024]{1,0:T(8,128)(2,1)S(1)}, bf16[128,1024]{1,0:T(8,128)(2,1)}, u32[]{:S(2)}, u32[]{:S(2)}) collective-permute-start(bf16[128,1024]{1,0:T(8,128)(2,1)S(1)} %collective-permute-done.16.refs_2_), channel_id=1, source_target_pairs={{0,8},{4,12},{8,0},{12,4},{1,9},{5,13},{9,1},{13,5},{2,10},{6,14},... | collective-permute-start | bytes 786440 | tf_op jit(solution)/shard_map/ppermute | solution.py:120
  31.3 0.6 collective-permute-done.8.refs_9_
  32.4 0.7 copy-done.2
  33.1 5.4 %collective-permute-done.17.refs_3_ = bf16[128,1024]{1,0:T(8,128)(2,1)} collective-permute-done((bf16[128,1024]{1,0:T(8,128)(2,1)S(1)}, bf16[128,1024]{1,0:T(8,128)(2,1)}, u32[]{:S(2)}, u32[]{:S(2)}) %collective-permute-start.17) | collective-permute-done | bytes 262176 | tf_op jit(solution)/shard_map/ppermute | solution.py:116
  38.7 2.1 %collective-permute-start.9 = (bf16[128,1024]{1,0:T(8,128)(2,1)S(1)}, bf16[128,1024]{1,0:T(8,128)(2,1)}, u32[]{:S(2)}, u32[]{:S(2)}) collective-permute-start(bf16[128,1024]{1,0:T(8,128)(2,1)S(1)} %collective-permute-done.1.refs_2_), channel_id=1, source_target_pairs={{0,8},{4,12},{8,0},{12,4},{1,9},{5,13},{9,1},{13,5},{2,10},{6,14},... | collective-permute-start | bytes 786440 | tf_op jit(solution)/shard_map/ppermute | solution.py:120
  41.3 2.4 %collective-permute-done.2.refs_3_ = bf16[128,1024]{1,0:T(8,128)(2,1)} collective-permute-done((bf16[128,1024]{1,0:T(8,128)(2,1)S(1)}, bf16[128,1024]{1,0:T(8,128)(2,1)}, u32[]{:S(2)}, u32[]{:S(2)}) %collective-permute-start.2) | collective-permute-done | bytes 262176 | tf_op jit(solution)/shard_map/ppermute | solution.py:116
  43.7 1.2 %collective-permute-start.10 = (bf16[128,1024]{1,0:T(8,128)(2,1)}, bf16[128,1024]{1,0:T(8,128)(2,1)}, u32[]{:S(2)}, u32[]{:S(2)}) collective-permute-start(bf16[128,1024]{1,0:T(8,128)(2,1)} %collective-permute-done.2.refs_3_), channel_id=1, source_target_pairs={{0,8},{4,12},{8,0},{12,4},{1,9},{5,13},{9,1},{13,5},{2,10},{6,14},... | collective-permute-start | bytes 786440 | tf_op jit(solution)/shard_map/ppermute | solution.py:120
  45.0 3.1 %collective-permute-done.25.refs_11_ = bf16[128,1024]{1,0:T(8,128)(2,1)} collective-permute-done((bf16[128,1024]{1,0:T(8,128)(2,1)}, bf16[128,1024]{1,0:T(8,128)(2,1)}, u32[]{:S(2)}, u32[]{:S(2)}) %collective-permute-start.25) | collective-permute-done | bytes 262176 | tf_op jit(solution)/shard_map/ppermute | solution.py:120
  48.1 0.6 dynamic_slice.6
  50.0 0.7 dynamic_slice.7
  51.4 0.7 concatenate.9.info
  52.0 1.7 %collective-permute-done.9.refs_10_ = bf16[128,1024]{1,0:T(8,128)(2,1)} collective-permute-done((bf16[128,1024]{1,0:T(8,128)(2,1)S(1)}, bf16[128,1024]{1,0:T(8,128)(2,1)}, u32[]{:S(2)}, u32[]{:S(2)}) %collective-permute-start.9) | collective-permute-done | bytes 262176 | tf_op jit(solution)/shard_map/ppermute | solution.py:120
  54.3 2.7 %collective-permute-done.10.refs_11_ = bf16[128,1024]{1,0:T(8,128)(2,1)} collective-permute-done((bf16[128,1024]{1,0:T(8,128)(2,1)}, bf16[128,1024]{1,0:T(8,128)(2,1)}, u32[]{:S(2)}, u32[]{:S(2)}) %collective-permute-start.10) | collective-permute-done | bytes 262176 | tf_op jit(solution)/shard_map/ppermute | solution.py:120
  57.5 0.9 %copy-done.1 = bf16[128,1024]{1,0:T(8,128)(2,1)S(1)} copy-done((bf16[128,1024]{1,0:T(8,128)(2,1)S(1)}, bf16[128,1024]{1,0:T(8,128)(2,1)}, u32[]{:S(2)}) %copy-start.1) | copy-done | bytes 262168
  58.5 0.9 %copy-done.5 = bf16[128,1024]{1,0:T(8,128)(2,1)S(1)} copy-done((bf16[128,1024]{1,0:T(8,128)(2,1)S(1)}, bf16[128,1024]{1,0:T(8,128)(2,1)}, u32[]{:S(2)}) %copy-start.5) | copy-done | bytes 262168
  59.4 15.6 %shard_map.55.refs_16_ = bf16[128,8192]{1,0:T(8,128)(2,1)} custom-call(s32[10]{0:T(128)S(1)} %concatenate.9.info, bf16[128,8192]{1,0:T(8,128)(2,1)} %query.3, bf16[128,1024]{1,0:T(8,128)(2,1)S(1)} %pad_maximum_fusion.1.refs_0_, bf16[128,1024]{1,0:T(8,128)(2,1)S(1)} %collective-permute-done.15.refs_1_, bf16[128,1024]{1,0:T(8,128)(2,1)S(1)} %collective-permute-done.16.refs_2_, ...), custom_call_target="tpu_custom_call" | custom-call | flops 3221225472 | bytes 8388608 | tf_op jit(solution)/shard_map/pallas_call | solution.py:92
  75.2 15.6 %shard_map.56 = bf16[128,8192]{1,0:T(8,128)(2,1)} custom-call(s32[10]{0:T(128)S(1)} %concatenate.9.info, bf16[128,8192]{1,0:T(8,128)(2,1)} %query.3, bf16[128,1024]{1,0:T(8,128)(2,1)S(1)} %pad_maximum_fusion.refs_0_, bf16[128,1024]{1,0:T(8,128)(2,1)S(1)} %collective-permute-done.refs_1_, ...), custom_call_target="tpu_custom_call", output_to_operand_aliasing={{}: (18, {})} | custom-call | flops 3221225472 | bytes 8388608 | tf_op jit(solution)/shard_map/pallas_call | solution.py:92
  (55 shorter events, 3.5 us)
Async XLA Ops:
  0.0 38.6 %copy-start.6 = (s32[4]{0:T(128)S(1)}, s32[4]{0:T(128)}, u32[]{:S(2)}) copy-start(s32[4]{0:T(128)} %param.8) | copy-start | bytes 52
  0.0 50.0 %copy-start.7 = (s32[2]{0:T(128)S(1)}, s32[2]{0:T(128)}, u32[]{:S(2)}) copy-start(s32[2]{0:T(128)} %param.9) | copy-start | bytes 28
  1.2 12.2 %collective-permute-start.15 = (bf16[128,1024]{1,0:T(8,128)(2,1)S(1)}, bf16[128,1024]{1,0:T(8,128)(2,1)S(1)}, u32[]{:S(2)}, u32[]{:S(2)}) collective-permute-start(bf16[128,1024]{1,0:T(8,128)(2,1)S(1)} %pad_maximum_fusion.1.refs_0_), channel_id=1, source_target_pairs={{0,1},{1,2},{2,3},{3,0},{4,5},{5,6},{6,7},{7,4},{8,9},{9,10},{10,1... | collective-permute-start | bytes 786440 | tf_op jit(solution)/shard_map/ppermute | solution.py:116
  4.3 9.2 %collective-permute-start.22 = (bf16[128,1024]{1,0:T(8,128)(2,1)S(1)}, bf16[128,1024]{1,0:T(8,128)(2,1)S(1)}, u32[]{:S(2)}, u32[]{:S(2)}) collective-permute-start(bf16[128,1024]{1,0:T(8,128)(2,1)S(1)} %pad_maximum_fusion.1.refs_0_), channel_id=1, source_target_pairs={{0,8},{4,12},{8,0},{12,4},{1,9},{5,13},{9,1},{13,5},{2,10},{6,14},... | collective-permute-start | bytes 786440 | tf_op jit(solution)/shard_map/ppermute | solution.py:120
  5.8 9.3 %collective-permute-start.18 = (bf16[128,1024]{1,0:T(8,128)(2,1)S(1)}, bf16[128,1024]{1,0:T(8,128)(2,1)S(1)}, u32[]{:S(2)}, u32[]{:S(2)}) collective-permute-start(bf16[128,1024]{1,0:T(8,128)(2,1)S(1)} %pad_maximum_fusion.1.refs_0_), channel_id=1, source_target_pairs={{0,4},{4,0},{8,12},{12,8},{1,5},{5,1},{9,13},{13,9},{2,6},{6,2},{1... | collective-permute-start | bytes 786440 | tf_op jit(solution)/shard_map/ppermute | solution.py:125
  5.8 12.4 %collective-permute-start = (bf16[128,1024]{1,0:T(8,128)(2,1)S(1)}, bf16[128,1024]{1,0:T(8,128)(2,1)S(1)}, u32[]{:S(2)}, u32[]{:S(2)}) collective-permute-start(bf16[128,1024]{1,0:T(8,128)(2,1)S(1)} %pad_maximum_fusion.refs_0_), channel_id=1, source_target_pairs={{0,1},{1,2},{2,3},{3,0},{4,5},{5,6},{6,7},{7,4},{8,9},{9,10},{10,1... | collective-permute-start | bytes 786440 | tf_op jit(solution)/shard_map/ppermute | solution.py:116
  7.4 11.2 %collective-permute-start.7 = (bf16[128,1024]{1,0:T(8,128)(2,1)S(1)}, bf16[128,1024]{1,0:T(8,128)(2,1)S(1)}, u32[]{:S(2)}, u32[]{:S(2)}) collective-permute-start(bf16[128,1024]{1,0:T(8,128)(2,1)S(1)} %pad_maximum_fusion.refs_0_), channel_id=1, source_target_pairs={{0,8},{4,12},{8,0},{12,4},{1,9},{5,13},{9,1},{13,5},{2,10},{6,14},... | collective-permute-start | bytes 786440 | tf_op jit(solution)/shard_map/ppermute | solution.py:120
  13.4 5.3 %collective-permute-start.3 = (bf16[128,1024]{1,0:T(8,128)(2,1)S(1)}, bf16[128,1024]{1,0:T(8,128)(2,1)S(1)}, u32[]{:S(2)}, u32[]{:S(2)}) collective-permute-start(bf16[128,1024]{1,0:T(8,128)(2,1)S(1)} %pad_maximum_fusion.refs_0_), channel_id=1, source_target_pairs={{0,4},{4,0},{8,12},{12,8},{1,5},{5,1},{9,13},{13,9},{2,6},{6,2},{1... | collective-permute-start | bytes 786440 | tf_op jit(solution)/shard_map/ppermute | solution.py:125
  13.5 10.8 %collective-permute-start.16 = (bf16[128,1024]{1,0:T(8,128)(2,1)S(1)}, bf16[128,1024]{1,0:T(8,128)(2,1)S(1)}, u32[]{:S(2)}, u32[]{:S(2)}) collective-permute-start(bf16[128,1024]{1,0:T(8,128)(2,1)S(1)} %collective-permute-done.15.refs_1_), channel_id=1, source_target_pairs={{0,1},{1,2},{2,3},{3,0},{4,5},{5,6},{6,7},{7,4},{8,9},{9,10},{10,1... | collective-permute-start | bytes 786440 | tf_op jit(solution)/shard_map/ppermute | solution.py:116
  15.1 11.0 %collective-permute-start.23 = (bf16[128,1024]{1,0:T(8,128)(2,1)S(1)}, bf16[128,1024]{1,0:T(8,128)(2,1)S(1)}, u32[]{:S(2)}, u32[]{:S(2)}) collective-permute-start(bf16[128,1024]{1,0:T(8,128)(2,1)S(1)} %collective-permute-done.15.refs_1_), channel_id=1, source_target_pairs={{0,8},{4,12},{8,0},{12,4},{1,9},{5,13},{9,1},{13,5},{2,10},{6,14},... | collective-permute-start | bytes 786440 | tf_op jit(solution)/shard_map/ppermute | solution.py:120
  18.2 7.9 %collective-permute-start.19 = (bf16[128,1024]{1,0:T(8,128)(2,1)S(1)}, bf16[128,1024]{1,0:T(8,128)(2,1)S(1)}, u32[]{:S(2)}, u32[]{:S(2)}) collective-permute-start(bf16[128,1024]{1,0:T(8,128)(2,1)S(1)} %collective-permute-done.15.refs_1_), channel_id=1, source_target_pairs={{0,4},{4,0},{8,12},{12,8},{1,5},{5,1},{9,13},{13,9},{2,6},{6,2},{1... | collective-permute-start | bytes 786440 | tf_op jit(solution)/shard_map/ppermute | solution.py:125
  18.6 8.7 %collective-permute-start.26 = (bf16[128,1024]{1,0:T(8,128)(2,1)S(1)}, bf16[128,1024]{1,0:T(8,128)(2,1)S(1)}, u32[]{:S(2)}, u32[]{:S(2)}) collective-permute-start(bf16[128,1024]{1,0:T(8,128)(2,1)S(1)} %collective-permute-done.22.refs_8_), channel_id=1, source_target_pairs={{0,4},{4,0},{8,12},{12,8},{1,5},{5,1},{9,13},{13,9},{2,6},{6,2},{1... | collective-permute-start | bytes 786440 | tf_op jit(solution)/shard_map/ppermute | solution.py:125
  18.7 10.8 %collective-permute-start.1 = (bf16[128,1024]{1,0:T(8,128)(2,1)S(1)}, bf16[128,1024]{1,0:T(8,128)(2,1)S(1)}, u32[]{:S(2)}, u32[]{:S(2)}) collective-permute-start(bf16[128,1024]{1,0:T(8,128)(2,1)S(1)} %collective-permute-done.refs_1_), channel_id=1, source_target_pairs={{0,1},{1,2},{2,3},{3,0},{4,5},{5,6},{6,7},{7,4},{8,9},{9,10},{10,1... | collective-permute-start | bytes 786440 | tf_op jit(solution)/shard_map/ppermute | solution.py:116
  24.3 7.6 %collective-permute-start.8 = (bf16[128,1024]{1,0:T(8,128)(2,1)S(1)}, bf16[128,1024]{1,0:T(8,128)(2,1)S(1)}, u32[]{:S(2)}, u32[]{:S(2)}) collective-permute-start(bf16[128,1024]{1,0:T(8,128)(2,1)S(1)} %collective-permute-done.refs_1_), channel_id=1, source_target_pairs={{0,8},{4,12},{8,0},{12,4},{1,9},{5,13},{9,1},{13,5},{2,10},{6,14},... | collective-permute-start | bytes 786440 | tf_op jit(solution)/shard_map/ppermute | solution.py:120
  26.1 5.8 %collective-permute-start.4 = (bf16[128,1024]{1,0:T(8,128)(2,1)S(1)}, bf16[128,1024]{1,0:T(8,128)(2,1)S(1)}, u32[]{:S(2)}, u32[]{:S(2)}) collective-permute-start(bf16[128,1024]{1,0:T(8,128)(2,1)S(1)} %collective-permute-done.refs_1_), channel_id=1, source_target_pairs={{0,4},{4,0},{8,12},{12,8},{1,5},{5,1},{9,13},{13,9},{2,6},{6,2},{1... | collective-permute-start | bytes 786440 | tf_op jit(solution)/shard_map/ppermute | solution.py:125
  26.8 5.6 %collective-permute-start.11 = (bf16[128,1024]{1,0:T(8,128)(2,1)S(1)}, bf16[128,1024]{1,0:T(8,128)(2,1)S(1)}, u32[]{:S(2)}, u32[]{:S(2)}) collective-permute-start(bf16[128,1024]{1,0:T(8,128)(2,1)S(1)} %collective-permute-done.7.refs_8_), channel_id=1, source_target_pairs={{0,4},{4,0},{8,12},{12,8},{1,5},{5,1},{9,13},{13,9},{2,6},{6,2},{1... | collective-permute-start | bytes 786440 | tf_op jit(solution)/shard_map/ppermute | solution.py:125
  28.0 10.6 %collective-permute-start.17 = (bf16[128,1024]{1,0:T(8,128)(2,1)S(1)}, bf16[128,1024]{1,0:T(8,128)(2,1)}, u32[]{:S(2)}, u32[]{:S(2)}) collective-permute-start(bf16[128,1024]{1,0:T(8,128)(2,1)S(1)} %collective-permute-done.16.refs_2_), channel_id=1, source_target_pairs={{0,1},{1,2},{2,3},{3,0},{4,5},{5,6},{6,7},{7,4},{8,9},{9,10},{10,1... | collective-permute-start | bytes 786440 | tf_op jit(solution)/shard_map/ppermute | solution.py:116
  29.6 9.1 %collective-permute-start.24 = (bf16[128,1024]{1,0:T(8,128)(2,1)S(1)}, bf16[128,1024]{1,0:T(8,128)(2,1)}, u32[]{:S(2)}, u32[]{:S(2)}) collective-permute-start(bf16[128,1024]{1,0:T(8,128)(2,1)S(1)} %collective-permute-done.16.refs_2_), channel_id=1, source_target_pairs={{0,8},{4,12},{8,0},{12,4},{1,9},{5,13},{9,1},{13,5},{2,10},{6,14},... | collective-permute-start | bytes 786440 | tf_op jit(solution)/shard_map/ppermute | solution.py:120
  31.9 8.9 %collective-permute-start.20 = (bf16[128,1024]{1,0:T(8,128)(2,1)S(1)}, bf16[128,1024]{1,0:T(8,128)(2,1)}, u32[]{:S(2)}, u32[]{:S(2)}) collective-permute-start(bf16[128,1024]{1,0:T(8,128)(2,1)S(1)} %collective-permute-done.16.refs_2_), channel_id=1, source_target_pairs={{0,4},{4,0},{8,12},{12,8},{1,5},{5,1},{9,13},{13,9},{2,6},{6,2},{1... | collective-permute-start | bytes 786440 | tf_op jit(solution)/shard_map/ppermute | solution.py:125
  31.9 8.9 %collective-permute-start.27 = (bf16[128,1024]{1,0:T(8,128)(2,1)S(1)}, bf16[128,1024]{1,0:T(8,128)(2,1)}, u32[]{:S(2)}, u32[]{:S(2)}) collective-permute-start(bf16[128,1024]{1,0:T(8,128)(2,1)S(1)} %collective-permute-done.23.refs_9_), channel_id=1, source_target_pairs={{0,4},{4,0},{8,12},{12,8},{1,5},{5,1},{9,13},{13,9},{2,6},{6,2},{1... | collective-permute-start | bytes 786440 | tf_op jit(solution)/shard_map/ppermute | solution.py:125
  33.1 10.6 %collective-permute-start.2 = (bf16[128,1024]{1,0:T(8,128)(2,1)S(1)}, bf16[128,1024]{1,0:T(8,128)(2,1)}, u32[]{:S(2)}, u32[]{:S(2)}) collective-permute-start(bf16[128,1024]{1,0:T(8,128)(2,1)S(1)} %collective-permute-done.1.refs_2_), channel_id=1, source_target_pairs={{0,1},{1,2},{2,3},{3,0},{4,5},{5,6},{6,7},{7,4},{8,9},{9,10},{10,1... | collective-permute-start | bytes 786440 | tf_op jit(solution)/shard_map/ppermute | solution.py:116
  38.6 9.6 %collective-permute-start.25 = (bf16[128,1024]{1,0:T(8,128)(2,1)}, bf16[128,1024]{1,0:T(8,128)(2,1)}, u32[]{:S(2)}, u32[]{:S(2)}) collective-permute-start(bf16[128,1024]{1,0:T(8,128)(2,1)} %collective-permute-done.17.refs_3_), channel_id=1, source_target_pairs={{0,8},{4,12},{8,0},{12,4},{1,9},{5,13},{9,1},{13,5},{2,10},{6,14},... | collective-permute-start | bytes 786440 | tf_op jit(solution)/shard_map/ppermute | solution.py:120
  38.7 15.1 %collective-permute-start.9 = (bf16[128,1024]{1,0:T(8,128)(2,1)S(1)}, bf16[128,1024]{1,0:T(8,128)(2,1)}, u32[]{:S(2)}, u32[]{:S(2)}) collective-permute-start(bf16[128,1024]{1,0:T(8,128)(2,1)S(1)} %collective-permute-done.1.refs_2_), channel_id=1, source_target_pairs={{0,8},{4,12},{8,0},{12,4},{1,9},{5,13},{9,1},{13,5},{2,10},{6,14},... | collective-permute-start | bytes 786440 | tf_op jit(solution)/shard_map/ppermute | solution.py:120
  40.8 13.0 %collective-permute-start.21 = (bf16[128,1024]{1,0:T(8,128)(2,1)}, bf16[128,1024]{1,0:T(8,128)(2,1)}, u32[]{:S(2)}, u32[]{:S(2)}) collective-permute-start(bf16[128,1024]{1,0:T(8,128)(2,1)} %collective-permute-done.17.refs_3_), channel_id=1, source_target_pairs={{0,4},{4,0},{8,12},{12,8},{1,5},{5,1},{9,13},{13,9},{2,6},{6,2},{1... | collective-permute-start | bytes 786440 | tf_op jit(solution)/shard_map/ppermute | solution.py:125
  40.8 13.5 %collective-permute-start.28 = (bf16[128,1024]{1,0:T(8,128)(2,1)}, bf16[128,1024]{1,0:T(8,128)(2,1)}, u32[]{:S(2)}, u32[]{:S(2)}) collective-permute-start(bf16[128,1024]{1,0:T(8,128)(2,1)} %collective-permute-done.24.refs_10_), channel_id=1, source_target_pairs={{0,4},{4,0},{8,12},{12,8},{1,5},{5,1},{9,13},{13,9},{2,6},{6,2},{1... | collective-permute-start | bytes 786440 | tf_op jit(solution)/shard_map/ppermute | solution.py:125
  43.7 13.3 %collective-permute-start.10 = (bf16[128,1024]{1,0:T(8,128)(2,1)}, bf16[128,1024]{1,0:T(8,128)(2,1)}, u32[]{:S(2)}, u32[]{:S(2)}) collective-permute-start(bf16[128,1024]{1,0:T(8,128)(2,1)} %collective-permute-done.2.refs_3_), channel_id=1, source_target_pairs={{0,8},{4,12},{8,0},{12,4},{1,9},{5,13},{9,1},{13,5},{2,10},{6,14},... | collective-permute-start | bytes 786440 | tf_op jit(solution)/shard_map/ppermute | solution.py:120
  48.1 8.9 %collective-permute-start.29 = (bf16[128,1024]{1,0:T(8,128)(2,1)}, bf16[128,1024]{1,0:T(8,128)(2,1)}, u32[]{:S(2)}, u32[]{:S(2)}) collective-permute-start(bf16[128,1024]{1,0:T(8,128)(2,1)} %collective-permute-done.25.refs_11_), channel_id=1, source_target_pairs={{0,4},{4,0},{8,12},{12,8},{1,5},{5,1},{9,13},{13,9},{2,6},{6,2},{1... | collective-permute-start | bytes 786440 | tf_op jit(solution)/shard_map/ppermute | solution.py:125
  53.7 21.4 %collective-permute-start.5 = (bf16[128,1024]{1,0:T(8,128)(2,1)S(1)}, bf16[128,1024]{1,0:T(8,128)(2,1)S(1)}, u32[]{:S(2)}, u32[]{:S(2)}) collective-permute-start(bf16[128,1024]{1,0:T(8,128)(2,1)S(1)} %collective-permute-done.1.refs_2_), channel_id=1, source_target_pairs={{0,4},{4,0},{8,12},{12,8},{1,5},{5,1},{9,13},{13,9},{2,6},{6,2},{1... | collective-permute-start | bytes 786440 | tf_op jit(solution)/shard_map/ppermute | solution.py:125
  53.7 21.4 %collective-permute-start.12 = (bf16[128,1024]{1,0:T(8,128)(2,1)S(1)}, bf16[128,1024]{1,0:T(8,128)(2,1)S(1)}, u32[]{:S(2)}, u32[]{:S(2)}) collective-permute-start(bf16[128,1024]{1,0:T(8,128)(2,1)S(1)} %collective-permute-done.8.refs_9_), channel_id=1, source_target_pairs={{0,4},{4,0},{8,12},{12,8},{1,5},{5,1},{9,13},{13,9},{2,6},{6,2},{1... | collective-permute-start | bytes 786440 | tf_op jit(solution)/shard_map/ppermute | solution.py:125
  54.2 20.9 %collective-permute-start.6 = (bf16[128,1024]{1,0:T(8,128)(2,1)}, bf16[128,1024]{1,0:T(8,128)(2,1)S(1)}, u32[]{:S(2)}, u32[]{:S(2)}) collective-permute-start(bf16[128,1024]{1,0:T(8,128)(2,1)} %collective-permute-done.2.refs_3_), channel_id=1, source_target_pairs={{0,4},{4,0},{8,12},{12,8},{1,5},{5,1},{9,13},{13,9},{2,6},{6,2},{1... | collective-permute-start | bytes 786440 | tf_op jit(solution)/shard_map/ppermute | solution.py:125
  57.0 18.1 %collective-permute-start.13 = (bf16[128,1024]{1,0:T(8,128)(2,1)}, bf16[128,1024]{1,0:T(8,128)(2,1)S(1)}, u32[]{:S(2)}, u32[]{:S(2)}) collective-permute-start(bf16[128,1024]{1,0:T(8,128)(2,1)} %collective-permute-done.9.refs_10_), channel_id=1, source_target_pairs={{0,4},{4,0},{8,12},{12,8},{1,5},{5,1},{9,13},{13,9},{2,6},{6,2},{1... | collective-permute-start | bytes 786440 | tf_op jit(solution)/shard_map/ppermute | solution.py:125
  57.0 18.1 %collective-permute-start.14 = (bf16[128,1024]{1,0:T(8,128)(2,1)}, bf16[128,1024]{1,0:T(8,128)(2,1)S(1)}, u32[]{:S(2)}, u32[]{:S(2)}) collective-permute-start(bf16[128,1024]{1,0:T(8,128)(2,1)} %collective-permute-done.10.refs_11_), channel_id=1, source_target_pairs={{0,4},{4,0},{8,12},{12,8},{1,5},{5,1},{9,13},{13,9},{2,6},{6,2},{1... | collective-permute-start | bytes 786440 | tf_op jit(solution)/shard_map/ppermute | solution.py:125
  (6 other events, 19.7 us)

commit v3 on v2

v3 whole, which is shorter than its diff:
```python
import functools
import math

import jax
import jax.numpy as jnp
from jax import lax
from jax.experimental import pallas as pl
from jax.experimental.pallas import tpu as pltpu
from jax.sharding import PartitionSpec as P

HD = 128
CORES = 2
HEADS_PER_TILE = 2
EXP2_SCALE = math.log2(math.e) / math.sqrt(HD)
LEAST_TOTAL, MOST_TOTAL = 1e-20, 1e30


def matmul_nt(a, b):
    return lax.dot_general(a, b, (((1,), (1,)), ((), ())), preferred_element_type=jnp.float32)


class Place:
    def __init__(self, sizes, placement, lengths):
        self.prompt_count, self.chips, self.ring, self.tokens = sizes
        self.blocks = self.chips * CORES
        self.index, self.head = lax.axis_index("blk"), lax.axis_index("head")
        self.placement = placement
        self.block = placement[self.index]
        slot = jnp.clip(self.block - self.prompt_count, 0, self.prompt_count - 1)
        rows = self.ring * self.tokens
        self.keep = jnp.where(self.block >= self.prompt_count, lengths[slot], rows)

    def source(self, slot):
        found = jnp.int32(0)
        for b in range(self.blocks):
            found = jnp.where(self.placement[b] == slot, b, found)
        found = jnp.where(slot == self.prompt_count, self.index, found)
        chips_back = lax.rem(self.index // CORES - found // CORES + self.chips, self.chips)
        return chips_back * CORES + lax.rem(self.index + found, CORES)

    def visible(self, slot, hop):
        return jnp.where(slot == self.prompt_count, self.head >= hop, self.block > slot)

    def kept(self):
        offsets = self.head * self.tokens + lax.broadcasted_iota(jnp.int32, (self.tokens, 1), 0)
        return offsets < self.keep


def exact(here, pieces, query, out, held, sem, kv_head, kv_heads, group):
    slots, tokens, ring = here.prompt_count + 1, here.tokens, here.ring
    rows = ring * tokens

    def fetch(slot, carry):
        wanted = here.source(slot)
        for source in range(here.blocks):

            @pl.when(wanted == source)
            def _():
                for hop in range(ring):
                    first = pl.multiple_of(lax.rem(here.head - hop + ring, ring) * tokens, tokens)
                    for i in range(2):
                        column = pl.multiple_of((i * kv_heads + kv_head) * HD, HD)
                        copy = pltpu.make_async_copy(
                            pieces[source * ring + hop].at[:, pl.ds(column, HD)],
                            held.at[slot, pl.ds(first, tokens), pl.ds(i * HD, HD)],
                            sem,
                        )
                        copy.start()
                        copy.wait()

        return carry

    lax.fori_loop(0, slots, fetch, 0)
    own_offset = here.head * tokens + lax.broadcasted_iota(jnp.int32, (tokens, rows), 0)
    key_offset = lax.broadcasted_iota(jnp.int32, (tokens, rows), 1)

    def one_head(head, carry):
        columns = pl.ds(pl.multiple_of(head * HD, HD), HD)
        query_one = query[:, columns]

        def score(slot):
            prompt_end = jnp.where(here.block > slot, rows, -1)
            newest = jnp.where(slot == here.prompt_count, own_offset, prompt_end)
            return jnp.where(key_offset <= newest, matmul_nt(query_one, held[slot, :, :HD]), -jnp.inf)

        row_max = lax.fori_loop(
            0,
            slots,
            lambda j, best: jnp.maximum(best, jnp.max(score(j), axis=1, keepdims=True)),
            jnp.full((tokens, 1), -jnp.inf, jnp.float32),
        )

        def add(slot, carry):
            total, summed = carry
            weights = jnp.exp2((score(slot) - row_max) * EXP2_SCALE)
            total += jnp.sum(weights, axis=1, keepdims=True)
            value = held[slot, :, HD:]
            return total, summed + jnp.dot(weights.astype(jnp.bfloat16), value, preferred_element_type=jnp.float32)

        zeros = jnp.zeros((tokens, 1), jnp.float32), jnp.zeros((tokens, HD), jnp.float32)
        total, summed = lax.fori_loop(0, slots, add, zeros)
        out[:, columns] = jnp.where(here.kept(), summed / total, 0.0).astype(out.dtype)
        return carry

    lax.fori_loop(0, group, one_head, 0)


def fold_kernel(sizes, hops, first, last, placement, lengths, query, *refs):
    prompt_count, chips, ring, tokens = sizes
    slots = prompt_count + 1
    here = Place(sizes, placement, lengths)
    used = list(range(ring)) if last else list(hops)
    refs = list(refs)
    pieces = [refs.pop(0) for _ in range(here.blocks * len(used))]
    before = None if first else refs.pop(0)
    out, held, ones, bias, sems = refs[:5]
    kv_head, kv_heads = pl.program_id(0), pl.num_programs(0)
    group = query.shape[1] // HD
    width = held.shape[1] // 2
    order = list(reversed(hops))
    masked = bias.shape[1]

    @pl.when(kv_head == 0)
    def _():
        def at(slot, i):
            return pl.ds(pl.multiple_of((slot * len(order) + i) * tokens, tokens), tokens)

        def fetch(slot, carry):
            wanted = here.source(slot)
            for source in range(here.blocks):

                @pl.when(wanted == source)
                def _():
                    for i, hop in enumerate(order):
                        piece = pieces[source * len(used) + used.index(hop)]
                        pltpu.make_async_copy(piece, held.at[at(slot, i)], sems.at[slot, i]).start()

            return carry

        def finish(slot, carry):
            for i, hop in enumerate(order):
                pltpu.make_async_copy(pieces[0], held.at[at(slot, i)], sems.at[slot, i]).wait()
                seen = here.visible(slot, hop)
                ones[at(slot, i)] = jnp.full((tokens, HD), jnp.where(seen, 1.0, 0.0), jnp.float32).astype(jnp.bfloat16)

                @pl.when(jnp.logical_not(seen))
                def _():
                    held[at(slot, i)] = jnp.zeros((tokens, held.shape[1]), held.dtype)

            return carry

        lax.fori_loop(0, slots, fetch, 0)
        if first:
            own = lax.broadcasted_iota(jnp.int32, (tokens, masked), 0)
            key = lax.broadcasted_iota(jnp.int32, (tokens, masked), 1) - (masked - tokens)
            bias[...] = jnp.where(key <= own, 0.0, -jnp.inf)
        lax.fori_loop(0, slots, finish, 0)

    key = held[:, pl.ds(pl.multiple_of(kv_head * HD, HD), HD)]
    value = held[:, pl.ds(pl.multiple_of(width + kv_head * HD, HD), HD)]
    value = jnp.concatenate([value, ones[...]], axis=1)
    kept = here.kept()
    least = jnp.full((tokens, HD), jnp.inf, jnp.float32)
    most = jnp.zeros((tokens, HD), jnp.float32)
    for tile in range(group // HEADS_PER_TILE):
        heads = range(tile * HEADS_PER_TILE, (tile + 1) * HEADS_PER_TILE)
        query_tile = jnp.concatenate([query[:, h * HD : (h + 1) * HD] for h in heads], axis=0)
        scores = matmul_nt(query_tile, key) * EXP2_SCALE
        if first:
            split = scores.shape[1] - masked
            tail = scores[:, split:].reshape(HEADS_PER_TILE, tokens, masked) + bias[...][None]
            tail = tail.reshape(HEADS_PER_TILE * tokens, masked)
            scores = tail if split == 0 else jnp.concatenate([scores[:, :split], tail], axis=1)
        weights = jnp.exp2(scores).astype(jnp.bfloat16)
        summed = jnp.dot(weights, value, preferred_element_type=jnp.float32)
        for i, h in enumerate(heads):
            columns = slice(h * 2 * HD, (h + 1) * 2 * HD)
            part = summed[i * tokens : (i + 1) * tokens]
            if not first:
                part = part + before[:, columns]
            if last:
                total = part[:, HD:]
                least, most = jnp.minimum(least, total), jnp.maximum(most, total)
                out[:, h * HD : (h + 1) * HD] = jnp.where(kept, part[:, :HD] / total, 0.0).astype(out.dtype)
            else:
                out[:, columns] = part
    if last:
        safe = (jnp.min(least) > LEAST_TOTAL) & (jnp.max(most) < MOST_TOTAL)

        @pl.when(jnp.logical_not(safe))
        def _():
            exact(here, pieces, query, out, refs[5], refs[6], kv_head, kv_heads, group)


def fold(placement, lengths, query_rows, pieces, sizes, hops, before, last):
    prompt_count, chips, ring, tokens = sizes
    slots, blocks = prompt_count + 1, chips * CORES
    first = before is None
    width = query_rows.shape[1]
    kv_width = pieces[0][0].shape[1] // 2
    kv_heads = kv_width // HD
    group = width // kv_width
    whole = pl.BlockSpec(memory_space=pl.ANY)

    def per_head(columns):
        return pl.BlockSpec((tokens, columns), lambda g, *_: (0, g))

    used = range(ring) if last else hops
    operands = [pieces[source][hop] for source in range(blocks) for hop in used]
    in_specs, args = [per_head(group * HD)] + [whole] * len(operands), [query_rows, *operands]
    if not first:
        in_specs.append(per_head(group * 2 * HD))
        args.append(before)
    keys = slots * len(hops) * tokens
    masked = tokens if tokens % HD == 0 else keys
    scratch = [
        pltpu.VMEM((keys, 2 * kv_width), jnp.bfloat16),
        pltpu.VMEM((keys, HD), jnp.bfloat16),
        pltpu.VMEM((tokens, masked), jnp.float32),
        pltpu.SemaphoreType.DMA((slots, len(hops))),
    ]
    if last:
        scratch += [pltpu.VMEM((slots, ring * tokens, 2 * HD), jnp.bfloat16), pltpu.SemaphoreType.DMA]
        out_shape, out_spec = jax.ShapeDtypeStruct((tokens, width), query_rows.dtype), per_head(group * HD)
    else:
        out_shape, out_spec = jax.ShapeDtypeStruct((tokens, 2 * width), jnp.float32), per_head(group * 2 * HD)
    work = tokens * group * kv_heads * keys
    return pl.pallas_call(
        functools.partial(fold_kernel, sizes, hops, first, last),
        grid_spec=pltpu.PrefetchScalarGridSpec(
            num_scalar_prefetch=2, grid=(kv_heads,), in_specs=in_specs, out_specs=out_spec, scratch_shapes=scratch
        ),
        out_shape=out_shape,
        cost_estimate=pl.CostEstimate(flops=6 * work * HD, bytes_accessed=12 << 20, transcendentals=work),
        compiler_params=pltpu.CompilerParams(vmem_limit_bytes=40 << 20),
    )(placement, lengths, *args)


def gather_pieces(own, chips):
    ring, blocks = lax.axis_size("head"), chips * CORES
    column = [own]
    for _ in range(ring - 1):
        column.append(lax.ppermute(column[-1], "head", [(i, (i + 1) % ring) for i in range(ring)]))
    planes = [column]
    for _ in range(chips - 1):
        planes.append(
            [lax.ppermute(x, "blk", [(i, (i + CORES) % blocks) for i in range(blocks)]) for x in planes[-1]]
        )
    pieces = []
    for plane in planes:
        pieces.append(plane)
        pieces.append([lax.ppermute(x, "blk", [(i, i ^ 1) for i in range(blocks)]) for x in plane])
    return pieces


def shards(query_rows, key_rows, value_rows, placement, lengths):
    block_count, ring = lax.axis_size("blk"), lax.axis_size("head")
    sizes = (block_count // 2, block_count // CORES, ring, query_rows.shape[0])
    pieces = gather_pieces(jnp.concatenate([key_rows, value_rows], axis=1), sizes[1])
    state = None
    for hops in (tuple(range(ring - 2)), (ring - 2,), (ring - 1,)):
        state = fold(placement, lengths, query_rows, pieces, sizes, hops, state, hops[-1] == ring - 1)
    return state


def solution(mesh):
    rows = P(("grp", "blk", "head"), None)
    return jax.shard_map(
        shards,
        mesh=mesh,
        in_specs=(rows, rows, rows, P("grp"), P("grp")),
        out_specs=rows,
        check_vma=False,
    )
```

time: 91.1 us -> 232 us (2.55)
  Pallas kernels: 31.3 us -> 156 us
  waiting for transfers between devices: 29 us -> 57.7 us
  starting transfers between devices: 21.2 us -> 8.85 us
    pallas_call x2 -> x3, Pallas kernels: 31.3 us -> 156 us  [fold(): pl.pallas_call(functools.partial(fold_kernel, sizes, hops, first, last),...]
    ppermute x6 -> x3, waiting for transfers between devices: 20.3 us -> 39.1 us  [gather_pieces(): lax.ppermute(column[-1], 'head', [(i, (i + 1) % ring) for i in range(ring)])]
    ppermute x8 -> x4, waiting for transfers between devices: 8.59 us -> 18.6 us  [gather_pieces(): lax.ppermute(x, 'blk', [(i, (i + CORES) % blocks) for i in range(blocks)])]
    ppermute x8 -> x4, starting transfers between devices: 10.4 us -> 4.52 us  [gather_pieces(): lax.ppermute(x, 'blk', [(i, (i + CORES) % blocks) for i in range(blocks)])]
    ppermute x6 -> x3, starting transfers between devices: 8.08 us -> 3.08 us  [gather_pieces(): lax.ppermute(column[-1], 'head', [(i, (i + 1) % ring) for i in range(ring)])]
    unnamed x16 -> x9, local copies, waits for them, and re-layouts: 4.01 us -> 7.1 us
  transfers between devices with their start and end apart: 30 -> 15, of which waited for: 12 -> 5; matrix products, arithmetic and copies ran while one was open for 2% -> 0% of each run, Pallas kernels for 17% -> 9%
where the time goes in v3:
time: 232 us; the launch traced here: 231 us
  Pallas kernels  156 us (67%)
  waiting for transfers between devices  57.7 us (25%)
  starting transfers between devices  8.85 us (4%)
  local copies, waits for them, and re-layouts  8.07 us (3%)
    pallas_call x3, Pallas kernels, fold(): pl.pallas_call(functools.partial(fold_kernel, sizes, hops, first, last),...  156 us
    ppermute x3, waiting for transfers between devices, gather_pieces(): lax.ppermute(column[-1], 'head', [(i, (i + 1) % ring) for i in range(ring)])  39.1 us
    ppermute x4, waiting for transfers between devices, gather_pieces(): lax.ppermute(x, 'blk', [(i, (i + CORES) % blocks) for i in range(blocks)])  18.6 us
    unnamed x9, local copies, waits for them, and re-layouts  7.1 us
  transfers between devices with their start and end apart: 15, of which 5 were waited for; matrix products, arithmetic and copies ran while one was open for 0% of the time, Pallas kernels for 9%

profile of v3, /device:TPU:0, one launch (start us, length us, event | category | flops | bytes accessed | tf_op | source)
XLA Modules:
  0.0 231.1 jit_solution(15335021350965844436)
XLA Ops:
  0.0 1.0 constant_dynamic-update-slice_fusion.1
  1.0 1.0 constant_dynamic-update-slice_fusion.refs_0_
  1.9 3.1 %collective-permute-start = (bf16[128,2048]{1,0:T(8,128)(2,1)S(1)}, bf16[128,2048]{1,0:T(8,128)(2,1)S(1)}, u32[]{:S(2)}, u32[]{:S(2)}) collective-permute-start(bf16[128,2048]{1,0:T(8,128)(2,1)S(1)} %constant_dynamic-update-slice_fusion.refs_0_), channel_id=1, source_target_pairs={{0,1},{1,2},{2,3},{3,0},{4,5},{5,6},{6,7},{7,4},{8,9},{9,10},{10,1... | collective-permute-start | bytes 1572872 | tf_op jit(solution)/shard_map/ppermute | solution.py:243
  5.0 13.9 %collective-permute-done.refs_1_ = bf16[128,2048]{1,0:T(8,128)(2,1)S(1)} collective-permute-done((bf16[128,2048]{1,0:T(8,128)(2,1)S(1)}, bf16[128,2048]{1,0:T(8,128)(2,1)S(1)}, u32[]{:S(2)}, u32[]{:S(2)}) %collective-permute-start) | collective-permute-done | bytes 524320 | tf_op jit(solution)/shard_map/ppermute | solution.py:243
  19.0 0.0 collective-permute-start.1
  19.0 1.5 collective-permute-start.7
  20.5 0.0 collective-permute-start.3
  20.5 13.4 %collective-permute-done.1.refs_0_.refs_2_ = bf16[128,2048]{1,0:T(8,128)(2,1)S(1)} collective-permute-done((bf16[128,2048]{1,0:T(8,128)(2,1)S(1)}, bf16[128,2048]{1,0:T(8,128)(2,1)S(1)}, u32[]{:S(2)}, u32[]{:S(2)}) %collective-permute-start.1) | collective-permute-done | bytes 524320 | tf_op jit(solution)/shard_map/ppermute | solution.py:243
  33.9 0.0 collective-permute-start.2
  33.9 1.2 collective-permute-start.8
  35.1 0.8 collective-permute-start.9
  35.9 0.0 collective-permute-done.3.refs_2_.refs_4_
  35.9 0.2 collective-permute-start.11
  36.1 11.7 %collective-permute-done.2.refs_3_ = bf16[128,2048]{1,0:T(8,128)(2,1)S(1)} collective-permute-done((bf16[128,2048]{1,0:T(8,128)(2,1)S(1)}, bf16[128,2048]{1,0:T(8,128)(2,1)S(1)}, u32[]{:S(2)}, u32[]{:S(2)}) %collective-permute-start.2) | collective-permute-done | bytes 524320 | tf_op jit(solution)/shard_map/ppermute | solution.py:243
  47.9 1.0 collective-permute-start.10
  48.9 0.0 collective-permute-start.12
  48.9 0.0 collective-permute-done.4.refs_3_.refs_5_
  48.9 0.5 collective-permute-start.5
  49.4 10.6 %collective-permute-done.9.refs_2_.refs_10_ = bf16[128,2048]{1,0:T(8,128)(2,1)S(1)} collective-permute-done((bf16[128,2048]{1,0:T(8,128)(2,1)S(1)}, bf16[128,2048]{1,0:T(8,128)(2,1)S(1)}, u32[]{:S(2)}, u32[]{:S(2)}) %collective-permute-start.9) | collective-permute-done | bytes 524320 | tf_op jit(solution)/shard_map/ppermute | solution.py:247
  60.0 0.0 collective-permute-start.13
  60.0 0.0 collective-permute-done.11.refs_6_.refs_12_
  60.0 0.5 collective-permute-start.6
  60.5 8.0 %collective-permute-done.10.refs_11_ = bf16[128,2048]{1,0:T(8,128)(2,1)S(1)} collective-permute-done((bf16[128,2048]{1,0:T(8,128)(2,1)S(1)}, bf16[128,2048]{1,0:T(8,128)(2,1)S(1)}, u32[]{:S(2)}, u32[]{:S(2)}) %collective-permute-start.10) | collective-permute-done | bytes 524320 | tf_op jit(solution)/shard_map/ppermute | solution.py:247
  68.6 1.6 copy-done.1
  70.1 0.7 copy-done.2
  70.8 0.7 copy-done.3
  71.5 11.3 %shard_map.55.refs_4_ = f32[128,16384]{1,0:T(8,128)} custom-call(s32[4]{0:T(128)S(1)} %copy-done.2, s32[2]{0:T(128)S(1)} %copy-done.3, bf16[128,8192]{1,0:T(8,128)(2,1)S(1)} %copy-done.1, bf16[128,2048]{1,0:T(8,128)(2,1)S(1)} %constant_dynamic-update-slice_fusion.refs_0_, bf16[128,2048]{1,0:T(8,128)(2,1)S(1)} %collective-permute-done.refs_1_, ...), custom_call_target="tpu_custom_call" | custom-call | flops 4831838208 | bytes 12582912 | tf_op jit(solution)/shard_map/pallas_call | solution.py:228
  82.8 10.2 %shard_map.56.refs_16_ = f32[128,16384]{1,0:T(8,128)S(1)} custom-call(s32[4]{0:T(128)S(1)} %copy-done.2, s32[2]{0:T(128)S(1)} %copy-done.3, bf16[128,8192]{1,0:T(8,128)(2,1)S(1)} %copy-done.1, bf16[128,2048]{1,0:T(8,128)(2,1)S(1)} %collective-permute-done.1.refs_0_.refs_2_, bf16[128,2048]{1,0:T(8,128)(2,1)S(1)} %collective-permute-done.5.refs_1_.refs_6_, ...), custom_call_target="tpu_custom_call" | custom-call | flops 2415919104 | bytes 12582912 | tf_op jit(solution)/shard_map/pallas_call | solution.py:228
  93.0 3.2 %copy-done = f32[128,16384]{1,0:T(8,128)} copy-done((f32[128,16384]{1,0:T(8,128)}, f32[128,16384]{1,0:T(8,128)S(1)}, u32[]{:S(2)}) %copy-start) | copy-done | bytes 8388632
  96.3 0.0 collective-permute-done.6.refs_7_
  96.3 0.0 collective-permute-done.14.refs_15_
  96.3 134.9 %shard_map.57 = bf16[128,8192]{1,0:T(8,128)(2,1)} custom-call(s32[4]{0:T(128)S(1)} %copy-done.2, s32[2]{0:T(128)S(1)} %copy-done.3, bf16[128,8192]{1,0:T(8,128)(2,1)S(1)} %copy-done.1, bf16[128,2048]{1,0:T(8,128)(2,1)S(1)} %constant_dynamic-update-slice_fusion.refs_0_, bf16[128,2048]{1,0:T(8,128)(2,1)S(1)} %collective-permute-done.refs_1_, ...), custom_call_target="tpu_custom_call" | custom-call | flops 2415919104 | bytes 12582912 | tf_op jit(solution)/shard_map/pallas_call | solution.py:228
  (11 shorter events, 0.0 us)
Async XLA Ops:
  1.9 17.0 %collective-permute-start = (bf16[128,2048]{1,0:T(8,128)(2,1)S(1)}, bf16[128,2048]{1,0:T(8,128)(2,1)S(1)}, u32[]{:S(2)}, u32[]{:S(2)}) collective-permute-start(bf16[128,2048]{1,0:T(8,128)(2,1)S(1)} %constant_dynamic-update-slice_fusion.refs_0_), channel_id=1, source_target_pairs={{0,1},{1,2},{2,3},{3,0},{4,5},{5,6},{6,7},{7,4},{8,9},{9,10},{10,1... | collective-permute-start | bytes 1572872 | tf_op jit(solution)/shard_map/ppermute | solution.py:243
  19.0 14.9 %collective-permute-start.1 = (bf16[128,2048]{1,0:T(8,128)(2,1)S(1)}, bf16[128,2048]{1,0:T(8,128)(2,1)S(1)}, u32[]{:S(2)}, u32[]{:S(2)}) collective-permute-start(bf16[128,2048]{1,0:T(8,128)(2,1)S(1)} %collective-permute-done.refs_1_), channel_id=1, source_target_pairs={{0,1},{1,2},{2,3},{3,0},{4,5},{5,6},{6,7},{7,4},{8,9},{9,10},{10,1... | collective-permute-start | bytes 1572872 | tf_op jit(solution)/shard_map/ppermute | solution.py:243
  19.0 16.2 %collective-permute-start.7 = (bf16[128,2048]{1,0:T(8,128)(2,1)S(1)}, bf16[128,2048]{1,0:T(8,128)(2,1)S(1)}, u32[]{:S(2)}, u32[]{:S(2)}) collective-permute-start(bf16[128,2048]{1,0:T(8,128)(2,1)S(1)} %constant_dynamic-update-slice_fusion.refs_0_), channel_id=1, source_target_pairs={{0,8},{4,12},{8,0},{12,4},{1,9},{5,13},{9,1},{13,5},{2,10},{6,14},... | collective-permute-start | bytes 1572872 | tf_op jit(solution)/shard_map/ppermute | solution.py:247
  20.5 15.5 %collective-permute-start.3 = (bf16[128,2048]{1,0:T(8,128)(2,1)S(1)}, bf16[128,2048]{1,0:T(8,128)(2,1)S(1)}, u32[]{:S(2)}, u32[]{:S(2)}) collective-permute-start(bf16[128,2048]{1,0:T(8,128)(2,1)S(1)} %constant_dynamic-update-slice_fusion.refs_0_), channel_id=1, source_target_pairs={{0,4},{4,0},{8,12},{12,8},{1,5},{5,1},{9,13},{13,9},{2,6},{6,2},{1... | collective-permute-start | bytes 1572872 | tf_op jit(solution)/shard_map/ppermute | solution.py:252
  33.9 14.0 %collective-permute-start.2 = (bf16[128,2048]{1,0:T(8,128)(2,1)S(1)}, bf16[128,2048]{1,0:T(8,128)(2,1)S(1)}, u32[]{:S(2)}, u32[]{:S(2)}) collective-permute-start(bf16[128,2048]{1,0:T(8,128)(2,1)S(1)} %collective-permute-done.1.refs_0_.refs_2_), channel_id=1, source_target_pairs={{0,1},{1,2},{2,3},{3,0},{4,5},{5,6},{6,7},{7,4},{8,9},{9,10},{10,1... | collective-permute-start | bytes 1572872 | tf_op jit(solution)/shard_map/ppermute | solution.py:243
  33.9 15.0 %collective-permute-start.8 = (bf16[128,2048]{1,0:T(8,128)(2,1)S(1)}, bf16[128,2048]{1,0:T(8,128)(2,1)S(1)}, u32[]{:S(2)}, u32[]{:S(2)}) collective-permute-start(bf16[128,2048]{1,0:T(8,128)(2,1)S(1)} %collective-permute-done.refs_1_), channel_id=1, source_target_pairs={{0,8},{4,12},{8,0},{12,4},{1,9},{5,13},{9,1},{13,5},{2,10},{6,14},... | collective-permute-start | bytes 1572872 | tf_op jit(solution)/shard_map/ppermute | solution.py:247
  35.1 13.7 %collective-permute-start.4 = (bf16[128,2048]{1,0:T(8,128)(2,1)S(1)}, bf16[128,2048]{1,0:T(8,128)(2,1)S(1)}, u32[]{:S(2)}, u32[]{:S(2)}) collective-permute-start(bf16[128,2048]{1,0:T(8,128)(2,1)S(1)} %collective-permute-done.refs_1_), channel_id=1, source_target_pairs={{0,4},{4,0},{8,12},{12,8},{1,5},{5,1},{9,13},{13,9},{2,6},{6,2},{1... | collective-permute-start | bytes 1572872 | tf_op jit(solution)/shard_map/ppermute | solution.py:252
  35.1 24.8 %collective-permute-start.9 = (bf16[128,2048]{1,0:T(8,128)(2,1)S(1)}, bf16[128,2048]{1,0:T(8,128)(2,1)S(1)}, u32[]{:S(2)}, u32[]{:S(2)}) collective-permute-start(bf16[128,2048]{1,0:T(8,128)(2,1)S(1)} %collective-permute-done.1.refs_0_.refs_2_), channel_id=1, source_target_pairs={{0,8},{4,12},{8,0},{12,4},{1,9},{5,13},{9,1},{13,5},{2,10},{6,14},... | collective-permute-start | bytes 1572872 | tf_op jit(solution)/shard_map/ppermute | solution.py:247
  35.9 24.1 %collective-permute-start.11 = (bf16[128,2048]{1,0:T(8,128)(2,1)S(1)}, bf16[128,2048]{1,0:T(8,128)(2,1)S(1)}, u32[]{:S(2)}, u32[]{:S(2)}) collective-permute-start(bf16[128,2048]{1,0:T(8,128)(2,1)S(1)} %collective-permute-done.7.refs_4_.refs_8_), channel_id=1, source_target_pairs={{0,4},{4,0},{8,12},{12,8},{1,5},{5,1},{9,13},{13,9},{2,6},{6,2},{1... | collective-permute-start | bytes 1572872 | tf_op jit(solution)/shard_map/ppermute | solution.py:252
  47.9 20.7 %collective-permute-start.10 = (bf16[128,2048]{1,0:T(8,128)(2,1)S(1)}, bf16[128,2048]{1,0:T(8,128)(2,1)S(1)}, u32[]{:S(2)}, u32[]{:S(2)}) collective-permute-start(bf16[128,2048]{1,0:T(8,128)(2,1)S(1)} %collective-permute-done.2.refs_3_), channel_id=1, source_target_pairs={{0,8},{4,12},{8,0},{12,4},{1,9},{5,13},{9,1},{13,5},{2,10},{6,14},... | collective-permute-start | bytes 1572872 | tf_op jit(solution)/shard_map/ppermute | solution.py:247
  48.9 19.7 %collective-permute-start.12 = (bf16[128,2048]{1,0:T(8,128)(2,1)S(1)}, bf16[128,2048]{1,0:T(8,128)(2,1)S(1)}, u32[]{:S(2)}, u32[]{:S(2)}) collective-permute-start(bf16[128,2048]{1,0:T(8,128)(2,1)S(1)} %collective-permute-done.8.refs_5_.refs_9_), channel_id=1, source_target_pairs={{0,4},{4,0},{8,12},{12,8},{1,5},{5,1},{9,13},{13,9},{2,6},{6,2},{1... | collective-permute-start | bytes 1572872 | tf_op jit(solution)/shard_map/ppermute | solution.py:252
  48.9 33.9 %collective-permute-start.5 = (bf16[128,2048]{1,0:T(8,128)(2,1)S(1)}, bf16[128,2048]{1,0:T(8,128)(2,1)S(1)}, u32[]{:S(2)}, u32[]{:S(2)}) collective-permute-start(bf16[128,2048]{1,0:T(8,128)(2,1)S(1)} %collective-permute-done.1.refs_0_.refs_2_), channel_id=1, source_target_pairs={{0,4},{4,0},{8,12},{12,8},{1,5},{5,1},{9,13},{13,9},{2,6},{6,2},{1... | collective-permute-start | bytes 1572872 | tf_op jit(solution)/shard_map/ppermute | solution.py:252
  60.0 22.8 %collective-permute-start.13 = (bf16[128,2048]{1,0:T(8,128)(2,1)S(1)}, bf16[128,2048]{1,0:T(8,128)(2,1)S(1)}, u32[]{:S(2)}, u32[]{:S(2)}) collective-permute-start(bf16[128,2048]{1,0:T(8,128)(2,1)S(1)} %collective-permute-done.9.refs_2_.refs_10_), channel_id=1, source_target_pairs={{0,4},{4,0},{8,12},{12,8},{1,5},{5,1},{9,13},{13,9},{2,6},{6,2},{1... | collective-permute-start | bytes 1572872 | tf_op jit(solution)/shard_map/ppermute | solution.py:252
  60.0 36.3 %collective-permute-start.6 = (bf16[128,2048]{1,0:T(8,128)(2,1)S(1)}, bf16[128,2048]{1,0:T(8,128)(2,1)S(1)}, u32[]{:S(2)}, u32[]{:S(2)}) collective-permute-start(bf16[128,2048]{1,0:T(8,128)(2,1)S(1)} %collective-permute-done.2.refs_3_), channel_id=1, source_target_pairs={{0,4},{4,0},{8,12},{12,8},{1,5},{5,1},{9,13},{13,9},{2,6},{6,2},{1... | collective-permute-start | bytes 1572872 | tf_op jit(solution)/shard_map/ppermute | solution.py:252
  68.5 27.7 %collective-permute-start.14 = (bf16[128,2048]{1,0:T(8,128)(2,1)S(1)}, bf16[128,2048]{1,0:T(8,128)(2,1)S(1)}, u32[]{:S(2)}, u32[]{:S(2)}) collective-permute-start(bf16[128,2048]{1,0:T(8,128)(2,1)S(1)} %collective-permute-done.10.refs_11_), channel_id=1, source_target_pairs={{0,4},{4,0},{8,12},{12,8},{1,5},{5,1},{9,13},{13,9},{2,6},{6,2},{1... | collective-permute-start | bytes 1572872 | tf_op jit(solution)/shard_map/ppermute | solution.py:252
  68.5 1.6 copy-start.1
  70.1 0.7 copy-start.2
  70.8 0.7 copy-start.3
  93.0 3.2 %copy-start = (f32[128,16384]{1,0:T(8,128)}, f32[128,16384]{1,0:T(8,128)S(1)}, u32[]{:S(2)}) copy-start(f32[128,16384]{1,0:T(8,128)S(1)} %shard_map.56.refs_16_) | copy-start | bytes 25165828

commit v4 on v3

v4 whole, which is shorter than its diff:
```python
import functools
import math

import jax
import jax.numpy as jnp
from jax import lax
from jax.experimental import pallas as pl
from jax.experimental.pallas import tpu as pltpu
from jax.sharding import PartitionSpec as P

HD = 128
CORES = 2
HEADS_PER_TILE = 2
SPLIT = (5, 8)
EXP2_SCALE = math.log2(math.e) / math.sqrt(HD)
LEAST_TOTAL, MOST_TOTAL = 1e-20, 1e30


def matmul_nt(a, b):
    return lax.dot_general(a, b, (((1,), (1,)), ((), ())), preferred_element_type=jnp.float32)


class Place:
    def __init__(self, sizes, placement, lengths):
        self.prompt_count, self.chips, self.ring, self.tokens = sizes
        self.blocks = self.chips * CORES
        self.index, self.head = lax.axis_index("blk"), lax.axis_index("head")
        self.placement = placement
        self.block = placement[self.index]
        slot = jnp.clip(self.block - self.prompt_count, 0, self.prompt_count - 1)
        rows = self.ring * self.tokens
        self.keep = jnp.where(self.block >= self.prompt_count, lengths[slot], rows)

    def source(self, slot):
        found = jnp.int32(0)
        for b in range(self.blocks):
            found = jnp.where(self.placement[b] == slot, b, found)
        found = jnp.where(slot == self.prompt_count, self.index, found)
        chips_back = lax.rem(self.index // CORES - found // CORES + self.chips, self.chips)
        return chips_back * CORES + lax.rem(self.index + found, CORES)

    def first_key(self, slot):
        own = (self.ring - 1 - self.head) * self.tokens
        return jnp.where(slot == self.prompt_count, own, jnp.where(self.block > slot, 0, self.ring * self.tokens))

    def kept(self):
        offsets = self.head * self.tokens + lax.broadcasted_iota(jnp.int32, (self.tokens, 1), 0)
        return offsets < self.keep


def exact(here, query, key, value, out, group):
    slots, tokens, rows = here.prompt_count + 1, here.tokens, here.ring * here.tokens
    key_row = lax.broadcasted_iota(jnp.int32, (tokens, rows), 1)
    newest_own = rows - tokens + lax.broadcasted_iota(jnp.int32, (tokens, rows), 0)

    def one_head(head, carry):
        columns = pl.ds(pl.multiple_of(head * HD, HD), HD)
        query_one = query[:, columns]

        def part(ref, slot):
            return ref[pl.ds(pl.multiple_of(slot * rows, rows), rows), :]

        def score(slot):
            newest = jnp.where(slot == here.prompt_count, newest_own, rows)
            seen = (key_row >= here.first_key(slot)) & (key_row <= newest)
            return jnp.where(seen, matmul_nt(query_one, part(key, slot)), -jnp.inf)

        row_max = lax.fori_loop(
            0,
            slots,
            lambda j, best: jnp.maximum(best, jnp.max(score(j), axis=1, keepdims=True)),
            jnp.full((tokens, 1), -jnp.inf, jnp.float32),
        )

        def add(slot, carry):
            total, summed = carry
            weights = jnp.exp2((score(slot) - row_max) * EXP2_SCALE)
            total += jnp.sum(weights, axis=1, keepdims=True)
            weights = weights.astype(jnp.bfloat16)
            return total, summed + jnp.dot(weights, part(value, slot), preferred_element_type=jnp.float32)

        zeros = jnp.zeros((tokens, 1), jnp.float32), jnp.zeros((tokens, HD), jnp.float32)
        total, summed = lax.fori_loop(0, slots, add, zeros)
        out[:, columns] = jnp.where(here.kept(), summed / total, 0.0).astype(out.dtype)
        return carry

    lax.fori_loop(0, group, one_head, 0)


def attend_kernel(sizes, placement, lengths, query, *refs):
    prompt_count, chips, ring, tokens = sizes
    slots = prompt_count + 1
    here = Place(sizes, placement, lengths)
    pieces, (out, held, ones, bias, sems) = refs[: here.blocks * ring], refs[-5:]
    kv_head, width = pl.program_id(0), held.shape[1] // 2
    group = query.shape[1] // HD
    masked = bias.shape[1]

    @pl.when(kv_head == 0)
    def _():
        def at(slot, hop):
            return pl.ds(pl.multiple_of((slot * ring + ring - 1 - hop) * tokens, tokens), tokens)

        def fetch(slot, carry):
            wanted = here.source(slot)
            for source in range(here.blocks):

                @pl.when(wanted == source)
                def _():
                    for hop in range(ring):
                        piece = pieces[source * ring + hop]
                        pltpu.make_async_copy(piece, held.at[at(slot, hop)], sems.at[slot, hop]).start()

            return carry

        def finish(slot, carry):
            for hop in range(ring):
                pltpu.make_async_copy(pieces[0], held.at[at(slot, hop)], sems.at[slot, hop]).wait()
                seen = (ring - 1 - hop) * tokens >= here.first_key(slot)
                ones[at(slot, hop)] = jnp.full((tokens, HD), jnp.where(seen, 1.0, 0.0), jnp.float32).astype(ones.dtype)

                @pl.when(jnp.logical_not(seen))
                def _():
                    held[at(slot, hop)] = jnp.zeros((tokens, held.shape[1]), held.dtype)

            return carry

        lax.fori_loop(0, slots, fetch, 0)
        own = lax.broadcasted_iota(jnp.int32, (tokens, masked), 0)
        key = lax.broadcasted_iota(jnp.int32, (tokens, masked), 1) - (masked - tokens)
        bias[...] = jnp.where(key <= own, 0.0, -jnp.inf)
        lax.fori_loop(0, slots, finish, 0)

    key = held.at[:, pl.ds(pl.multiple_of(kv_head * HD, HD), HD)]
    value = held.at[:, pl.ds(pl.multiple_of(width + kv_head * HD, HD), HD)]
    keys, values = key[...], jnp.concatenate([value[...], ones[...]], axis=1)
    kept = here.kept()
    least = jnp.full((tokens, HD), jnp.inf, jnp.float32)
    most = jnp.zeros((tokens, HD), jnp.float32)
    for tile in range(group // HEADS_PER_TILE):
        heads = range(tile * HEADS_PER_TILE, (tile + 1) * HEADS_PER_TILE)
        query_tile = jnp.concatenate([query[:, h * HD : (h + 1) * HD] for h in heads], axis=0)
        scores = matmul_nt(query_tile, keys) * EXP2_SCALE
        split = scores.shape[1] - masked
        tail = scores[:, split:].reshape(HEADS_PER_TILE, tokens, masked) + bias[...][None]
        tail = tail.reshape(HEADS_PER_TILE * tokens, masked)
        scores = tail if split == 0 else jnp.concatenate([scores[:, :split], tail], axis=1)
        weights = jnp.exp2(scores).astype(jnp.bfloat16)
        summed = jnp.dot(weights, values, preferred_element_type=jnp.float32)
        for i, h in enumerate(heads):
            part = summed[i * tokens : (i + 1) * tokens]
            total = part[:, HD:]
            least, most = jnp.minimum(least, total), jnp.maximum(most, total)
            out[:, h * HD : (h + 1) * HD] = jnp.where(kept, part[:, :HD] / total, 0.0).astype(out.dtype)
    safe = (jnp.min(least) > LEAST_TOTAL) & (jnp.max(most) < MOST_TOTAL)

    @pl.when(jnp.logical_not(safe))
    def _():
        exact(here, query, key, value, out, group)


def attend(placement, lengths, query_rows, pieces, sizes, kv_heads, first_head, previous):
    prompt_count, chips, ring, tokens = sizes
    slots = prompt_count + 1
    piece_width = pieces[0].shape[1]
    group = query_rows.shape[1] // HD // kv_heads
    chunk_heads = piece_width // (2 * HD)
    own_spec = pl.BlockSpec((tokens, group * HD), lambda g, *_: (0, first_head + g))
    whole = pl.BlockSpec(memory_space=pl.ANY)
    in_specs, args, aliases = [own_spec] + [whole] * len(pieces), [placement, lengths, query_rows, *pieces], {}
    if previous is not None:
        aliases = {len(args): 0}
        in_specs.append(whole)
        args.append(previous)
    keys = slots * ring * tokens
    masked = tokens if tokens % HD == 0 else keys
    work = tokens * group * chunk_heads * keys
    return pl.pallas_call(
        functools.partial(attend_kernel, sizes),
        grid_spec=pltpu.PrefetchScalarGridSpec(
            num_scalar_prefetch=2,
            grid=(chunk_heads,),
            in_specs=in_specs,
            out_specs=own_spec,
            scratch_shapes=[
                pltpu.VMEM((keys, piece_width), jnp.bfloat16),
                pltpu.VMEM((keys, HD), jnp.bfloat16),
                pltpu.VMEM((tokens, masked), jnp.float32),
                pltpu.SemaphoreType.DMA((slots, ring)),
            ],
        ),
        out_shape=jax.ShapeDtypeStruct(query_rows.shape, query_rows.dtype),
        input_output_aliases=aliases,
        cost_estimate=pl.CostEstimate(flops=6 * work * HD, bytes_accessed=8 << 20, transcendentals=work),
        compiler_params=pltpu.CompilerParams(vmem_limit_bytes=40 << 20),
    )(*args)


def after(x, *others):
    return lax.optimization_barrier((x, *others))[0]


def shards(query_rows, key_rows, value_rows, placement, lengths):
    blocks, ring = lax.axis_size("blk"), lax.axis_size("head")
    chips = blocks // CORES
    sizes = (blocks // 2, chips, ring, query_rows.shape[0])
    kv_heads = key_rows.shape[1] // HD
    cut = kv_heads * SPLIT[0] // SPLIT[1]

    def next_hop(x):
        return lax.ppermute(x, "head", [(i, (i + 1) % ring) for i in range(ring)])

    def next_chip(x):
        return lax.ppermute(x, "blk", [(i, (i + CORES) % blocks) for i in range(blocks)])

    def other_core(x):
        return lax.ppermute(x, "blk", [(i, i ^ 1) for i in range(blocks)])

    def packed(columns):
        return jnp.concatenate([key_rows[:, columns], value_rows[:, columns]], axis=1)

    def collect(planes, last_after):
        for _ in range(chips - len(planes)):
            planes.append([next_chip(x) for x in planes[-1]])
        if last_after is not None:
            planes[-1][-1] = after(planes[-1][-1], last_after)
        pieces = []
        for plane in planes:
            pieces += plane
            pieces += [other_core(x) for x in plane]
        return pieces

    own_a, own_b = packed(slice(0, cut * HD)), packed(slice(cut * HD, kv_heads * HD))
    column_a, across_a = [own_a], [next_chip(own_a)]
    column_b, across_b = [own_b], [next_chip(own_b)]
    for hop in range(1, ring):
        waits = ([across_a[hop - 2]] if hop > 1 else []) + ([across_b[0]] if hop == 3 else [])
        column_a.append(next_hop(after(column_a[-1], *waits) if waits else column_a[-1]))
        across_a.append(next_chip(column_a[-1]))
    for hop in range(1, ring):
        column_b.append(next_hop(after(column_b[-1], column_a[-2] if hop == 1 else column_a[-1], across_a[hop - 3 + ring - 2])))
        across_b.append(next_chip(column_b[-1]))
    out = attend(placement, lengths, query_rows, collect([column_a, across_a], None), sizes, kv_heads, 0, None)
    pieces_b = collect([column_b, across_b], out)
    return attend(placement, lengths, query_rows, pieces_b, sizes, kv_heads, cut, out)


def solution(mesh):
    rows = P(("grp", "blk", "head"), None)
    return jax.shard_map(
        shards,
        mesh=mesh,
        in_specs=(rows, rows, rows, P("grp"), P("grp")),
        out_specs=rows,
        check_vma=False,
    )
```

time: 232 us -> 215 us (0.927)
  waiting for transfers between devices: 57.7 us -> 42.3 us
  starting transfers between devices: 8.85 us -> 18.3 us
  Pallas kernels: 156 us -> 149 us
  local copies, waits for them, and re-layouts: 8.07 us -> 5.3 us
    ppermute x15 -> x30, waiting for transfers between devices: 57.7 us -> 42.3 us  [the longest x6 22.7 us: next_hop(): return lax.ppermute(x, 'head', [(i, (i + 1) % ring) for i in range(ring)])]
    ppermute x15 -> x30, starting transfers between devices: 8.85 us -> 18.3 us  [the longest x8 9.02 us: next_chip(): lax.ppermute(x, 'blk', [(i, (i + CORES) % blocks) for i in range(blocks)])]
    pallas_call x3 -> x2, Pallas kernels: 156 us -> 149 us  [attend(): pl.pallas_call(functools.partial(attend_kernel, sizes), grid_spec=pltpu.P...]
    unnamed x9 -> x6, local copies, waits for them, and re-layouts: 7.1 us -> 1.6 us
    slice x0 -> x4, local copies, waits for them, and re-layouts: none -> 3.7 us  [the longest x2 1.86 us: packed(): key_rows[:, columns]]
  transfers between devices with their start and end apart: 15 -> 30, of which waited for: 5 -> 13; matrix products, arithmetic and copies ran while one was open for 0% -> 1% of each run, Pallas kernels for 9% -> 42%
where the time goes in v4:
time: 215 us
  Pallas kernels  149 us (69%)
  waiting for transfers between devices  42.3 us (20%)
  starting transfers between devices  18.3 us (9%)
  local copies, waits for them, and re-layouts  5.3 us (2%)
    pallas_call x2, Pallas kernels, attend(): pl.pallas_call(functools.partial(attend_kernel, sizes), grid_spec=pltpu.P...  149 us
    ppermute x6, waiting for transfers between devices, next_hop(): return lax.ppermute(x, 'head', [(i, (i + 1) % ring) for i in range(ring)])  22.7 us
    ppermute x8, waiting for transfers between devices, next_chip(): lax.ppermute(x, 'blk', [(i, (i + CORES) % blocks) for i in range(blocks)])  18.1 us
    ppermute x8, starting transfers between devices, next_chip(): lax.ppermute(x, 'blk', [(i, (i + CORES) % blocks) for i in range(blocks)])  9.02 us
    ppermute x6, starting transfers between devices, next_hop(): return lax.ppermute(x, 'head', [(i, (i + 1) % ring) for i in range(ring)])  6.35 us
  transfers between devices with their start and end apart: 30, of which 13 were waited for; matrix products, arithmetic and copies ran while one was open for 1% of the time, Pallas kernels for 42%

profile of v4, /device:TPU:0, one launch (start us, length us, event | category | flops | bytes accessed | tf_op | source)
XLA Modules:
  0.0 214.7 jit_solution(13869717436929392389)
XLA Ops:
  0.0 1.0 slice.14
  1.0 0.9 slice.15
  1.9 3.1 %collective-permute-start = (bf16[128,1280]{1,0:T(8,128)(2,1)S(1)}, bf16[128,1280]{1,0:T(8,128)(2,1)S(1)}, u32[]{:S(2)}, u32[]{:S(2)}) collective-permute-start(bf16[128,1280]{1,0:T(8,128)(2,1)S(1)} %pad_maximum_fusion.refs_0_), channel_id=1, source_target_pairs={{0,1},{1,2},{2,3},{3,0},{4,5},{5,6},{6,7},{7,4},{8,9},{9,10},{10,1... | collective-permute-start | bytes 983048 | tf_op jit(solution)/shard_map/ppermute | solution.py:211
  5.0 1.5 collective-permute-start.1
  6.5 8.2 %collective-permute-done.refs_1_ = bf16[128,1280]{1,0:T(8,128)(2,1)S(1)} collective-permute-done((bf16[128,1280]{1,0:T(8,128)(2,1)S(1)}, bf16[128,1280]{1,0:T(8,128)(2,1)S(1)}, u32[]{:S(2)}, u32[]{:S(2)}) %collective-permute-start) | collective-permute-done | bytes 327712 | tf_op jit(solution)/shard_map/ppermute | solution.py:211
  14.8 1.0 collective-permute-start.2
  15.8 1.5 collective-permute-start.4
  17.3 0.9 slice.12
  18.2 0.9 slice.13
  19.1 0.6 collective-permute-start.5
  19.7 0.5 collective-permute-start.18
  20.2 7.7 %collective-permute-done.5.refs_8_ = bf16[128,768]{1,0:T(8,128)(2,1)S(1)} collective-permute-done((bf16[128,768]{1,0:T(8,128)(2,1)S(1)}, bf16[128,768]{1,0:T(8,128)(2,1)S(1)}, u32[]{:S(2)}, u32[]{:S(2)}) %collective-permute-start.5) | collective-permute-done | bytes 196640 | tf_op jit(solution)/shard_map/ppermute | solution.py:214
  28.0 1.6 collective-permute-start.6
  29.5 0.7 collective-permute-start.3
  30.2 1.4 collective-permute-start.8
  31.6 7.8 %collective-permute-done.6.refs_3_ = bf16[128,1280]{1,0:T(8,128)(2,1)S(1)} collective-permute-done((bf16[128,1280]{1,0:T(8,128)(2,1)S(1)}, bf16[128,1280]{1,0:T(8,128)(2,1)S(1)}, u32[]{:S(2)}, u32[]{:S(2)}) %collective-permute-start.6) | collective-permute-done | bytes 327712 | tf_op jit(solution)/shard_map/ppermute | solution.py:211
  39.5 1.0 collective-permute-start.21
  40.5 1.1 collective-permute-done.3.refs_1_
  41.6 0.6 collective-permute-start.20
  42.3 4.8 %collective-permute-done.21.refs_11_ = bf16[128,1280]{1,0:T(8,128)(2,1)S(1)} collective-permute-done((bf16[128,1280]{1,0:T(8,128)(2,1)S(1)}, bf16[128,1280]{1,0:T(8,128)(2,1)S(1)}, u32[]{:S(2)}, u32[]{:S(2)}) %collective-permute-start.21) | collective-permute-done | bytes 327712 | tf_op jit(solution)/shard_map/ppermute | solution.py:214
  47.1 3.6 %collective-permute-done.7.refs_2_ = bf16[128,768]{1,0:T(8,128)(2,1)S(1)} collective-permute-done((bf16[128,768]{1,0:T(8,128)(2,1)S(1)}, bf16[128,768]{1,0:T(8,128)(2,1)S(1)}, u32[]{:S(2)}, u32[]{:S(2)}) %collective-permute-start.7) | collective-permute-done | bytes 196640 | tf_op jit(solution)/shard_map/ppermute | solution.py:211
  50.7 1.0 collective-permute-start.14
  51.7 5.5 %collective-permute-done.14.refs_9_ = bf16[128,768]{1,0:T(8,128)(2,1)S(1)} collective-permute-done((bf16[128,768]{1,0:T(8,128)(2,1)S(1)}, bf16[128,768]{1,0:T(8,128)(2,1)S(1)}, u32[]{:S(2)}, u32[]{:S(2)}) %collective-permute-start.14) | collective-permute-done | bytes 196640 | tf_op jit(solution)/shard_map/ppermute | solution.py:214
  57.2 0.5 collective-permute-start.26
  57.8 1.9 collective-permute-done.9.refs_3_
  59.8 1.0 collective-permute-start.15
  60.8 1.0 collective-permute-start.16
  61.8 1.6 copy-done
  63.4 91.0 %shard_map.55.refs_16_ = bf16[128,8192]{1,0:T(8,128)(2,1)} custom-call(s32[4]{0:T(128)S(1)} %copy-done.1, s32[2]{0:T(128)S(1)} %copy-done.2, bf16[128,8192]{1,0:T(8,128)(2,1)S(1)} %copy-done, bf16[128,1280]{1,0:T(8,128)(2,1)S(1)} %pad_maximum_fusion.refs_0_, bf16[128,1280]{1,0:T(8,128)(2,1)S(1)} %collective-permute-done.refs_1_, ...), custom_call_target="tpu_custom_call" | custom-call | flops 6039797760 | bytes 8388608 | tf_op jit(solution)/shard_map/pallas_call | solution.py:178
  154.5 0.5 collective-permute-start.12
  155.1 0.4 collective-permute-start.28
  157.1 57.7 %shard_map.56 = bf16[128,8192]{1,0:T(8,128)(2,1)} custom-call(s32[4]{0:T(128)S(1)} %copy-done.1, s32[2]{0:T(128)S(1)} %copy-done.2, bf16[128,8192]{1,0:T(8,128)(2,1)S(1)} %copy-done, bf16[128,768]{1,0:T(8,128)(2,1)S(1)} %pad_maximum_fusion.1.refs_0_, bf16[128,768]{1,0:T(8,128)(2,1)S(1)} %collective-permute-done.3.refs_1_, ...), custom_call_target="tpu_custom_call", output_to_operand_aliasing={{}: (19, {})} | custom-call | flops 3623878656 | bytes 8388608 | tf_op jit(solution)/shard_map/pallas_call | solution.py:178
  (42 shorter events, 2.0 us)
Async XLA Ops:
  0.0 61.8 %copy-start.1 = (s32[4]{0:T(128)S(1)}, s32[4]{0:T(128)}, u32[]{:S(2)}) copy-start(s32[4]{0:T(128)} %placement.3) | copy-start | bytes 52
  0.0 61.8 %copy-start.2 = (s32[2]{0:T(128)S(1)}, s32[2]{0:T(128)}, u32[]{:S(2)}) copy-start(s32[2]{0:T(128)} %lengths.3) | copy-start | bytes 28
  1.9 12.8 %collective-permute-start = (bf16[128,1280]{1,0:T(8,128)(2,1)S(1)}, bf16[128,1280]{1,0:T(8,128)(2,1)S(1)}, u32[]{:S(2)}, u32[]{:S(2)}) collective-permute-start(bf16[128,1280]{1,0:T(8,128)(2,1)S(1)} %pad_maximum_fusion.refs_0_), channel_id=1, source_target_pairs={{0,1},{1,2},{2,3},{3,0},{4,5},{5,6},{6,7},{7,4},{8,9},{9,10},{10,1... | collective-permute-start | bytes 983048 | tf_op jit(solution)/shard_map/ppermute | solution.py:211
  5.0 9.7 %collective-permute-start.1 = (bf16[128,1280]{1,0:T(8,128)(2,1)S(1)}, bf16[128,1280]{1,0:T(8,128)(2,1)S(1)}, u32[]{:S(2)}, u32[]{:S(2)}) collective-permute-start(bf16[128,1280]{1,0:T(8,128)(2,1)S(1)} %pad_maximum_fusion.refs_0_), channel_id=1, source_target_pairs={{0,8},{4,12},{8,0},{12,4},{1,9},{5,13},{9,1},{13,5},{2,10},{6,14},... | collective-permute-start | bytes 983048 | tf_op jit(solution)/shard_map/ppermute | solution.py:214
  14.8 13.2 %collective-permute-start.2 = (bf16[128,1280]{1,0:T(8,128)(2,1)S(1)}, bf16[128,1280]{1,0:T(8,128)(2,1)S(1)}, u32[]{:S(2)}, u32[]{:S(2)}) collective-permute-start(bf16[128,1280]{1,0:T(8,128)(2,1)S(1)} %collective-permute-done.refs_1_), channel_id=1, source_target_pairs={{0,1},{1,2},{2,3},{3,0},{4,5},{5,6},{6,7},{7,4},{8,9},{9,10},{10,1... | collective-permute-start | bytes 983048 | tf_op jit(solution)/shard_map/ppermute | solution.py:211
  15.8 12.2 %collective-permute-start.4 = (bf16[128,1280]{1,0:T(8,128)(2,1)S(1)}, bf16[128,1280]{1,0:T(8,128)(2,1)S(1)}, u32[]{:S(2)}, u32[]{:S(2)}) collective-permute-start(bf16[128,1280]{1,0:T(8,128)(2,1)S(1)} %collective-permute-done.refs_1_), channel_id=1, source_target_pairs={{0,8},{4,12},{8,0},{12,4},{1,9},{5,13},{9,1},{13,5},{2,10},{6,14},... | collective-permute-start | bytes 983048 | tf_op jit(solution)/shard_map/ppermute | solution.py:214
  19.1 8.9 %collective-permute-start.5 = (bf16[128,768]{1,0:T(8,128)(2,1)S(1)}, bf16[128,768]{1,0:T(8,128)(2,1)S(1)}, u32[]{:S(2)}, u32[]{:S(2)}) collective-permute-start(bf16[128,768]{1,0:T(8,128)(2,1)S(1)} %pad_maximum_fusion.1.refs_0_), channel_id=1, source_target_pairs={{0,8},{4,12},{8,0},{12,4},{1,9},{5,13},{9,1},{13,5},{2,10},{6,14},... | collective-permute-start | bytes 589832 | tf_op jit(solution)/shard_map/ppermute | solution.py:214
  19.7 10.5 %collective-permute-start.17 = (bf16[128,1280]{1,0:T(8,128)(2,1)S(1)}, bf16[128,1280]{1,0:T(8,128)(2,1)S(1)}, u32[]{:S(2)}, u32[]{:S(2)}) collective-permute-start(bf16[128,1280]{1,0:T(8,128)(2,1)S(1)} %pad_maximum_fusion.refs_0_), channel_id=1, source_target_pairs={{0,4},{4,0},{8,12},{12,8},{1,5},{5,1},{9,13},{13,9},{2,6},{6,2},{1... | collective-permute-start | bytes 983048 | tf_op jit(solution)/shard_map/ppermute | solution.py:217
  19.7 11.9 %collective-permute-start.18 = (bf16[128,1280]{1,0:T(8,128)(2,1)S(1)}, bf16[128,1280]{1,0:T(8,128)(2,1)S(1)}, u32[]{:S(2)}, u32[]{:S(2)}) collective-permute-start(bf16[128,1280]{1,0:T(8,128)(2,1)S(1)} %collective-permute-done.refs_1_), channel_id=1, source_target_pairs={{0,4},{4,0},{8,12},{12,8},{1,5},{5,1},{9,13},{13,9},{2,6},{6,2},{1... | collective-permute-start | bytes 983048 | tf_op jit(solution)/shard_map/ppermute | solution.py:217
  28.0 11.5 %collective-permute-start.6 = (bf16[128,1280]{1,0:T(8,128)(2,1)S(1)}, bf16[128,1280]{1,0:T(8,128)(2,1)S(1)}, u32[]{:S(2)}, u32[]{:S(2)}) collective-permute-start(bf16[128,1280]{1,0:T(8,128)(2,1)S(1)} %collective-permute-done.2.refs_2_), channel_id=1, source_target_pairs={{0,1},{1,2},{2,3},{3,0},{4,5},{5,6},{6,7},{7,4},{8,9},{9,10},{10,1... | collective-permute-start | bytes 983048 | tf_op jit(solution)/shard_map/ppermute | solution.py:211
  29.5 12.0 %collective-permute-start.22 = (bf16[128,1280]{1,0:T(8,128)(2,1)S(1)}, bf16[128,1280]{1,0:T(8,128)(2,1)S(1)}, u32[]{:S(2)}, u32[]{:S(2)}) collective-permute-start(bf16[128,1280]{1,0:T(8,128)(2,1)S(1)} %collective-permute-done.1.refs_8_), channel_id=1, source_target_pairs={{0,4},{4,0},{8,12},{12,8},{1,5},{5,1},{9,13},{13,9},{2,6},{6,2},{1... | collective-permute-start | bytes 983048 | tf_op jit(solution)/shard_map/ppermute | solution.py:217
  29.5 12.0 %collective-permute-start.3 = (bf16[128,768]{1,0:T(8,128)(2,1)S(1)}, bf16[128,768]{1,0:T(8,128)(2,1)S(1)}, u32[]{:S(2)}, u32[]{:S(2)}) collective-permute-start(bf16[128,768]{1,0:T(8,128)(2,1)S(1)} %pad_maximum_fusion.1.refs_0_), channel_id=1, source_target_pairs={{0,1},{1,2},{2,3},{3,0},{4,5},{5,6},{6,7},{7,4},{8,9},{9,10},{10,1... | collective-permute-start | bytes 589832 | tf_op jit(solution)/shard_map/ppermute | solution.py:211
  30.2 11.4 %collective-permute-start.8 = (bf16[128,1280]{1,0:T(8,128)(2,1)S(1)}, bf16[128,1280]{1,0:T(8,128)(2,1)S(1)}, u32[]{:S(2)}, u32[]{:S(2)}) collective-permute-start(bf16[128,1280]{1,0:T(8,128)(2,1)S(1)} %collective-permute-done.2.refs_2_), channel_id=1, source_target_pairs={{0,8},{4,12},{8,0},{12,4},{1,9},{5,13},{9,1},{13,5},{2,10},{6,14},... | collective-permute-start | bytes 983048 | tf_op jit(solution)/shard_map/ppermute | solution.py:214
  31.6 10.5 %collective-permute-start.19 = (bf16[128,1280]{1,0:T(8,128)(2,1)S(1)}, bf16[128,1280]{1,0:T(8,128)(2,1)S(1)}, u32[]{:S(2)}, u32[]{:S(2)}) collective-permute-start(bf16[128,1280]{1,0:T(8,128)(2,1)S(1)} %collective-permute-done.2.refs_2_), channel_id=1, source_target_pairs={{0,4},{4,0},{8,12},{12,8},{1,5},{5,1},{9,13},{13,9},{2,6},{6,2},{1... | collective-permute-start | bytes 983048 | tf_op jit(solution)/shard_map/ppermute | solution.py:217
  39.5 7.6 %collective-permute-start.21 = (bf16[128,1280]{1,0:T(8,128)(2,1)S(1)}, bf16[128,1280]{1,0:T(8,128)(2,1)S(1)}, u32[]{:S(2)}, u32[]{:S(2)}) collective-permute-start(bf16[128,1280]{1,0:T(8,128)(2,1)S(1)} %collective-permute-done.6.refs_3_), channel_id=1, source_target_pairs={{0,8},{4,12},{8,0},{12,4},{1,9},{5,13},{9,1},{13,5},{2,10},{6,14},... | collective-permute-start | bytes 983048 | tf_op jit(solution)/shard_map/ppermute | solution.py:214
  41.6 10.1 %collective-permute-start.23 = (bf16[128,1280]{1,0:T(8,128)(2,1)S(1)}, bf16[128,1280]{1,0:T(8,128)(2,1)S(1)}, u32[]{:S(2)}, u32[]{:S(2)}) collective-permute-start(bf16[128,1280]{1,0:T(8,128)(2,1)S(1)} %collective-permute-done.4.refs_9_), channel_id=1, source_target_pairs={{0,4},{4,0},{8,12},{12,8},{1,5},{5,1},{9,13},{13,9},{2,6},{6,2},{1... | collective-permute-start | bytes 983048 | tf_op jit(solution)/shard_map/ppermute | solution.py:217
  41.6 9.1 %collective-permute-start.7 = (bf16[128,768]{1,0:T(8,128)(2,1)S(1)}, bf16[128,768]{1,0:T(8,128)(2,1)S(1)}, u32[]{:S(2)}, u32[]{:S(2)}) collective-permute-start(bf16[128,768]{1,0:T(8,128)(2,1)S(1)} %collective-permute-done.3.refs_1_), channel_id=1, source_target_pairs={{0,1},{1,2},{2,3},{3,0},{4,5},{5,6},{6,7},{7,4},{8,9},{9,10},{10,1... | collective-permute-start | bytes 589832 | tf_op jit(solution)/shard_map/ppermute | solution.py:211
  41.6 15.6 %collective-permute-start.20 = (bf16[128,1280]{1,0:T(8,128)(2,1)S(1)}, bf16[128,1280]{1,0:T(8,128)(2,1)S(1)}, u32[]{:S(2)}, u32[]{:S(2)}) collective-permute-start(bf16[128,1280]{1,0:T(8,128)(2,1)S(1)} %collective-permute-done.6.refs_3_), channel_id=1, source_target_pairs={{0,4},{4,0},{8,12},{12,8},{1,5},{5,1},{9,13},{13,9},{2,6},{6,2},{1... | collective-permute-start | bytes 983048 | tf_op jit(solution)/shard_map/ppermute | solution.py:217
  42.2 15.6 %collective-permute-start.24 = (bf16[128,1280]{1,0:T(8,128)(2,1)S(1)}, bf16[128,1280]{1,0:T(8,128)(2,1)S(1)}, u32[]{:S(2)}, u32[]{:S(2)}) collective-permute-start(bf16[128,1280]{1,0:T(8,128)(2,1)S(1)} %collective-permute-done.8.refs_10_), channel_id=1, source_target_pairs={{0,4},{4,0},{8,12},{12,8},{1,5},{5,1},{9,13},{13,9},{2,6},{6,2},{1... | collective-permute-start | bytes 983048 | tf_op jit(solution)/shard_map/ppermute | solution.py:217
  47.1 13.7 %collective-permute-start.25 = (bf16[128,1280]{1,0:T(8,128)(2,1)S(1)}, bf16[128,1280]{1,0:T(8,128)(2,1)S(1)}, u32[]{:S(2)}, u32[]{:S(2)}) collective-permute-start(bf16[128,1280]{1,0:T(8,128)(2,1)S(1)} %collective-permute-done.21.refs_11_), channel_id=1, source_target_pairs={{0,4},{4,0},{8,12},{12,8},{1,5},{5,1},{9,13},{13,9},{2,6},{6,2},{1... | collective-permute-start | bytes 983048 | tf_op jit(solution)/shard_map/ppermute | solution.py:217
  50.7 6.5 %collective-permute-start.14 = (bf16[128,768]{1,0:T(8,128)(2,1)S(1)}, bf16[128,768]{1,0:T(8,128)(2,1)S(1)}, u32[]{:S(2)}, u32[]{:S(2)}) collective-permute-start(bf16[128,768]{1,0:T(8,128)(2,1)S(1)} %collective-permute-done.3.refs_1_), channel_id=1, source_target_pairs={{0,8},{4,12},{8,0},{12,4},{1,9},{5,13},{9,1},{13,5},{2,10},{6,14},... | collective-permute-start | bytes 589832 | tf_op jit(solution)/shard_map/ppermute | solution.py:214
  51.7 8.1 %collective-permute-start.9 = (bf16[128,768]{1,0:T(8,128)(2,1)S(1)}, bf16[128,768]{1,0:T(8,128)(2,1)S(1)}, u32[]{:S(2)}, u32[]{:S(2)}) collective-permute-start(bf16[128,768]{1,0:T(8,128)(2,1)S(1)} %collective-permute-done.7.refs_2_), channel_id=1, source_target_pairs={{0,1},{1,2},{2,3},{3,0},{4,5},{5,6},{6,7},{7,4},{8,9},{9,10},{10,1... | collective-permute-start | bytes 589832 | tf_op jit(solution)/shard_map/ppermute | solution.py:211
  57.2 97.3 %collective-permute-start.10 = (bf16[128,768]{1,0:T(8,128)(2,1)S(1)}, bf16[128,768]{1,0:T(8,128)(2,1)S(1)}, u32[]{:S(2)}, u32[]{:S(2)}) collective-permute-start(bf16[128,768]{1,0:T(8,128)(2,1)S(1)} %pad_maximum_fusion.1.refs_0_), channel_id=1, source_target_pairs={{0,4},{4,0},{8,12},{12,8},{1,5},{5,1},{9,13},{13,9},{2,6},{6,2},{1... | collective-permute-start | bytes 589832 | tf_op jit(solution)/shard_map/ppermute | solution.py:217
  57.2 97.8 %collective-permute-start.26 = (bf16[128,768]{1,0:T(8,128)(2,1)S(1)}, bf16[128,768]{1,0:T(8,128)(2,1)S(1)}, u32[]{:S(2)}, u32[]{:S(2)}) collective-permute-start(bf16[128,768]{1,0:T(8,128)(2,1)S(1)} %collective-permute-done.5.refs_8_), channel_id=1, source_target_pairs={{0,4},{4,0},{8,12},{12,8},{1,5},{5,1},{9,13},{13,9},{2,6},{6,2},{1... | collective-permute-start | bytes 589832 | tf_op jit(solution)/shard_map/ppermute | solution.py:217
  57.8 97.8 %collective-permute-start.11 = (bf16[128,768]{1,0:T(8,128)(2,1)S(1)}, bf16[128,768]{1,0:T(8,128)(2,1)S(1)}, u32[]{:S(2)}, u32[]{:S(2)}) collective-permute-start(bf16[128,768]{1,0:T(8,128)(2,1)S(1)} %collective-permute-done.3.refs_1_), channel_id=1, source_target_pairs={{0,4},{4,0},{8,12},{12,8},{1,5},{5,1},{9,13},{13,9},{2,6},{6,2},{1... | collective-permute-start | bytes 589832 | tf_op jit(solution)/shard_map/ppermute | solution.py:217
  59.8 95.4 %collective-permute-start.15 = (bf16[128,768]{1,0:T(8,128)(2,1)S(1)}, bf16[128,768]{1,0:T(8,128)(2,1)S(1)}, u32[]{:S(2)}, u32[]{:S(2)}) collective-permute-start(bf16[128,768]{1,0:T(8,128)(2,1)S(1)} %collective-permute-done.7.refs_2_), channel_id=1, source_target_pairs={{0,8},{4,12},{8,0},{12,4},{1,9},{5,13},{9,1},{13,5},{2,10},{6,14},... | collective-permute-start | bytes 589832 | tf_op jit(solution)/shard_map/ppermute | solution.py:214
  60.8 93.7 %collective-permute-start.16 = (bf16[128,768]{1,0:T(8,128)(2,1)S(1)}, bf16[128,768]{1,0:T(8,128)(2,1)S(1)}, u32[]{:S(2)}, u32[]{:S(2)}) collective-permute-start(bf16[128,768]{1,0:T(8,128)(2,1)S(1)} %collective-permute-done.9.refs_3_), channel_id=1, source_target_pairs={{0,8},{4,12},{8,0},{12,4},{1,9},{5,13},{9,1},{13,5},{2,10},{6,14},... | collective-permute-start | bytes 589832 | tf_op jit(solution)/shard_map/ppermute | solution.py:214
  154.4 1.5 collective-permute-start.27
  154.5 1.7 collective-permute-start.12
  155.0 1.5 collective-permute-start.13
  155.1 1.7 collective-permute-start.28
  155.5 1.5 collective-permute-start.29
  (1 other events, 1.6 us)

commit v5 on v4

v5 whole, which is shorter than its diff:
```python
import functools
import math

import jax
import jax.numpy as jnp
from jax import lax
from jax.experimental import pallas as pl
from jax.experimental.pallas import tpu as pltpu
from jax.sharding import PartitionSpec as P

HD = 128
CORES = 2
HEADS_PER_TILE = 2
SPLIT = (4, 8)
EXP2_SCALE = math.log2(math.e) / math.sqrt(HD)
LEAST_TOTAL, MOST_TOTAL = 1e-20, 1e30


def matmul_nt(a, b):
    return lax.dot_general(a, b, (((1,), (1,)), ((), ())), preferred_element_type=jnp.float32)


class Place:
    def __init__(self, sizes, info):
        self.prompt_count, self.chips, self.ring, self.tokens = sizes
        self.blocks, self.slots = self.chips * CORES, self.prompt_count + 1
        self.info = info

    def source(self, slot):
        return self.info[2 + slot]

    def first_key(self, slot):
        return self.info[2 + self.slots + slot]

    def kept(self):
        offsets = self.info[1] + lax.broadcasted_iota(jnp.int32, (self.tokens, 1), 0)
        return offsets < self.info[0]


def exact(here, query, key, value, out, group):
    slots, tokens, rows = here.prompt_count + 1, here.tokens, here.ring * here.tokens
    key_row = lax.broadcasted_iota(jnp.int32, (tokens, rows), 1)
    newest_own = rows - tokens + lax.broadcasted_iota(jnp.int32, (tokens, rows), 0)

    def one_head(head, carry):
        columns = pl.ds(pl.multiple_of(head * HD, HD), HD)
        query_one = query[:, columns]

        def part(ref, slot):
            return ref[pl.ds(pl.multiple_of(slot * rows, rows), rows), :]

        def score(slot):
            newest = jnp.where(slot == here.prompt_count, newest_own, rows)
            seen = (key_row >= here.first_key(slot)) & (key_row <= newest)
            return jnp.where(seen, matmul_nt(query_one, part(key, slot)), -jnp.inf)

        row_max = lax.fori_loop(
            0,
            slots,
            lambda j, best: jnp.maximum(best, jnp.max(score(j), axis=1, keepdims=True)),
            jnp.full((tokens, 1), -jnp.inf, jnp.float32),
        )

        def add(slot, carry):
            total, summed = carry
            weights = jnp.exp2((score(slot) - row_max) * EXP2_SCALE)
            total += jnp.sum(weights, axis=1, keepdims=True)
            weights = weights.astype(jnp.bfloat16)
            return total, summed + jnp.dot(weights, part(value, slot), preferred_element_type=jnp.float32)

        zeros = jnp.zeros((tokens, 1), jnp.float32), jnp.zeros((tokens, HD), jnp.float32)
        total, summed = lax.fori_loop(0, slots, add, zeros)
        out[:, columns] = jnp.where(here.kept(), summed / total, 0.0).astype(out.dtype)
        return carry

    lax.fori_loop(0, group, one_head, 0)


def attend_kernel(sizes, where, groups, info, query, *refs):
    prompt_count, chips, ring, tokens = sizes
    here = Place(sizes, info)
    arrays, (out, held, ones, bias, sems) = refs[:-5], refs[-5:]
    kv_head = pl.program_id(0)
    group = query.shape[1] // HD
    masked = bias.shape[1]

    def at(slot, hop):
        return pl.ds(pl.multiple_of((slot * ring + ring - 1 - hop) * tokens, tokens), tokens)

    def seen(slot, hop):
        return (ring - 1 - hop) * tokens >= here.first_key(slot)

    def fetch_of(index, source, slot, hop):
        chunk, low, high, first = groups[index]
        array, column = where[chunk, source, hop]
        return pltpu.make_async_copy(
            arrays[array].at[:, (column + low) * 2 * HD : (column + high) * 2 * HD],
            held.at[at(slot, hop), first * 2 * HD : (first + high - low) * 2 * HD],
            sems.at[index, slot, hop],
        )

    @pl.when(kv_head == 0)
    def _():
        for index in range(len(groups)):

            def fetch(slot, carry):
                wanted = here.source(slot)
                for source in range(here.blocks):

                    @pl.when(wanted == source)
                    def _():
                        for hop in range(ring):

                            @pl.when(seen(slot, hop))
                            def _():
                                fetch_of(index, source, slot, hop).start()

                return carry

            lax.fori_loop(0, here.slots, fetch, 0)

        def fill(slot, carry):
            for hop in range(ring):
                count = jnp.where(seen(slot, hop), 1.0, 0.0)
                ones[at(slot, hop)] = jnp.full((tokens, HD), count, jnp.float32).astype(ones.dtype)

                @pl.when(jnp.logical_not(seen(slot, hop)))
                def _():
                    held[at(slot, hop)] = jnp.zeros((tokens, held.shape[1]), held.dtype)

            return carry

        lax.fori_loop(0, here.slots, fill, 0)
        own = lax.broadcasted_iota(jnp.int32, (tokens, masked), 0)
        key = lax.broadcasted_iota(jnp.int32, (tokens, masked), 1) - (masked - tokens)
        bias[...] = jnp.where(key <= own, 0.0, -jnp.inf)

    for index, (_, _, _, first) in enumerate(groups):

        @pl.when(kv_head == first)
        def _():
            def finish(slot, carry):
                for hop in range(ring):

                    @pl.when(seen(slot, hop))
                    def _():
                        fetch_of(index, 0, slot, hop).wait()

                return carry

            lax.fori_loop(0, here.slots, finish, 0)

    key = held.at[:, pl.ds(pl.multiple_of(kv_head * 2 * HD, 2 * HD), HD)]
    value = held.at[:, pl.ds(pl.multiple_of(kv_head * 2 * HD + HD, HD), HD)]
    keys, values = key[...], jnp.concatenate([value[...], ones[...]], axis=1)
    kept = here.kept()
    least = jnp.full((tokens, HD), jnp.inf, jnp.float32)
    most = jnp.zeros((tokens, HD), jnp.float32)
    for tile in range(group // HEADS_PER_TILE):
        heads = range(tile * HEADS_PER_TILE, (tile + 1) * HEADS_PER_TILE)
        query_tile = jnp.concatenate([query[:, h * HD : (h + 1) * HD] for h in heads], axis=0)
        scores = matmul_nt(query_tile, keys) * EXP2_SCALE
        split = scores.shape[1] - masked
        tail = scores[:, split:].reshape(HEADS_PER_TILE, tokens, masked) + bias[...][None]
        tail = tail.reshape(HEADS_PER_TILE * tokens, masked)
        scores = tail if split == 0 else jnp.concatenate([scores[:, :split], tail], axis=1)
        weights = jnp.exp2(scores).astype(jnp.bfloat16)
        summed = jnp.dot(weights, values, preferred_element_type=jnp.float32)
        for i, h in enumerate(heads):
            part = summed[i * tokens : (i + 1) * tokens]
            total = part[:, HD:]
            least, most = jnp.minimum(least, total), jnp.maximum(most, total)
            out[:, h * HD : (h + 1) * HD] = jnp.where(kept, part[:, :HD] / total, 0.0).astype(out.dtype)
    safe = (jnp.min(least) > LEAST_TOTAL) & (jnp.max(most) < MOST_TOTAL)

    @pl.when(jnp.logical_not(safe))
    def _():
        exact(here, query, key, value, out, group)


def attend(info, query_rows, arrays, where, groups, sizes, kv_heads):
    prompt_count, chips, ring, tokens = sizes
    slots = prompt_count + 1
    group = query_rows.shape[1] // HD // kv_heads
    own_spec = pl.BlockSpec((tokens, group * HD), lambda g, *_: (0, g))
    whole = pl.BlockSpec(memory_space=pl.ANY)
    keys = slots * ring * tokens
    masked = tokens if tokens % HD == 0 else keys
    work = tokens * group * kv_heads * keys
    return pl.pallas_call(
        functools.partial(attend_kernel, sizes, where, groups),
        grid_spec=pltpu.PrefetchScalarGridSpec(
            num_scalar_prefetch=1,
            grid=(kv_heads,),
            in_specs=[own_spec] + [whole] * len(arrays),
            out_specs=own_spec,
            scratch_shapes=[
                pltpu.VMEM((keys, kv_heads * 2 * HD), jnp.bfloat16),
                pltpu.VMEM((keys, HD), jnp.bfloat16),
                pltpu.VMEM((tokens, masked), jnp.float32),
                pltpu.SemaphoreType.DMA((len(groups), slots, ring)),
            ],
        ),
        out_shape=jax.ShapeDtypeStruct(query_rows.shape, query_rows.dtype),
        cost_estimate=pl.CostEstimate(flops=6 * work * HD, bytes_accessed=12 << 20, transcendentals=work),
        compiler_params=pltpu.CompilerParams(vmem_limit_bytes=40 << 20),
    )(info, pltpu.with_memory_space_constraint(query_rows, pltpu.HBM), *arrays)


def pack_kernel(first, end, key, value, out, sems):
    copies = []
    for h in range(first, end):
        for i, x in enumerate((key, value)):
            place = 2 * (h - first) + i
            column = out.at[:, place * HD : (place + 1) * HD]
            copies.append(pltpu.make_async_copy(x.at[:, h * HD : (h + 1) * HD], column, sems.at[place]))
    for copy in copies:
        copy.start()
    for copy in copies:
        copy.wait()


def pack(key_rows, value_rows, first, end):
    whole = pl.BlockSpec(memory_space=pl.ANY)
    count = 2 * (end - first)
    return pl.pallas_call(
        functools.partial(pack_kernel, first, end),
        in_specs=[whole, whole],
        out_specs=whole,
        scratch_shapes=[pltpu.SemaphoreType.DMA((count,))],
        out_shape=jax.ShapeDtypeStruct((key_rows.shape[0], count * HD), key_rows.dtype),
        cost_estimate=pl.CostEstimate(flops=0, bytes_accessed=1 << 19, transcendentals=0),
    )(key_rows, value_rows)


def after(x, *others):
    return lax.optimization_barrier((x, *others))[0]


def scalars(placement, lengths, sizes):
    prompt_count, chips, ring, tokens = sizes
    blocks = chips * CORES
    index, head = lax.axis_index("blk"), lax.axis_index("head")
    block = jnp.sum(jnp.where(jnp.arange(blocks) == index, placement, 0))
    length = jnp.sum(jnp.where(jnp.arange(prompt_count) == block - prompt_count, lengths, 0))
    keep = jnp.where(block >= prompt_count, length, ring * tokens)
    prompt = jnp.arange(prompt_count)
    found = jnp.sum(jnp.where(placement[None, :] == prompt[:, None], jnp.arange(blocks)[None, :], 0), axis=1)
    source = (index // CORES - found // CORES) % chips * CORES + (index + found) % CORES
    first_key = jnp.where(block > prompt, 0, ring * tokens)
    parts = [keep[None], (head * tokens)[None], source, jnp.zeros((1,), jnp.int32), first_key]
    return jnp.concatenate([x.astype(jnp.int32) for x in parts] + [((ring - 1 - head) * tokens)[None]])


def shards(query_rows, key_rows, value_rows, placement, lengths):
    blocks, ring = lax.axis_size("blk"), lax.axis_size("head")
    chips = blocks // CORES
    sizes = (blocks // 2, chips, ring, query_rows.shape[0])
    kv_heads = key_rows.shape[1] // HD
    cut = kv_heads * SPLIT[0] // SPLIT[1]

    def next_hop(x):
        return lax.ppermute(x, "head", [(i, (i + 1) % ring) for i in range(ring)])

    def next_chip(x):
        return lax.ppermute(x, "blk", [(i, (i + CORES) % blocks) for i in range(blocks)])

    def other_core(x):
        return lax.ppermute(x, "blk", [(i, i ^ 1) for i in range(blocks)])

    bounds = (0, cut, kv_heads)
    owns = [pack(key_rows, value_rows, bounds[c], bounds[c + 1]) for c in range(2)]
    info = scalars(*lax.optimization_barrier((placement, lengths, owns[1]))[:2], sizes)
    columns, acrosses = [[x] for x in owns], [[] for _ in owns]
    for hop in range(ring):
        for c in range(2):
            column, across = columns[c], acrosses[c]
            x = column[hop]
            if hop > 0:
                x = after(x, across[hop - 1], *([info] if hop == 1 else []))
            if hop < ring - 1:
                column.append(next_hop(x))
            if hop < ring - 1 or c == 0:
                across.append(next_chip(x))
            else:
                across.append(next_hop(after(across[-1], x)))
    planes = [columns, acrosses]
    bundles = [[(0, c, hop) for c in range(2)] + [(1, c, hop - 1) for c in range(2) if hop] for hop in range(ring)]
    bundles.append([(1, c, ring - 1) for c in range(2)])
    for back in range(2, chips):
        planes.append([[next_chip(x) for x in part] for part in planes[-1]])
        bundles.append([(back, c, hop) for hop in range(ring) for c in range(2)])
    arrays, where = [], {}
    for back, plane in enumerate(planes):
        for c in range(2):
            for hop in range(ring):
                where[c, back * CORES, hop] = len(arrays), 0
                arrays.append(plane[c][hop])
    for bundle in bundles:
        column = 0
        for back, c, hop in bundle:
            where[c, back * CORES + 1, hop] = len(arrays), column
            column += bounds[c + 1] - bounds[c]
        arrays.append(other_core(jnp.concatenate([planes[back][c][hop] for back, c, hop in bundle], axis=1)))
    groups = [(0, 0, 1, 0), (0, 1, cut, 1), (1, 0, kv_heads - cut, cut)]
    return attend(info, query_rows, arrays, where, groups, sizes, kv_heads)


def solution(mesh):
    rows = P(("grp", "blk", "head"), None)
    return jax.shard_map(
        shards,
        mesh=mesh,
        in_specs=(rows, rows, rows, P("grp"), P("grp")),
        out_specs=rows,
        check_vma=False,
    )
```

time: 215 us -> 219 us (1.019)
  Pallas kernels: 149 us -> 165 us
  waiting for transfers between devices: 42.3 us -> 34 us
  local copies, waits for them, and re-layouts: 5.3 us -> 0.09 us
  starting transfers between devices: 18.3 us -> 13.3 us
  other arithmetic: 0.05 us -> 4.3 us
    pallas_call x2 -> x3, Pallas kernels: 149 us -> 165 us  [the longest x1 147 us: attend(): pl.pallas_call(functools.partial(attend_kernel, sizes, where, groups), gr...]
    ppermute x6 -> x7, waiting for transfers between devices: 22.7 us -> 14.6 us  [next_hop(): return lax.ppermute(x, 'head', [(i, (i + 1) % ring) for i in range(ring)])]
    slice x4 -> x0, local copies, waits for them, and re-layouts: 3.7 us -> none  [the longest x2 1.86 us: packed(): key_rows[:, columns]]
    reduce_sum x0 -> x3, other arithmetic: none -> 3.37 us  [the longest x1 1.32 us: scalars(): block = jnp.sum(jnp.where(jnp.arange(blocks) == index, placement, 0))]
    ppermute x16 -> x5, starting transfers between devices: 2.91 us -> 0.22 us  [other_core(): return lax.ppermute(x, 'blk', [(i, i ^ 1) for i in range(blocks)])]
    ppermute x6 -> x7, starting transfers between devices: 6.35 us -> 4.81 us  [next_hop(): return lax.ppermute(x, 'head', [(i, (i + 1) % ring) for i in range(ring)])]
    ppermute x8 -> x7, starting transfers between devices: 9.02 us -> 8.23 us  [next_chip(): lax.ppermute(x, 'blk', [(i, (i + CORES) % blocks) for i in range(blocks)])]
    ppermute x8 -> x7, waiting for transfers between devices: 18.1 us -> 17.4 us  [next_chip(): lax.ppermute(x, 'blk', [(i, (i + CORES) % blocks) for i in range(blocks)])]
  transfers between devices with their start and end apart: 30 -> 19, of which waited for: 13 -> 11; matrix products, arithmetic and copies ran while one was open for 1% -> 2% of each run, Pallas kernels for 42% -> 4%
where the time goes in v5:
time: 219 us; the launch traced here: 218 us
  Pallas kernels  165 us (75%)
  waiting for transfers between devices  34 us (16%)
  starting transfers between devices  13.3 us (6%)
  other arithmetic  4.3 us (2%)
    pallas_call x1, Pallas kernels, attend(): pl.pallas_call(functools.partial(attend_kernel, sizes, where, groups), gr...  147 us
    pallas_call x2, Pallas kernels, pack(): pl.pallas_call(functools.partial(pack_kernel, first, end), in_specs=[whol...  18.2 us
    ppermute x7, waiting for transfers between devices, next_chip(): lax.ppermute(x, 'blk', [(i, (i + CORES) % blocks) for i in range(blocks)])  17.4 us
    ppermute x7, waiting for transfers between devices, next_hop(): return lax.ppermute(x, 'head', [(i, (i + 1) % ring) for i in range(ring)])  14.6 us
    ppermute x7, starting transfers between devices, next_chip(): lax.ppermute(x, 'blk', [(i, (i + CORES) % blocks) for i in range(blocks)])  8.23 us
    ppermute x7, starting transfers between devices, next_hop(): return lax.ppermute(x, 'head', [(i, (i + 1) % ring) for i in range(ring)])  4.81 us
  transfers between devices with their start and end apart: 19, of which 11 were waited for; matrix products, arithmetic and copies ran while one was open for 2% of the time, Pallas kernels for 4%

profile of v5, /device:TPU:0, one launch (start us, length us, event | category | flops | bytes accessed | tf_op | source)
XLA Modules:
  0.0 218.3 jit_solution(10927076621191497302)
XLA Ops:
  0.0 9.1 %shard_map.56.refs_0_ = bf16[128,1024]{1,0:T(8,128)(2,1)} custom-call(bf16[128,1024]{1,0:T(8,128)(2,1)} %key.3, bf16[128,1024]{1,0:T(8,128)(2,1)} %value.3), custom_call_target="tpu_custom_call" | custom-call | bytes 524288 | tf_op jit(solution)/shard_map/pallas_call | solution.py:226
  9.1 3.0 %collective-permute-start.1 = (bf16[128,1024]{1,0:T(8,128)(2,1)}, bf16[128,1024]{1,0:T(8,128)(2,1)S(1)}, u32[]{:S(2)}, u32[]{:S(2)}) collective-permute-start(bf16[128,1024]{1,0:T(8,128)(2,1)} %shard_map.56.refs_0_), channel_id=1, source_target_pairs={{0,8},{4,12},{8,0},{12,4},{1,9},{5,13},{9,1},{13,5},{2,10},{6,14},... | collective-permute-start | bytes 786440 | tf_op jit(solution)/shard_map/ppermute | solution.py:266
  12.1 1.6 collective-permute-start
  13.7 9.1 %shard_map.55.refs_4_ = bf16[128,1024]{1,0:T(8,128)(2,1)} custom-call(bf16[128,1024]{1,0:T(8,128)(2,1)} %key.3, bf16[128,1024]{1,0:T(8,128)(2,1)} %value.3), custom_call_target="tpu_custom_call" | custom-call | bytes 524288 | tf_op jit(solution)/shard_map/pallas_call | solution.py:226
  22.8 0.6 collective-permute-start.6
  23.4 1.6 collective-permute-start.5
  25.0 0.8 fusion
  25.8 1.3 fusion.2
  27.7 1.3 fusion.3
  30.2 0.7 compare_select_fusion.4
  30.9 0.1 concatenate.18.info
  31.0 1.6 collective-permute-start.3
  32.5 1.6 collective-permute-start.2
  34.1 0.5 collective-permute-start.8
  34.8 0.1 collective-permute-start.15
  34.9 5.4 %collective-permute-done.3.refs_9_ = bf16[128,1024]{1,0:T(8,128)(2,1)S(1)} collective-permute-done((bf16[128,1024]{1,0:T(8,128)(2,1)S(1)}, bf16[128,1024]{1,0:T(8,128)(2,1)S(1)}, u32[]{:S(2)}, u32[]{:S(2)}) %collective-permute-start.3) | collective-permute-done | bytes 262176 | tf_op jit(solution)/shard_map/ppermute | solution.py:266
  40.3 3.3 %collective-permute-done.2.refs_2_ = bf16[128,1024]{1,0:T(8,128)(2,1)S(1)} collective-permute-done((bf16[128,1024]{1,0:T(8,128)(2,1)S(1)}, bf16[128,1024]{1,0:T(8,128)(2,1)S(1)}, u32[]{:S(2)}, u32[]{:S(2)}) %collective-permute-start.2) | collective-permute-done | bytes 262176 | tf_op jit(solution)/shard_map/ppermute | solution.py:263
  43.6 0.5 collective-permute-start.10
  44.1 1.8 collective-permute-done.8.refs_13_
  45.9 3.3 %collective-permute-done.7.refs_6_ = bf16[128,1024]{1,0:T(8,128)(2,1)S(1)} collective-permute-done((bf16[128,1024]{1,0:T(8,128)(2,1)S(1)}, bf16[128,1024]{1,0:T(8,128)(2,1)S(1)}, u32[]{:S(2)}, u32[]{:S(2)}) %collective-permute-start.7) | collective-permute-done | bytes 262176 | tf_op jit(solution)/shard_map/ppermute | solution.py:263
  49.2 0.4 collective-permute-start.12
  49.6 2.7 %collective-permute-done.10.refs_10_ = bf16[128,1024]{1,0:T(8,128)(2,1)S(1)} collective-permute-done((bf16[128,1024]{1,0:T(8,128)(2,1)S(1)}, bf16[128,1024]{1,0:T(8,128)(2,1)S(1)}, u32[]{:S(2)}, u32[]{:S(2)}) %collective-permute-start.10) | collective-permute-done | bytes 262176 | tf_op jit(solution)/shard_map/ppermute | solution.py:266
  52.3 2.7 %collective-permute-done.4.refs_3_ = bf16[128,1024]{1,0:T(8,128)(2,1)S(1)} collective-permute-done((bf16[128,1024]{1,0:T(8,128)(2,1)S(1)}, bf16[128,1024]{1,0:T(8,128)(2,1)S(1)}, u32[]{:S(2)}, u32[]{:S(2)}) %collective-permute-start.4) | collective-permute-done | bytes 262176 | tf_op jit(solution)/shard_map/ppermute | solution.py:263
  55.0 0.5 collective-permute-done.12.refs_14_
  55.6 2.3 %collective-permute-done.9.refs_7_ = bf16[128,1024]{1,0:T(8,128)(2,1)S(1)} collective-permute-done((bf16[128,1024]{1,0:T(8,128)(2,1)S(1)}, bf16[128,1024]{1,0:T(8,128)(2,1)S(1)}, u32[]{:S(2)}, u32[]{:S(2)}) %collective-permute-start.9) | collective-permute-done | bytes 262176 | tf_op jit(solution)/shard_map/ppermute | solution.py:263
  57.9 0.1 collective-permute-start.17
  58.0 1.6 collective-permute-start.11
  59.7 7.0 %collective-permute-done.11.refs_11_ = bf16[128,1024]{1,0:T(8,128)(2,1)S(1)} collective-permute-done((bf16[128,1024]{1,0:T(8,128)(2,1)S(1)}, bf16[128,1024]{1,0:T(8,128)(2,1)S(1)}, u32[]{:S(2)}, u32[]{:S(2)}) %collective-permute-start.11) | collective-permute-done | bytes 262176 | tf_op jit(solution)/shard_map/ppermute | solution.py:266
  66.7 3.1 %collective-permute-done.13.refs_15_ = bf16[128,1024]{1,0:T(8,128)(2,1)S(1)} collective-permute-done((bf16[128,1024]{1,0:T(8,128)(2,1)S(1)}, bf16[128,1024]{1,0:T(8,128)(2,1)S(1)}, u32[]{:S(2)}, u32[]{:S(2)}) %collective-permute-start.13) | collective-permute-done | bytes 262176 | tf_op jit(solution)/shard_map/ppermute | solution.py:263
  69.8 0.1 collective-permute-start.18
  69.9 1.9 collective-permute-done.18.refs_20_
  71.8 146.5 %shard_map.57 = bf16[128,8192]{1,0:T(8,128)(2,1)} custom-call(s32[8]{0:T(128)S(1)} %concatenate.18.info, bf16[128,8192]{1,0:T(8,128)(2,1)} %query.1, bf16[128,1024]{1,0:T(8,128)(2,1)S(1)} %copy-done, bf16[128,1024]{1,0:T(8,128)(2,1)S(1)} %collective-permute-done.refs_1_, bf16[128,1024]{1,0:T(8,128)(2,1)S(1)} %collective-permute-done.2.refs_2_, ...), custom_call_target="tpu_custom_call" | custom-call | flops 9663676416 | bytes 12582912 | tf_op jit(solution)/shard_map/pallas_call | solution.py:190
  (23 shorter events, 0.4 us)
Async XLA Ops:
  9.1 21.8 %collective-permute-start.1 = (bf16[128,1024]{1,0:T(8,128)(2,1)}, bf16[128,1024]{1,0:T(8,128)(2,1)S(1)}, u32[]{:S(2)}, u32[]{:S(2)}) collective-permute-start(bf16[128,1024]{1,0:T(8,128)(2,1)} %shard_map.56.refs_0_), channel_id=1, source_target_pairs={{0,8},{4,12},{8,0},{12,4},{1,9},{5,13},{9,1},{13,5},{2,10},{6,14},... | collective-permute-start | bytes 786440 | tf_op jit(solution)/shard_map/ppermute | solution.py:266
  12.1 18.8 %collective-permute-start = (bf16[128,1024]{1,0:T(8,128)(2,1)}, bf16[128,1024]{1,0:T(8,128)(2,1)S(1)}, u32[]{:S(2)}, u32[]{:S(2)}) collective-permute-start(bf16[128,1024]{1,0:T(8,128)(2,1)} %shard_map.56.refs_0_), channel_id=1, source_target_pairs={{0,1},{1,2},{2,3},{3,0},{4,5},{5,6},{6,7},{7,4},{8,9},{9,10},{10,1... | collective-permute-start | bytes 786440 | tf_op jit(solution)/shard_map/ppermute | solution.py:263
  22.8 11.3 %collective-permute-start.6 = (bf16[128,1024]{1,0:T(8,128)(2,1)}, bf16[128,1024]{1,0:T(8,128)(2,1)S(1)}, u32[]{:S(2)}, u32[]{:S(2)}) collective-permute-start(bf16[128,1024]{1,0:T(8,128)(2,1)} %shard_map.55.refs_4_), channel_id=1, source_target_pairs={{0,8},{4,12},{8,0},{12,4},{1,9},{5,13},{9,1},{13,5},{2,10},{6,14},... | collective-permute-start | bytes 786440 | tf_op jit(solution)/shard_map/ppermute | solution.py:266
  23.4 10.7 %collective-permute-start.5 = (bf16[128,1024]{1,0:T(8,128)(2,1)}, bf16[128,1024]{1,0:T(8,128)(2,1)S(1)}, u32[]{:S(2)}, u32[]{:S(2)}) collective-permute-start(bf16[128,1024]{1,0:T(8,128)(2,1)} %shard_map.55.refs_4_), channel_id=1, source_target_pairs={{0,1},{1,2},{2,3},{3,0},{4,5},{5,6},{6,7},{7,4},{8,9},{9,10},{10,1... | collective-permute-start | bytes 786440 | tf_op jit(solution)/shard_map/ppermute | solution.py:263
  31.0 9.3 %collective-permute-start.3 = (bf16[128,1024]{1,0:T(8,128)(2,1)S(1)}, bf16[128,1024]{1,0:T(8,128)(2,1)S(1)}, u32[]{:S(2)}, u32[]{:S(2)}) collective-permute-start(bf16[128,1024]{1,0:T(8,128)(2,1)S(1)} %collective-permute-done.refs_1_), channel_id=1, source_target_pairs={{0,8},{4,12},{8,0},{12,4},{1,9},{5,13},{9,1},{13,5},{2,10},{6,14},... | collective-permute-start | bytes 786440 | tf_op jit(solution)/shard_map/ppermute | solution.py:266
  32.5 11.0 %collective-permute-start.2 = (bf16[128,1024]{1,0:T(8,128)(2,1)S(1)}, bf16[128,1024]{1,0:T(8,128)(2,1)S(1)}, u32[]{:S(2)}, u32[]{:S(2)}) collective-permute-start(bf16[128,1024]{1,0:T(8,128)(2,1)S(1)} %collective-permute-done.refs_1_), channel_id=1, source_target_pairs={{0,1},{1,2},{2,3},{3,0},{4,5},{5,6},{6,7},{7,4},{8,9},{9,10},{10,1... | collective-permute-start | bytes 786440 | tf_op jit(solution)/shard_map/ppermute | solution.py:263
  34.1 11.8 %collective-permute-start.8 = (bf16[128,1024]{1,0:T(8,128)(2,1)S(1)}, bf16[128,1024]{1,0:T(8,128)(2,1)S(1)}, u32[]{:S(2)}, u32[]{:S(2)}) collective-permute-start(bf16[128,1024]{1,0:T(8,128)(2,1)S(1)} %collective-permute-done.5.refs_5_), channel_id=1, source_target_pairs={{0,8},{4,12},{8,0},{12,4},{1,9},{5,13},{9,1},{13,5},{2,10},{6,14},... | collective-permute-start | bytes 786440 | tf_op jit(solution)/shard_map/ppermute | solution.py:266
  34.6 14.5 %collective-permute-start.7 = (bf16[128,1024]{1,0:T(8,128)(2,1)S(1)}, bf16[128,1024]{1,0:T(8,128)(2,1)S(1)}, u32[]{:S(2)}, u32[]{:S(2)}) collective-permute-start(bf16[128,1024]{1,0:T(8,128)(2,1)S(1)} %collective-permute-done.5.refs_5_), channel_id=1, source_target_pairs={{0,1},{1,2},{2,3},{3,0},{4,5},{5,6},{6,7},{7,4},{8,9},{9,10},{10,1... | collective-permute-start | bytes 786440 | tf_op jit(solution)/shard_map/ppermute | solution.py:263
  34.8 24.8 %copy-start = (bf16[128,1024]{1,0:T(8,128)(2,1)S(1)}, bf16[128,1024]{1,0:T(8,128)(2,1)}, u32[]{:S(2)}) copy-start(bf16[128,1024]{1,0:T(8,128)(2,1)} %shard_map.56.refs_0_) | copy-start | bytes 786436
  34.8 24.8 %copy-start.1 = (bf16[128,1024]{1,0:T(8,128)(2,1)S(1)}, bf16[128,1024]{1,0:T(8,128)(2,1)}, u32[]{:S(2)}) copy-start(bf16[128,1024]{1,0:T(8,128)(2,1)} %shard_map.55.refs_4_) | copy-start | bytes 786436
  34.8 35.1 %collective-permute-start.15 = (bf16[128,4096]{1,0:T(8,128)(2,1)S(1)}, bf16[128,4096]{1,0:T(8,128)(2,1)S(1)}, u32[]{:S(2)}, u32[]{:S(2)}) collective-permute-start(bf16[128,4096]{1,0:T(8,128)(2,1)S(1)} %pad_maximum_fusion), channel_id=1, source_target_pairs={{0,4},{4,0},{8,12},{12,8},{1,5},{5,1},{9,13},{13,9},{2,6},{6,2},{1... | collective-permute-start | bytes 3145736 | tf_op jit(solution)/shard_map/ppermute | solution.py:269
  43.6 8.7 %collective-permute-start.10 = (bf16[128,1024]{1,0:T(8,128)(2,1)S(1)}, bf16[128,1024]{1,0:T(8,128)(2,1)S(1)}, u32[]{:S(2)}, u32[]{:S(2)}) collective-permute-start(bf16[128,1024]{1,0:T(8,128)(2,1)S(1)} %collective-permute-done.2.refs_2_), channel_id=1, source_target_pairs={{0,8},{4,12},{8,0},{12,4},{1,9},{5,13},{9,1},{13,5},{2,10},{6,14},... | collective-permute-start | bytes 786440 | tf_op jit(solution)/shard_map/ppermute | solution.py:266
  44.1 10.9 %collective-permute-start.4 = (bf16[128,1024]{1,0:T(8,128)(2,1)S(1)}, bf16[128,1024]{1,0:T(8,128)(2,1)S(1)}, u32[]{:S(2)}, u32[]{:S(2)}) collective-permute-start(bf16[128,1024]{1,0:T(8,128)(2,1)S(1)} %collective-permute-done.2.refs_2_), channel_id=1, source_target_pairs={{0,1},{1,2},{2,3},{3,0},{4,5},{5,6},{6,7},{7,4},{8,9},{9,10},{10,1... | collective-permute-start | bytes 786440 | tf_op jit(solution)/shard_map/ppermute | solution.py:263
  49.2 6.4 %collective-permute-start.12 = (bf16[128,1024]{1,0:T(8,128)(2,1)S(1)}, bf16[128,1024]{1,0:T(8,128)(2,1)S(1)}, u32[]{:S(2)}, u32[]{:S(2)}) collective-permute-start(bf16[128,1024]{1,0:T(8,128)(2,1)S(1)} %collective-permute-done.7.refs_6_), channel_id=1, source_target_pairs={{0,8},{4,12},{8,0},{12,4},{1,9},{5,13},{9,1},{13,5},{2,10},{6,14},... | collective-permute-start | bytes 786440 | tf_op jit(solution)/shard_map/ppermute | solution.py:266
  49.6 8.3 %collective-permute-start.9 = (bf16[128,1024]{1,0:T(8,128)(2,1)S(1)}, bf16[128,1024]{1,0:T(8,128)(2,1)S(1)}, u32[]{:S(2)}, u32[]{:S(2)}) collective-permute-start(bf16[128,1024]{1,0:T(8,128)(2,1)S(1)} %collective-permute-done.7.refs_6_), channel_id=1, source_target_pairs={{0,1},{1,2},{2,3},{3,0},{4,5},{5,6},{6,7},{7,4},{8,9},{9,10},{10,1... | collective-permute-start | bytes 786440 | tf_op jit(solution)/shard_map/ppermute | solution.py:263
  52.3 19.5 %collective-permute-start.16 = (bf16[128,4096]{1,0:T(8,128)(2,1)S(1)}, bf16[128,4096]{1,0:T(8,128)(2,1)S(1)}, u32[]{:S(2)}, u32[]{:S(2)}) collective-permute-start(bf16[128,4096]{1,0:T(8,128)(2,1)S(1)} %pad_maximum_fusion.1), channel_id=1, source_target_pairs={{0,4},{4,0},{8,12},{12,8},{1,5},{5,1},{9,13},{13,9},{2,6},{6,2},{1... | collective-permute-start | bytes 3145736 | tf_op jit(solution)/shard_map/ppermute | solution.py:269
  57.9 13.9 %collective-permute-start.17 = (bf16[128,4096]{1,0:T(8,128)(2,1)S(1)}, bf16[128,4096]{1,0:T(8,128)(2,1)S(1)}, u32[]{:S(2)}, u32[]{:S(2)}) collective-permute-start(bf16[128,4096]{1,0:T(8,128)(2,1)S(1)} %pad_maximum_fusion.2), channel_id=1, source_target_pairs={{0,4},{4,0},{8,12},{12,8},{1,5},{5,1},{9,13},{13,9},{2,6},{6,2},{1... | collective-permute-start | bytes 3145736 | tf_op jit(solution)/shard_map/ppermute | solution.py:269
  58.0 8.7 %collective-permute-start.11 = (bf16[128,1024]{1,0:T(8,128)(2,1)S(1)}, bf16[128,1024]{1,0:T(8,128)(2,1)S(1)}, u32[]{:S(2)}, u32[]{:S(2)}) collective-permute-start(bf16[128,1024]{1,0:T(8,128)(2,1)S(1)} %collective-permute-done.4.refs_3_), channel_id=1, source_target_pairs={{0,8},{4,12},{8,0},{12,4},{1,9},{5,13},{9,1},{13,5},{2,10},{6,14},... | collective-permute-start | bytes 786440 | tf_op jit(solution)/shard_map/ppermute | solution.py:266
  59.6 10.2 %collective-permute-start.13 = (bf16[128,1024]{1,0:T(8,128)(2,1)S(1)}, bf16[128,1024]{1,0:T(8,128)(2,1)S(1)}, u32[]{:S(2)}, u32[]{:S(2)}) collective-permute-start(bf16[128,1024]{1,0:T(8,128)(2,1)S(1)} %collective-permute-done.12.refs_14_), channel_id=1, source_target_pairs={{0,1},{1,2},{2,3},{3,0},{4,5},{5,6},{6,7},{7,4},{8,9},{9,10},{10,1... | collective-permute-start | bytes 786440 | tf_op jit(solution)/shard_map/ppermute | solution.py:263
  66.7 3.2 %collective-permute-start.14 = (bf16[128,2048]{1,0:T(8,128)(2,1)S(1)}, bf16[128,2048]{1,0:T(8,128)(2,1)S(1)}, u32[]{:S(2)}, u32[]{:S(2)}) collective-permute-start(bf16[128,2048]{1,0:T(8,128)(2,1)S(1)} %pad_maximum_fusion.3), channel_id=1, source_target_pairs={{0,4},{4,0},{8,12},{12,8},{1,5},{5,1},{9,13},{13,9},{2,6},{6,2},{1... | collective-permute-start | bytes 1572872 | tf_op jit(solution)/shard_map/ppermute | solution.py:269
  69.8 2.0 collective-permute-start.18

commit v6 on v5

--- a/solution.py
+++ b/solution.py
@@ -203,7 +203,7 @@
         ),
         out_shape=jax.ShapeDtypeStruct(query_rows.shape, query_rows.dtype),
         cost_estimate=pl.CostEstimate(flops=6 * work * HD, bytes_accessed=12 << 20, transcendentals=work),
-        compiler_params=pltpu.CompilerParams(vmem_limit_bytes=40 << 20),
+        compiler_params=pltpu.CompilerParams(vmem_limit_bytes=2 * keys * kv_heads * 2 * HD * 2),
     )(info, pltpu.with_memory_space_constraint(query_rows, pltpu.HBM), *arrays)
 
 
@@ -230,6 +230,7 @@
         scratch_shapes=[pltpu.SemaphoreType.DMA((count,))],
         out_shape=jax.ShapeDtypeStruct((key_rows.shape[0], count * HD), key_rows.dtype),
         cost_estimate=pl.CostEstimate(flops=0, bytes_accessed=1 << 19, transcendentals=0),
+        compiler_params=pltpu.CompilerParams(vmem_limit_bytes=1 << 18),
     )(key_rows, value_rows)
 
 

time: 219 us -> 204 us (0.932)
  the two profiles are of different devices: /device:TPU:0 before, /device:TPU:1 now
where the time goes in v6:
time: 204 us
  Pallas kernels  147 us (72%)
  starting transfers between devices  23.7 us (12%)
  waiting for transfers between devices  23.3 us (11%)
  other arithmetic  4.27 us (2%)
  local copies, waits for them, and re-layouts  3.88 us (2%)
    pallas_call x1, Pallas kernels, attend(): pl.pallas_call(functools.partial(attend_kernel, sizes, where, groups), gr...  147 us
    ppermute x5, starting transfers between devices, other_core(): return lax.ppermute(x, 'blk', [(i, i ^ 1) for i in range(blocks)])  13.2 us
    ppermute x7, waiting for transfers between devices, next_chip(): lax.ppermute(x, 'blk', [(i, (i + CORES) % blocks) for i in range(blocks)])  11.1 us
    ppermute x7, waiting for transfers between devices, next_hop(): return lax.ppermute(x, 'head', [(i, (i + 1) % ring) for i in range(ring)])  10.6 us
    ppermute x7, starting transfers between devices, next_chip(): lax.ppermute(x, 'blk', [(i, (i + CORES) % blocks) for i in range(blocks)])  6.56 us
  transfers between devices with their start and end apart: 19, of which 10 were waited for; matrix products, arithmetic and copies ran while one was open for 2% of the time, Pallas kernels for 0%

profile of v6, /device:TPU:1, one launch (start us, length us, event | category | flops | bytes accessed | tf_op | source)
XLA Modules:
  0.0 203.9 jit_solution(10483183461549805613)
XLA Ops:
  0.0 0.9 copy-done
  1.0 0.9 copy-done.2
  2.1 2.1 %collective-permute-start.1 = (bf16[128,1024]{1,0:T(8,128)(2,1)S(1)}, bf16[128,1024]{1,0:T(8,128)(2,1)S(1)}, u32[]{:S(2)}, u32[]{:S(2)}) collective-permute-start(bf16[128,1024]{1,0:T(8,128)(2,1)S(1)} %shard_map.56.refs_0_), channel_id=1, source_target_pairs={{0,8},{4,12},{8,0},{12,4},{1,9},{5,13},{9,1},{13,5},{2,10},{6,14},... | collective-permute-start | bytes 786440 | tf_op jit(solution)/shard_map/ppermute | solution.py:267
  4.2 1.3 collective-permute-start
  5.5 0.9 copy-done.1
  6.4 0.9 copy-done.3
  7.5 0.3 collective-permute-start.6
  7.9 1.3 collective-permute-start.5
  9.2 0.8 fusion
  9.9 1.3 fusion.2
  11.9 1.3 fusion.3
  14.3 0.7 compare_select_fusion.4
  15.1 1.3 collective-permute-start.3
  16.4 1.3 collective-permute-start.2
  17.7 0.9 collective-permute-done.5.refs_5_
  18.6 0.7 collective-permute-start.8
  19.3 1.7 collective-permute-start.15
  21.2 2.7 %collective-permute-done.2.refs_2_ = bf16[128,1024]{1,0:T(8,128)(2,1)S(1)} collective-permute-done((bf16[128,1024]{1,0:T(8,128)(2,1)S(1)}, bf16[128,1024]{1,0:T(8,128)(2,1)S(1)}, u32[]{:S(2)}, u32[]{:S(2)}) %collective-permute-start.2) | collective-permute-done | bytes 262176 | tf_op jit(solution)/shard_map/ppermute | solution.py:264
  24.2 2.8 %collective-permute-done.8.refs_13_ = bf16[128,1024]{1,0:T(8,128)(2,1)S(1)} collective-permute-done((bf16[128,1024]{1,0:T(8,128)(2,1)S(1)}, bf16[128,1024]{1,0:T(8,128)(2,1)S(1)}, u32[]{:S(2)}, u32[]{:S(2)}) %collective-permute-start.8) | collective-permute-done | bytes 262176 | tf_op jit(solution)/shard_map/ppermute | solution.py:267
  26.9 2.6 %collective-permute-done.7.refs_6_ = bf16[128,1024]{1,0:T(8,128)(2,1)S(1)} collective-permute-done((bf16[128,1024]{1,0:T(8,128)(2,1)S(1)}, bf16[128,1024]{1,0:T(8,128)(2,1)S(1)}, u32[]{:S(2)}, u32[]{:S(2)}) %collective-permute-start.7) | collective-permute-done | bytes 262176 | tf_op jit(solution)/shard_map/ppermute | solution.py:264
  29.5 0.6 collective-permute-start.12
  30.2 1.7 collective-permute-done.10.refs_10_
  31.9 6.3 %collective-permute-start.16 = (bf16[128,4096]{1,0:T(8,128)(2,1)S(1)}, bf16[128,4096]{1,0:T(8,128)(2,1)S(1)}, u32[]{:S(2)}, u32[]{:S(2)}) collective-permute-start(bf16[128,4096]{1,0:T(8,128)(2,1)S(1)} %pad_maximum_fusion.1), channel_id=1, source_target_pairs={{0,4},{4,0},{8,12},{12,8},{1,5},{5,1},{9,13},{13,9},{2,6},{6,2},{1... | collective-permute-start | bytes 3145736 | tf_op jit(solution)/shard_map/ppermute | solution.py:270
  38.2 2.5 %collective-permute-done.9.refs_7_ = bf16[128,1024]{1,0:T(8,128)(2,1)S(1)} collective-permute-done((bf16[128,1024]{1,0:T(8,128)(2,1)S(1)}, bf16[128,1024]{1,0:T(8,128)(2,1)S(1)}, u32[]{:S(2)}, u32[]{:S(2)}) %collective-permute-start.9) | collective-permute-done | bytes 262176 | tf_op jit(solution)/shard_map/ppermute | solution.py:264
  40.8 3.1 %collective-permute-start.17 = (bf16[128,4096]{1,0:T(8,128)(2,1)S(1)}, bf16[128,4096]{1,0:T(8,128)(2,1)S(1)}, u32[]{:S(2)}, u32[]{:S(2)}) collective-permute-start(bf16[128,4096]{1,0:T(8,128)(2,1)S(1)} %pad_maximum_fusion.2), channel_id=1, source_target_pairs={{0,4},{4,0},{8,12},{12,8},{1,5},{5,1},{9,13},{13,9},{2,6},{6,2},{1... | collective-permute-start | bytes 3145736 | tf_op jit(solution)/shard_map/ppermute | solution.py:270
  43.9 1.3 collective-permute-start.11
  45.2 6.5 %collective-permute-done.11.refs_11_ = bf16[128,1024]{1,0:T(8,128)(2,1)S(1)} collective-permute-done((bf16[128,1024]{1,0:T(8,128)(2,1)S(1)}, bf16[128,1024]{1,0:T(8,128)(2,1)S(1)}, u32[]{:S(2)}, u32[]{:S(2)}) %collective-permute-start.11) | collective-permute-done | bytes 262176 | tf_op jit(solution)/shard_map/ppermute | solution.py:267
  51.8 0.8 collective-permute-start.14
  52.6 1.9 collective-permute-done.13.refs_15_
  54.6 1.2 collective-permute-start.18
  55.8 1.5 collective-permute-done.18.refs_20_
  57.4 146.5 %shard_map.57 = bf16[128,8192]{1,0:T(8,128)(2,1)} custom-call(s32[8]{0:T(128)S(1)} %concatenate.18.info, bf16[128,8192]{1,0:T(8,128)(2,1)} %query.1, bf16[128,1024]{1,0:T(8,128)(2,1)S(1)} %shard_map.56.refs_0_, bf16[128,1024]{1,0:T(8,128)(2,1)S(1)} %collective-permute-done.refs_1_, bf16[128,1024]{1,0:T(8,128)(2,1)S(1)} %collective-permute-done.2.refs_2_, ...), custom_call_target="tpu_custom_call" | custom-call | flops 9663676416 | bytes 12582912 | tf_op jit(solution)/shard_map/pallas_call | solution.py:190
  (27 shorter events, 1.1 us)
Async XLA Ops:
  0.0 0.9 copy-start
  1.0 0.9 copy-start.2
  2.1 13.0 %collective-permute-start.1 = (bf16[128,1024]{1,0:T(8,128)(2,1)S(1)}, bf16[128,1024]{1,0:T(8,128)(2,1)S(1)}, u32[]{:S(2)}, u32[]{:S(2)}) collective-permute-start(bf16[128,1024]{1,0:T(8,128)(2,1)S(1)} %shard_map.56.refs_0_), channel_id=1, source_target_pairs={{0,8},{4,12},{8,0},{12,4},{1,9},{5,13},{9,1},{13,5},{2,10},{6,14},... | collective-permute-start | bytes 786440 | tf_op jit(solution)/shard_map/ppermute | solution.py:267
  4.2 10.9 %collective-permute-start = (bf16[128,1024]{1,0:T(8,128)(2,1)S(1)}, bf16[128,1024]{1,0:T(8,128)(2,1)S(1)}, u32[]{:S(2)}, u32[]{:S(2)}) collective-permute-start(bf16[128,1024]{1,0:T(8,128)(2,1)S(1)} %shard_map.56.refs_0_), channel_id=1, source_target_pairs={{0,1},{1,2},{2,3},{3,0},{4,5},{5,6},{6,7},{7,4},{8,9},{9,10},{10,1... | collective-permute-start | bytes 786440 | tf_op jit(solution)/shard_map/ppermute | solution.py:264
  5.5 0.9 copy-start.1
  6.4 0.9 copy-start.3
  7.5 10.1 %collective-permute-start.6 = (bf16[128,1024]{1,0:T(8,128)(2,1)S(1)}, bf16[128,1024]{1,0:T(8,128)(2,1)S(1)}, u32[]{:S(2)}, u32[]{:S(2)}) collective-permute-start(bf16[128,1024]{1,0:T(8,128)(2,1)S(1)} %shard_map.55.refs_4_), channel_id=1, source_target_pairs={{0,8},{4,12},{8,0},{12,4},{1,9},{5,13},{9,1},{13,5},{2,10},{6,14},... | collective-permute-start | bytes 786440 | tf_op jit(solution)/shard_map/ppermute | solution.py:267
  7.9 10.7 %collective-permute-start.5 = (bf16[128,1024]{1,0:T(8,128)(2,1)S(1)}, bf16[128,1024]{1,0:T(8,128)(2,1)S(1)}, u32[]{:S(2)}, u32[]{:S(2)}) collective-permute-start(bf16[128,1024]{1,0:T(8,128)(2,1)S(1)} %shard_map.55.refs_4_), channel_id=1, source_target_pairs={{0,1},{1,2},{2,3},{3,0},{4,5},{5,6},{6,7},{7,4},{8,9},{9,10},{10,1... | collective-permute-start | bytes 786440 | tf_op jit(solution)/shard_map/ppermute | solution.py:264
  15.1 6.1 %collective-permute-start.3 = (bf16[128,1024]{1,0:T(8,128)(2,1)S(1)}, bf16[128,1024]{1,0:T(8,128)(2,1)S(1)}, u32[]{:S(2)}, u32[]{:S(2)}) collective-permute-start(bf16[128,1024]{1,0:T(8,128)(2,1)S(1)} %collective-permute-done.refs_1_), channel_id=1, source_target_pairs={{0,8},{4,12},{8,0},{12,4},{1,9},{5,13},{9,1},{13,5},{2,10},{6,14},... | collective-permute-start | bytes 786440 | tf_op jit(solution)/shard_map/ppermute | solution.py:267
  16.4 7.5 %collective-permute-start.2 = (bf16[128,1024]{1,0:T(8,128)(2,1)S(1)}, bf16[128,1024]{1,0:T(8,128)(2,1)S(1)}, u32[]{:S(2)}, u32[]{:S(2)}) collective-permute-start(bf16[128,1024]{1,0:T(8,128)(2,1)S(1)} %collective-permute-done.refs_1_), channel_id=1, source_target_pairs={{0,1},{1,2},{2,3},{3,0},{4,5},{5,6},{6,7},{7,4},{8,9},{9,10},{10,1... | collective-permute-start | bytes 786440 | tf_op jit(solution)/shard_map/ppermute | solution.py:264
  18.6 8.3 %collective-permute-start.8 = (bf16[128,1024]{1,0:T(8,128)(2,1)S(1)}, bf16[128,1024]{1,0:T(8,128)(2,1)S(1)}, u32[]{:S(2)}, u32[]{:S(2)}) collective-permute-start(bf16[128,1024]{1,0:T(8,128)(2,1)S(1)} %collective-permute-done.5.refs_5_), channel_id=1, source_target_pairs={{0,8},{4,12},{8,0},{12,4},{1,9},{5,13},{9,1},{13,5},{2,10},{6,14},... | collective-permute-start | bytes 786440 | tf_op jit(solution)/shard_map/ppermute | solution.py:267
  19.3 10.3 %collective-permute-start.7 = (bf16[128,1024]{1,0:T(8,128)(2,1)S(1)}, bf16[128,1024]{1,0:T(8,128)(2,1)S(1)}, u32[]{:S(2)}, u32[]{:S(2)}) collective-permute-start(bf16[128,1024]{1,0:T(8,128)(2,1)S(1)} %collective-permute-done.5.refs_5_), channel_id=1, source_target_pairs={{0,1},{1,2},{2,3},{3,0},{4,5},{5,6},{6,7},{7,4},{8,9},{9,10},{10,1... | collective-permute-start | bytes 786440 | tf_op jit(solution)/shard_map/ppermute | solution.py:264
  19.3 36.5 %collective-permute-start.15 = (bf16[128,4096]{1,0:T(8,128)(2,1)S(1)}, bf16[128,4096]{1,0:T(8,128)(2,1)S(1)}, u32[]{:S(2)}, u32[]{:S(2)}) collective-permute-start(bf16[128,4096]{1,0:T(8,128)(2,1)S(1)} %pad_maximum_fusion), channel_id=1, source_target_pairs={{0,4},{4,0},{8,12},{12,8},{1,5},{5,1},{9,13},{13,9},{2,6},{6,2},{1... | collective-permute-start | bytes 3145736 | tf_op jit(solution)/shard_map/ppermute | solution.py:270
  23.9 8.0 %collective-permute-start.10 = (bf16[128,1024]{1,0:T(8,128)(2,1)S(1)}, bf16[128,1024]{1,0:T(8,128)(2,1)S(1)}, u32[]{:S(2)}, u32[]{:S(2)}) collective-permute-start(bf16[128,1024]{1,0:T(8,128)(2,1)S(1)} %collective-permute-done.2.refs_2_), channel_id=1, source_target_pairs={{0,8},{4,12},{8,0},{12,4},{1,9},{5,13},{9,1},{13,5},{2,10},{6,14},... | collective-permute-start | bytes 786440 | tf_op jit(solution)/shard_map/ppermute | solution.py:267
  24.1 14.1 %collective-permute-start.4 = (bf16[128,1024]{1,0:T(8,128)(2,1)S(1)}, bf16[128,1024]{1,0:T(8,128)(2,1)S(1)}, u32[]{:S(2)}, u32[]{:S(2)}) collective-permute-start(bf16[128,1024]{1,0:T(8,128)(2,1)S(1)} %collective-permute-done.2.refs_2_), channel_id=1, source_target_pairs={{0,1},{1,2},{2,3},{3,0},{4,5},{5,6},{6,7},{7,4},{8,9},{9,10},{10,1... | collective-permute-start | bytes 786440 | tf_op jit(solution)/shard_map/ppermute | solution.py:264
  29.5 8.7 %collective-permute-start.12 = (bf16[128,1024]{1,0:T(8,128)(2,1)S(1)}, bf16[128,1024]{1,0:T(8,128)(2,1)S(1)}, u32[]{:S(2)}, u32[]{:S(2)}) collective-permute-start(bf16[128,1024]{1,0:T(8,128)(2,1)S(1)} %collective-permute-done.7.refs_6_), channel_id=1, source_target_pairs={{0,8},{4,12},{8,0},{12,4},{1,9},{5,13},{9,1},{13,5},{2,10},{6,14},... | collective-permute-start | bytes 786440 | tf_op jit(solution)/shard_map/ppermute | solution.py:267
  30.1 10.6 %collective-permute-start.9 = (bf16[128,1024]{1,0:T(8,128)(2,1)S(1)}, bf16[128,1024]{1,0:T(8,128)(2,1)S(1)}, u32[]{:S(2)}, u32[]{:S(2)}) collective-permute-start(bf16[128,1024]{1,0:T(8,128)(2,1)S(1)} %collective-permute-done.7.refs_6_), channel_id=1, source_target_pairs={{0,1},{1,2},{2,3},{3,0},{4,5},{5,6},{6,7},{7,4},{8,9},{9,10},{10,1... | collective-permute-start | bytes 786440 | tf_op jit(solution)/shard_map/ppermute | solution.py:264
  31.9 25.4 %collective-permute-start.16 = (bf16[128,4096]{1,0:T(8,128)(2,1)S(1)}, bf16[128,4096]{1,0:T(8,128)(2,1)S(1)}, u32[]{:S(2)}, u32[]{:S(2)}) collective-permute-start(bf16[128,4096]{1,0:T(8,128)(2,1)S(1)} %pad_maximum_fusion.1), channel_id=1, source_target_pairs={{0,4},{4,0},{8,12},{12,8},{1,5},{5,1},{9,13},{13,9},{2,6},{6,2},{1... | collective-permute-start | bytes 3145736 | tf_op jit(solution)/shard_map/ppermute | solution.py:270
  40.8 16.5 %collective-permute-start.17 = (bf16[128,4096]{1,0:T(8,128)(2,1)S(1)}, bf16[128,4096]{1,0:T(8,128)(2,1)S(1)}, u32[]{:S(2)}, u32[]{:S(2)}) collective-permute-start(bf16[128,4096]{1,0:T(8,128)(2,1)S(1)} %pad_maximum_fusion.2), channel_id=1, source_target_pairs={{0,4},{4,0},{8,12},{12,8},{1,5},{5,1},{9,13},{13,9},{2,6},{6,2},{1... | collective-permute-start | bytes 3145736 | tf_op jit(solution)/shard_map/ppermute | solution.py:270
  43.9 7.9 %collective-permute-start.11 = (bf16[128,1024]{1,0:T(8,128)(2,1)S(1)}, bf16[128,1024]{1,0:T(8,128)(2,1)S(1)}, u32[]{:S(2)}, u32[]{:S(2)}) collective-permute-start(bf16[128,1024]{1,0:T(8,128)(2,1)S(1)} %collective-permute-done.4.refs_3_), channel_id=1, source_target_pairs={{0,8},{4,12},{8,0},{12,4},{1,9},{5,13},{9,1},{13,5},{2,10},{6,14},... | collective-permute-start | bytes 786440 | tf_op jit(solution)/shard_map/ppermute | solution.py:267
  45.2 9.3 %collective-permute-start.13 = (bf16[128,1024]{1,0:T(8,128)(2,1)S(1)}, bf16[128,1024]{1,0:T(8,128)(2,1)S(1)}, u32[]{:S(2)}, u32[]{:S(2)}) collective-permute-start(bf16[128,1024]{1,0:T(8,128)(2,1)S(1)} %collective-permute-done.12.refs_14_), channel_id=1, source_target_pairs={{0,1},{1,2},{2,3},{3,0},{4,5},{5,6},{6,7},{7,4},{8,9},{9,10},{10,1... | collective-permute-start | bytes 786440 | tf_op jit(solution)/shard_map/ppermute | solution.py:264
  51.8 4.0 %collective-permute-start.14 = (bf16[128,2048]{1,0:T(8,128)(2,1)S(1)}, bf16[128,2048]{1,0:T(8,128)(2,1)S(1)}, u32[]{:S(2)}, u32[]{:S(2)}) collective-permute-start(bf16[128,2048]{1,0:T(8,128)(2,1)S(1)} %pad_maximum_fusion.3), channel_id=1, source_target_pairs={{0,4},{4,0},{8,12},{12,8},{1,5},{5,1},{9,13},{13,9},{2,6},{6,2},{1... | collective-permute-start | bytes 1572872 | tf_op jit(solution)/shard_map/ppermute | solution.py:270
  54.6 2.8 %collective-permute-start.18 = (bf16[128,2048]{1,0:T(8,128)(2,1)S(1)}, bf16[128,2048]{1,0:T(8,128)(2,1)S(1)}, u32[]{:S(2)}, u32[]{:S(2)}) collective-permute-start(bf16[128,2048]{1,0:T(8,128)(2,1)S(1)} %pad_maximum_fusion.4), channel_id=1, source_target_pairs={{0,4},{4,0},{8,12},{12,8},{1,5},{5,1},{9,13},{13,9},{2,6},{6,2},{1... | collective-permute-start | bytes 1572872 | tf_op jit(solution)/shard_map/ppermute | solution.py:270

commit v7 on v6

v7 whole, which is shorter than its diff:
```python
import functools
import math

import jax
import jax.numpy as jnp
from jax import lax
from jax.experimental import pallas as pl
from jax.experimental.pallas import tpu as pltpu
from jax.sharding import PartitionSpec as P

HD = 128
CORES = 2
HEADS_PER_TILE = 2
EXP2_SCALE = math.log2(math.e) / math.sqrt(HD)
LEAST_TOTAL, MOST_TOTAL = 1e-20, 1e30


def matmul_nt(a, b):
    return lax.dot_general(a, b, (((1,), (1,)), ((), ())), preferred_element_type=jnp.float32)


class Place:
    def __init__(self, sizes, placement, lengths):
        self.prompt_count, self.chips, self.ring, self.tokens = sizes
        self.blocks, self.slots = self.chips * CORES, self.prompt_count + 1
        self.index, self.head = lax.axis_index("blk"), lax.axis_index("head")
        self.placement, self.lengths = placement, lengths
        self.block = placement[self.index]

    def source(self, slot):
        found = self.index
        for b in range(self.blocks):
            found = jnp.where(self.placement[b] == slot, b, found)
        found = jnp.where(slot == self.prompt_count, self.index, found)
        back = lax.shift_right_logical(self.index, 1) - lax.shift_right_logical(found, 1)
        return jnp.where(back < 0, back + self.chips, back) * CORES + ((self.index ^ found) & 1)

    def first_key(self, slot):
        own = (self.ring - 1 - self.head) * self.tokens
        return jnp.where(slot == self.prompt_count, own, jnp.where(self.block > slot, 0, self.ring * self.tokens))

    def kept(self):
        keep = jnp.int32(self.ring * self.tokens)
        for response in range(self.prompt_count):
            keep = jnp.where(self.block == self.prompt_count + response, self.lengths[response], keep)
        offsets = self.head * self.tokens + lax.broadcasted_iota(jnp.int32, (self.tokens, 1), 0)
        return offsets < keep


def exact(here, query, key, value, out, group):
    slots, tokens, rows = here.prompt_count + 1, here.tokens, here.ring * here.tokens
    key_row = lax.broadcasted_iota(jnp.int32, (tokens, rows), 1)
    newest_own = rows - tokens + lax.broadcasted_iota(jnp.int32, (tokens, rows), 0)

    def one_head(head, carry):
        columns = pl.ds(pl.multiple_of(head * HD, HD), HD)
        query_one = query[:, columns]

        def part(ref, slot):
            return ref[pl.ds(pl.multiple_of(slot * rows, rows), rows), :]

        def score(slot):
            newest = jnp.where(slot == here.prompt_count, newest_own, rows)
            seen = (key_row >= here.first_key(slot)) & (key_row <= newest)
            return jnp.where(seen, matmul_nt(query_one, part(key, slot)), -jnp.inf)

        row_max = lax.fori_loop(
            0,
            slots,
            lambda j, best: jnp.maximum(best, jnp.max(score(j), axis=1, keepdims=True)),
            jnp.full((tokens, 1), -jnp.inf, jnp.float32),
        )

        def add(slot, carry):
            total, summed = carry
            weights = jnp.exp2((score(slot) - row_max) * EXP2_SCALE)
            total += jnp.sum(weights, axis=1, keepdims=True)
            weights = weights.astype(jnp.bfloat16)
            return total, summed + jnp.dot(weights, part(value, slot), preferred_element_type=jnp.float32)

        zeros = jnp.zeros((tokens, 1), jnp.float32), jnp.zeros((tokens, HD), jnp.float32)
        total, summed = lax.fori_loop(0, slots, add, zeros)
        out[:, columns] = jnp.where(here.kept(), summed / total, 0.0).astype(out.dtype)
        return carry

    lax.fori_loop(0, group, one_head, 0)


def attend_kernel(sizes, where, groups, placement, lengths, query, *refs):
    prompt_count, chips, ring, tokens = sizes
    here = Place(sizes, placement, lengths)
    arrays, (out, held_key, held_value, ones, bias, sems) = refs[:-6], refs[-6:]
    kv_head = pl.program_id(0)
    group = query.shape[1] // HD
    masked = bias.shape[1]

    def at(slot, hop):
        return pl.ds(pl.multiple_of((slot * ring + ring - 1 - hop) * tokens, tokens), tokens)

    def seen(slot, hop):
        return (ring - 1 - hop) * tokens >= here.first_key(slot)

    def fetch_of(index, kind, source, slot, hop):
        low, high = groups[index]
        array, column = where[kind, source, hop]
        return pltpu.make_async_copy(
            arrays[array].at[:, column + low * HD : column + high * HD],
            (held_key, held_value)[kind].at[at(slot, hop), low * HD : high * HD],
            sems.at[index, kind, slot, hop],
        )

    @pl.when(kv_head == 0)
    def _():
        for index in range(len(groups)):

            def fetch(slot, carry):
                wanted = here.source(slot)
                for source in range(here.blocks):

                    @pl.when(wanted == source)
                    def _():
                        for hop in range(ring):

                            @pl.when(seen(slot, hop))
                            def _():
                                for kind in range(2):
                                    fetch_of(index, kind, source, slot, hop).start()

                return carry

            lax.fori_loop(0, here.slots, fetch, 0)

        def fill(slot, carry):
            for hop in range(ring):
                count = jnp.where(seen(slot, hop), 1.0, 0.0)
                ones[at(slot, hop)] = jnp.full((tokens, HD), count, jnp.float32).astype(ones.dtype)

                @pl.when(jnp.logical_not(seen(slot, hop)))
                def _():
                    for held in (held_key, held_value):
                        held[at(slot, hop)] = jnp.zeros((tokens, held.shape[1]), held.dtype)

            return carry

        lax.fori_loop(0, here.slots, fill, 0)
        own = lax.broadcasted_iota(jnp.int32, (tokens, masked), 0)
        key = lax.broadcasted_iota(jnp.int32, (tokens, masked), 1) - (masked - tokens)
        bias[...] = jnp.where(key <= own, 0.0, -jnp.inf)

    for index, (first, _) in enumerate(groups):

        @pl.when(kv_head == first)
        def _():
            def finish(slot, carry):
                for hop in range(ring):

                    @pl.when(seen(slot, hop))
                    def _():
                        for kind in range(2):
                            fetch_of(index, kind, 0, slot, hop).wait()

                return carry

            lax.fori_loop(0, here.slots, finish, 0)

    column = pl.ds(pl.multiple_of(kv_head * HD, HD), HD)
    key, value = held_key.at[:, column], held_value.at[:, column]
    kept = here.kept()
    span = HEADS_PER_TILE * HD

    def one_tile(tile, carry):
        least, most = carry
        columns = pl.ds(pl.multiple_of(tile * span, span), span)
        query_tile = query[:, columns]
        query_tile = jnp.concatenate([query_tile[:, h * HD : (h + 1) * HD] for h in range(HEADS_PER_TILE)], axis=0)
        scores = matmul_nt(query_tile, key[...]) * EXP2_SCALE
        split = scores.shape[1] - masked
        tail = scores[:, split:].reshape(HEADS_PER_TILE, tokens, masked) + bias[...][None]
        tail = tail.reshape(HEADS_PER_TILE * tokens, masked)
        scores = tail if split == 0 else jnp.concatenate([scores[:, :split], tail], axis=1)
        weights = jnp.exp2(scores).astype(jnp.bfloat16)
        values = jnp.concatenate([value[...], ones[...]], axis=1)
        summed = jnp.dot(weights, values, preferred_element_type=jnp.float32)
        results = []
        for i in range(HEADS_PER_TILE):
            part = summed[i * tokens : (i + 1) * tokens]
            total = part[:, HD:]
            least, most = jnp.minimum(least, total), jnp.maximum(most, total)
            results.append(jnp.where(kept, part[:, :HD] / total, 0.0).astype(out.dtype))
        out[:, columns] = jnp.concatenate(results, axis=1)
        return least, most

    zeros = jnp.zeros((tokens, HD), jnp.float32)
    least, most = lax.fori_loop(0, group // HEADS_PER_TILE, one_tile, (zeros + jnp.inf, zeros))
    safe = (jnp.min(least) > LEAST_TOTAL) & (jnp.max(most) < MOST_TOTAL)

    @pl.when(jnp.logical_not(safe))
    def _():
        exact(here, query, key, value, out, group)


def attend(placement, lengths, query_rows, arrays, where, groups, sizes, kv_heads):
    prompt_count, chips, ring, tokens = sizes
    slots = prompt_count + 1
    group = query_rows.shape[1] // HD // kv_heads
    own_spec = pl.BlockSpec((tokens, group * HD), lambda g, *_: (0, g))
    whole = pl.BlockSpec(memory_space=pl.ANY)
    keys = slots * ring * tokens
    masked = tokens if tokens % HD == 0 else keys
    work = tokens * group * kv_heads * keys
    return pl.pallas_call(
        functools.partial(attend_kernel, sizes, where, groups),
        grid_spec=pltpu.PrefetchScalarGridSpec(
            num_scalar_prefetch=2,
            grid=(kv_heads,),
            in_specs=[own_spec] + [whole] * len(arrays),
            out_specs=own_spec,
            scratch_shapes=[
                pltpu.VMEM((keys, kv_heads * HD), jnp.bfloat16),
                pltpu.VMEM((keys, kv_heads * HD), jnp.bfloat16),
                pltpu.VMEM((keys, HD), jnp.bfloat16),
                pltpu.VMEM((tokens, masked), jnp.float32),
                pltpu.SemaphoreType.DMA((len(groups), 2, slots, ring)),
            ],
        ),
        out_shape=jax.ShapeDtypeStruct(query_rows.shape, query_rows.dtype),
        cost_estimate=pl.CostEstimate(flops=6 * work * HD, bytes_accessed=12 << 20, transcendentals=work),
        compiler_params=pltpu.CompilerParams(vmem_limit_bytes=2 * keys * kv_heads * 2 * HD * 2),
    )(placement, lengths, pltpu.with_memory_space_constraint(query_rows, pltpu.HBM), *arrays)


def after(x, *others):
    return lax.optimization_barrier((x, *others))[0]


def shards(query_rows, key_rows, value_rows, placement, lengths):
    blocks, ring = lax.axis_size("blk"), lax.axis_size("head")
    chips = blocks // CORES
    sizes = (blocks // 2, chips, ring, query_rows.shape[0])
    width = key_rows.shape[1]
    kv_heads = width // HD

    def next_hop(x):
        return lax.ppermute(x, "head", [(i, (i + 1) % ring) for i in range(ring)])

    def next_chip(x):
        return lax.ppermute(x, "blk", [(i, (i + CORES) % blocks) for i in range(blocks)])

    def other_core(x):
        return lax.ppermute(x, "blk", [(i, i ^ 1) for i in range(blocks)])

    columns, acrosses = [[key_rows], [value_rows]], [[], []]
    for hop in range(ring):
        for c in range(2):
            column, across = columns[c], acrosses[c]
            x = column[hop]
            if hop > 0:
                x = after(x, across[hop - 1])
            if hop < ring - 1:
                column.append(next_hop(x))
            if hop < ring - 1 or c == 1:
                across.append(next_chip(x))
            else:
                across.append(next_hop(after(across[-1], x)))
    planes = [columns, acrosses]
    bundles = [[(0, c, hop) for c in range(2)] + [(1, c, hop - 1) for c in range(2) if hop] for hop in range(ring - 1)]
    bundles += [[(0, c, ring - 1), (1, c, ring - 2)] for c in range(2)] + [[(1, c, ring - 1)] for c in range(2)]
    for back in range(2, chips):
        planes.append([[next_chip(x) for x in part] for part in planes[-1]])
        bundles.append([(back, c, hop) for hop in range(ring) for c in range(2)])
    arrays, where = [], {}
    for back, plane in enumerate(planes):
        for c in range(2):
            for hop in range(ring):
                where[c, back * CORES, hop] = len(arrays), 0
                arrays.append(plane[c][hop])
    for bundle in bundles:
        for place, (back, c, hop) in enumerate(bundle):
            where[c, back * CORES + 1, hop] = len(arrays), place * width
        packed = jnp.concatenate([planes[back][c][hop] for back, c, hop in bundle], axis=1)
        for c in range(2):
            if bundle == bundles[ring - 1 + c]:
                packed = after(packed, planes[1][c][ring - 1])
        if bundle == bundles[ring + 2]:
            packed = after(packed, arrays[-1])
        arrays.append(other_core(packed))
    groups = [(0, 1), (1, kv_heads)]
    return attend(placement, lengths, query_rows, arrays, where, groups, sizes, kv_heads)


def solution(mesh):
    rows = P(("grp", "blk", "head"), None)
    return jax.shard_map(
        shards,
        mesh=mesh,
        in_specs=(rows, rows, rows, P("grp"), P("grp")),
        out_specs=rows,
        check_vma=False,
    )
```

time: 204 us -> 208 us (1.020)
  waiting for transfers between devices: 23.3 us -> 34.8 us
  Pallas kernels: 147 us -> 154 us
  starting transfers between devices: 23.7 us -> 18.9 us
  other arithmetic: 4.27 us -> 0.24 us
  local copies, waits for them, and re-layouts: 3.88 us -> 0.02 us
    pallas_call x1, Pallas kernels: 147 us -> 154 us  [attend(): pl.pallas_call(functools.partial(attend_kernel, sizes, where, groups), gr...]
    ppermute x7, waiting for transfers between devices: 10.6 us -> 17.6 us  [next_hop(): return lax.ppermute(x, 'head', [(i, (i + 1) % ring) for i in range(ring)])]
    ppermute x5 -> x7, starting transfers between devices: 13.2 us -> 8.77 us  [other_core(): return lax.ppermute(x, 'blk', [(i, i ^ 1) for i in range(blocks)])]
    ppermute x7, waiting for transfers between devices: 11.1 us -> 15 us  [next_chip(): lax.ppermute(x, 'blk', [(i, (i + CORES) % blocks) for i in range(blocks)])]
    unnamed x8, local copies, waits for them, and re-layouts: 3.8 us -> 0.02 us
    reduce_sum x3 -> x0, other arithmetic: 3.33 us -> none  [the longest x1 1.29 us: scalars(): block = jnp.sum(jnp.where(jnp.arange(blocks) == index, placement, 0))]
  transfers between devices with their start and end apart: 19 -> 21, of which waited for: 10 -> 15; matrix products, arithmetic and copies ran while one was open for 2% -> 0% of each run, Pallas kernels for 0% -> 0%
where the time goes in v7:
time: 208 us
  Pallas kernels  154 us (74%)
  waiting for transfers between devices  34.8 us (17%)
  starting transfers between devices  18.9 us (9%)
    pallas_call x1, Pallas kernels, attend(): pl.pallas_call(functools.partial(attend_kernel, sizes, where, groups), gr...  154 us
    ppermute x7, waiting for transfers between devices, next_hop(): return lax.ppermute(x, 'head', [(i, (i + 1) % ring) for i in range(ring)])  17.6 us
    ppermute x7, waiting for transfers between devices, next_chip(): lax.ppermute(x, 'blk', [(i, (i + CORES) % blocks) for i in range(blocks)])  15 us
    ppermute x7, starting transfers between devices, other_core(): return lax.ppermute(x, 'blk', [(i, i ^ 1) for i in range(blocks)])  8.77 us
    ppermute x7, starting transfers between devices, next_hop(): return lax.ppermute(x, 'head', [(i, (i + 1) % ring) for i in range(ring)])  5.39 us
    ppermute x7, starting transfers between devices, next_chip(): lax.ppermute(x, 'blk', [(i, (i + CORES) % blocks) for i in range(blocks)])  4.74 us
  transfers between devices with their start and end apart: 21, of which 15 were waited for; matrix products, arithmetic and copies ran while one was open for 0% of the time, Pallas kernels for 0%

profile of v7, /device:TPU:1, one launch (start us, length us, event | category | flops | bytes accessed | tf_op | source)
XLA Modules:
  0.0 207.6 jit_solution(11563400891009102618)
XLA Ops:
  0.0 2.0 collective-permute-start.1
  2.0 1.3 collective-permute-start
  3.3 0.3 collective-permute-start.6
  3.6 1.3 collective-permute-start.5
  4.9 3.5 %collective-permute-done.1.refs_8_ = bf16[128,1024]{1,0:T(8,128)(2,1)S(1)} collective-permute-done((bf16[128,1024]{1,0:T(8,128)(2,1)}, bf16[128,1024]{1,0:T(8,128)(2,1)S(1)}, u32[]{:S(2)}, u32[]{:S(2)}) %collective-permute-start.1) | collective-permute-done | bytes 262176 | tf_op jit(solution)/shard_map/ppermute | solution.py:247
  8.4 2.8 %collective-permute-done.refs_1_ = bf16[128,1024]{1,0:T(8,128)(2,1)S(1)} collective-permute-done((bf16[128,1024]{1,0:T(8,128)(2,1)}, bf16[128,1024]{1,0:T(8,128)(2,1)S(1)}, u32[]{:S(2)}, u32[]{:S(2)}) %collective-permute-start) | collective-permute-done | bytes 262176 | tf_op jit(solution)/shard_map/ppermute | solution.py:244
  11.1 0.5 collective-permute-start.3
  11.6 2.4 %collective-permute-done.6.refs_12_ = bf16[128,1024]{1,0:T(8,128)(2,1)S(1)} collective-permute-done((bf16[128,1024]{1,0:T(8,128)(2,1)}, bf16[128,1024]{1,0:T(8,128)(2,1)S(1)}, u32[]{:S(2)}, u32[]{:S(2)}) %collective-permute-start.6) | collective-permute-done | bytes 262176 | tf_op jit(solution)/shard_map/ppermute | solution.py:247
  14.0 2.8 %collective-permute-done.5.refs_5_ = bf16[128,1024]{1,0:T(8,128)(2,1)S(1)} collective-permute-done((bf16[128,1024]{1,0:T(8,128)(2,1)}, bf16[128,1024]{1,0:T(8,128)(2,1)S(1)}, u32[]{:S(2)}, u32[]{:S(2)}) %collective-permute-start.5) | collective-permute-done | bytes 262176 | tf_op jit(solution)/shard_map/ppermute | solution.py:244
  16.7 0.5 collective-permute-start.8
  17.2 1.1 collective-permute-done.3.refs_9_
  18.3 3.9 %collective-permute-done.2.refs_2_ = bf16[128,1024]{1,0:T(8,128)(2,1)S(1)} collective-permute-done((bf16[128,1024]{1,0:T(8,128)(2,1)S(1)}, bf16[128,1024]{1,0:T(8,128)(2,1)S(1)}, u32[]{:S(2)}, u32[]{:S(2)}) %collective-permute-start.2) | collective-permute-done | bytes 262176 | tf_op jit(solution)/shard_map/ppermute | solution.py:244
  22.2 0.1 pad_maximum_fusion
  22.3 3.7 %collective-permute-start.15 = (bf16[128,4096]{1,0:T(8,128)(2,1)S(1)}, bf16[128,4096]{1,0:T(8,128)(2,1)S(1)}, u32[]{:S(2)}, u32[]{:S(2)}) collective-permute-start(bf16[128,4096]{1,0:T(8,128)(2,1)S(1)} %pad_maximum_fusion), channel_id=1, source_target_pairs={{0,4},{4,0},{8,12},{12,8},{1,5},{5,1},{9,13},{13,9},{2,6},{6,2},{1... | collective-permute-start | bytes 3145736 | tf_op jit(solution)/shard_map/ppermute | solution.py:250
  26.0 1.8 collective-permute-done.7.refs_6_
  27.8 0.4 collective-permute-start.9
  28.2 1.4 collective-permute-done.10.refs_10_
  29.5 2.4 %collective-permute-start.11 = (bf16[128,1024]{1,0:T(8,128)(2,1)S(1)}, bf16[128,1024]{1,0:T(8,128)(2,1)S(1)}, u32[]{:S(2)}, u32[]{:S(2)}) collective-permute-start(bf16[128,1024]{1,0:T(8,128)(2,1)S(1)} %collective-permute-done.10.refs_10_), channel_id=1, source_target_pairs={{0,1},{1,2},{2,3},{3,0},{4,5},{5,6},{6,7},{7,4},{8,9},{9,10},{10,1... | collective-permute-start | bytes 786440 | tf_op jit(solution)/shard_map/ppermute | solution.py:244
  32.1 3.9 %collective-permute-done.12.refs_14_ = bf16[128,1024]{1,0:T(8,128)(2,1)S(1)} collective-permute-done((bf16[128,1024]{1,0:T(8,128)(2,1)S(1)}, bf16[128,1024]{1,0:T(8,128)(2,1)S(1)}, u32[]{:S(2)}, u32[]{:S(2)}) %collective-permute-start.12) | collective-permute-done | bytes 262176 | tf_op jit(solution)/shard_map/ppermute | solution.py:247
  36.0 1.7 collective-permute-start.16
  37.7 3.6 %collective-permute-done.9.refs_7_ = bf16[128,1024]{1,0:T(8,128)(2,1)S(1)} collective-permute-done((bf16[128,1024]{1,0:T(8,128)(2,1)S(1)}, bf16[128,1024]{1,0:T(8,128)(2,1)S(1)}, u32[]{:S(2)}, u32[]{:S(2)}) %collective-permute-start.9) | collective-permute-done | bytes 262176 | tf_op jit(solution)/shard_map/ppermute | solution.py:244
  41.3 1.3 collective-permute-start.14
  42.6 1.5 collective-permute-start.13
  44.1 2.8 %collective-permute-done.11.refs_11_ = bf16[128,1024]{1,0:T(8,128)(2,1)S(1)} collective-permute-done((bf16[128,1024]{1,0:T(8,128)(2,1)S(1)}, bf16[128,1024]{1,0:T(8,128)(2,1)S(1)}, u32[]{:S(2)}, u32[]{:S(2)}) %collective-permute-start.11) | collective-permute-done | bytes 262176 | tf_op jit(solution)/shard_map/ppermute | solution.py:244
  46.9 0.8 collective-permute-start.19
  47.8 2.8 %collective-permute-done.13.refs_15_ = bf16[128,1024]{1,0:T(8,128)(2,1)S(1)} collective-permute-done((bf16[128,1024]{1,0:T(8,128)(2,1)S(1)}, bf16[128,1024]{1,0:T(8,128)(2,1)S(1)}, u32[]{:S(2)}, u32[]{:S(2)}) %collective-permute-start.13) | collective-permute-done | bytes 262176 | tf_op jit(solution)/shard_map/ppermute | solution.py:247
  50.6 0.7 collective-permute-start.17
  51.4 0.5 collective-permute-start.20
  51.9 1.0 collective-permute-done.17.refs_19_
  52.9 0.7 collective-permute-done.18.refs_20_
  53.6 0.4 collective-permute-done.20.refs_22_
  54.0 153.6 %shard_map.55 = bf16[128,8192]{1,0:T(8,128)(2,1)} custom-call(s32[4]{0:T(128)S(1)} %copy-done.2, s32[2]{0:T(128)S(1)} %copy-done.3, bf16[128,8192]{1,0:T(8,128)(2,1)} %query.1, bf16[128,1024]{1,0:T(8,128)(2,1)S(1)} %copy-done, bf16[128,1024]{1,0:T(8,128)(2,1)S(1)} %collective-permute-done.refs_1_, bf16[128,1024]{1,0:T(8,128)(2,1)S(1)} %collective-permute-done.2.refs_2_, ...), custom_call_target="tpu_custom_call" | custom-call | flops 9663676416 | bytes 12582912 | tf_op jit(solution)/shard_map/pallas_call | solution.py:211
  (24 shorter events, 0.2 us)
Async XLA Ops:
  0.0 37.7 %copy-start = (bf16[128,1024]{1,0:T(8,128)(2,1)S(1)}, bf16[128,1024]{1,0:T(8,128)(2,1)}, u32[]{:S(2)}) copy-start(bf16[128,1024]{1,0:T(8,128)(2,1)} %refs_0_.1) | copy-start | bytes 786436
  0.0 37.7 %copy-start.1 = (bf16[128,1024]{1,0:T(8,128)(2,1)S(1)}, bf16[128,1024]{1,0:T(8,128)(2,1)}, u32[]{:S(2)}) copy-start(bf16[128,1024]{1,0:T(8,128)(2,1)} %refs_4_.1) | copy-start | bytes 786436
  0.0 8.3 %collective-permute-start.1 = (bf16[128,1024]{1,0:T(8,128)(2,1)}, bf16[128,1024]{1,0:T(8,128)(2,1)S(1)}, u32[]{:S(2)}, u32[]{:S(2)}) collective-permute-start(bf16[128,1024]{1,0:T(8,128)(2,1)} %refs_0_.1), channel_id=1, source_target_pairs={{0,8},{4,12},{8,0},{12,4},{1,9},{5,13},{9,1},{13,5},{2,10},{6,14},... | collective-permute-start | bytes 786440 | tf_op jit(solution)/shard_map/ppermute | solution.py:247
  2.0 9.1 %collective-permute-start = (bf16[128,1024]{1,0:T(8,128)(2,1)}, bf16[128,1024]{1,0:T(8,128)(2,1)S(1)}, u32[]{:S(2)}, u32[]{:S(2)}) collective-permute-start(bf16[128,1024]{1,0:T(8,128)(2,1)} %refs_0_.1), channel_id=1, source_target_pairs={{0,1},{1,2},{2,3},{3,0},{4,5},{5,6},{6,7},{7,4},{8,9},{9,10},{10,1... | collective-permute-start | bytes 786440 | tf_op jit(solution)/shard_map/ppermute | solution.py:244
  3.3 10.6 %collective-permute-start.6 = (bf16[128,1024]{1,0:T(8,128)(2,1)}, bf16[128,1024]{1,0:T(8,128)(2,1)S(1)}, u32[]{:S(2)}, u32[]{:S(2)}) collective-permute-start(bf16[128,1024]{1,0:T(8,128)(2,1)} %refs_4_.1), channel_id=1, source_target_pairs={{0,8},{4,12},{8,0},{12,4},{1,9},{5,13},{9,1},{13,5},{2,10},{6,14},... | collective-permute-start | bytes 786440 | tf_op jit(solution)/shard_map/ppermute | solution.py:247
  3.6 13.1 %collective-permute-start.5 = (bf16[128,1024]{1,0:T(8,128)(2,1)}, bf16[128,1024]{1,0:T(8,128)(2,1)S(1)}, u32[]{:S(2)}, u32[]{:S(2)}) collective-permute-start(bf16[128,1024]{1,0:T(8,128)(2,1)} %refs_4_.1), channel_id=1, source_target_pairs={{0,1},{1,2},{2,3},{3,0},{4,5},{5,6},{6,7},{7,4},{8,9},{9,10},{10,1... | collective-permute-start | bytes 786440 | tf_op jit(solution)/shard_map/ppermute | solution.py:244
  11.1 7.2 %collective-permute-start.3 = (bf16[128,1024]{1,0:T(8,128)(2,1)S(1)}, bf16[128,1024]{1,0:T(8,128)(2,1)S(1)}, u32[]{:S(2)}, u32[]{:S(2)}) collective-permute-start(bf16[128,1024]{1,0:T(8,128)(2,1)S(1)} %collective-permute-done.refs_1_), channel_id=1, source_target_pairs={{0,8},{4,12},{8,0},{12,4},{1,9},{5,13},{9,1},{13,5},{2,10},{6,14},... | collective-permute-start | bytes 786440 | tf_op jit(solution)/shard_map/ppermute | solution.py:247
  11.6 10.6 %collective-permute-start.2 = (bf16[128,1024]{1,0:T(8,128)(2,1)S(1)}, bf16[128,1024]{1,0:T(8,128)(2,1)S(1)}, u32[]{:S(2)}, u32[]{:S(2)}) collective-permute-start(bf16[128,1024]{1,0:T(8,128)(2,1)S(1)} %collective-permute-done.refs_1_), channel_id=1, source_target_pairs={{0,1},{1,2},{2,3},{3,0},{4,5},{5,6},{6,7},{7,4},{8,9},{9,10},{10,1... | collective-permute-start | bytes 786440 | tf_op jit(solution)/shard_map/ppermute | solution.py:244
  16.7 9.3 %collective-permute-start.8 = (bf16[128,1024]{1,0:T(8,128)(2,1)S(1)}, bf16[128,1024]{1,0:T(8,128)(2,1)S(1)}, u32[]{:S(2)}, u32[]{:S(2)}) collective-permute-start(bf16[128,1024]{1,0:T(8,128)(2,1)S(1)} %collective-permute-done.5.refs_5_), channel_id=1, source_target_pairs={{0,8},{4,12},{8,0},{12,4},{1,9},{5,13},{9,1},{13,5},{2,10},{6,14},... | collective-permute-start | bytes 786440 | tf_op jit(solution)/shard_map/ppermute | solution.py:247
  17.2 10.6 %collective-permute-start.7 = (bf16[128,1024]{1,0:T(8,128)(2,1)S(1)}, bf16[128,1024]{1,0:T(8,128)(2,1)S(1)}, u32[]{:S(2)}, u32[]{:S(2)}) collective-permute-start(bf16[128,1024]{1,0:T(8,128)(2,1)S(1)} %collective-permute-done.5.refs_5_), channel_id=1, source_target_pairs={{0,1},{1,2},{2,3},{3,0},{4,5},{5,6},{6,7},{7,4},{8,9},{9,10},{10,1... | collective-permute-start | bytes 786440 | tf_op jit(solution)/shard_map/ppermute | solution.py:244
  22.2 7.3 %collective-permute-start.10 = (bf16[128,1024]{1,0:T(8,128)(2,1)S(1)}, bf16[128,1024]{1,0:T(8,128)(2,1)S(1)}, u32[]{:S(2)}, u32[]{:S(2)}) collective-permute-start(bf16[128,1024]{1,0:T(8,128)(2,1)S(1)} %collective-permute-done.2.refs_2_), channel_id=1, source_target_pairs={{0,8},{4,12},{8,0},{12,4},{1,9},{5,13},{9,1},{13,5},{2,10},{6,14},... | collective-permute-start | bytes 786440 | tf_op jit(solution)/shard_map/ppermute | solution.py:247
  22.3 31.7 %copy-start.2 = (s32[4]{0:T(128)S(1)}, s32[4]{0:T(128)}, u32[]{:S(2)}) copy-start(s32[4]{0:T(128)} %placement.1) | copy-start | bytes 52
  22.3 31.7 %copy-start.3 = (s32[2]{0:T(128)S(1)}, s32[2]{0:T(128)}, u32[]{:S(2)}) copy-start(s32[2]{0:T(128)} %lengths.1) | copy-start | bytes 28
  22.3 29.6 %collective-permute-start.15 = (bf16[128,4096]{1,0:T(8,128)(2,1)S(1)}, bf16[128,4096]{1,0:T(8,128)(2,1)S(1)}, u32[]{:S(2)}, u32[]{:S(2)}) collective-permute-start(bf16[128,4096]{1,0:T(8,128)(2,1)S(1)} %pad_maximum_fusion), channel_id=1, source_target_pairs={{0,4},{4,0},{8,12},{12,8},{1,5},{5,1},{9,13},{13,9},{2,6},{6,2},{1... | collective-permute-start | bytes 3145736 | tf_op jit(solution)/shard_map/ppermute | solution.py:250
  26.0 16.6 %collective-permute-start.4 = (bf16[128,1024]{1,0:T(8,128)(2,1)S(1)}, bf16[128,1024]{1,0:T(8,128)(2,1)S(1)}, u32[]{:S(2)}, u32[]{:S(2)}) collective-permute-start(bf16[128,1024]{1,0:T(8,128)(2,1)S(1)} %collective-permute-done.2.refs_2_), channel_id=1, source_target_pairs={{0,1},{1,2},{2,3},{3,0},{4,5},{5,6},{6,7},{7,4},{8,9},{9,10},{10,1... | collective-permute-start | bytes 786440 | tf_op jit(solution)/shard_map/ppermute | solution.py:244
  27.8 8.1 %collective-permute-start.12 = (bf16[128,1024]{1,0:T(8,128)(2,1)S(1)}, bf16[128,1024]{1,0:T(8,128)(2,1)S(1)}, u32[]{:S(2)}, u32[]{:S(2)}) collective-permute-start(bf16[128,1024]{1,0:T(8,128)(2,1)S(1)} %collective-permute-done.7.refs_6_), channel_id=1, source_target_pairs={{0,8},{4,12},{8,0},{12,4},{1,9},{5,13},{9,1},{13,5},{2,10},{6,14},... | collective-permute-start | bytes 786440 | tf_op jit(solution)/shard_map/ppermute | solution.py:247
  27.8 13.4 %collective-permute-start.9 = (bf16[128,1024]{1,0:T(8,128)(2,1)S(1)}, bf16[128,1024]{1,0:T(8,128)(2,1)S(1)}, u32[]{:S(2)}, u32[]{:S(2)}) collective-permute-start(bf16[128,1024]{1,0:T(8,128)(2,1)S(1)} %collective-permute-done.7.refs_6_), channel_id=1, source_target_pairs={{0,1},{1,2},{2,3},{3,0},{4,5},{5,6},{6,7},{7,4},{8,9},{9,10},{10,1... | collective-permute-start | bytes 786440 | tf_op jit(solution)/shard_map/ppermute | solution.py:244
  29.5 17.4 %collective-permute-start.11 = (bf16[128,1024]{1,0:T(8,128)(2,1)S(1)}, bf16[128,1024]{1,0:T(8,128)(2,1)S(1)}, u32[]{:S(2)}, u32[]{:S(2)}) collective-permute-start(bf16[128,1024]{1,0:T(8,128)(2,1)S(1)} %collective-permute-done.10.refs_10_), channel_id=1, source_target_pairs={{0,1},{1,2},{2,3},{3,0},{4,5},{5,6},{6,7},{7,4},{8,9},{9,10},{10,1... | collective-permute-start | bytes 786440 | tf_op jit(solution)/shard_map/ppermute | solution.py:244
  36.0 17.7 %collective-permute-start.16 = (bf16[128,4096]{1,0:T(8,128)(2,1)S(1)}, bf16[128,4096]{1,0:T(8,128)(2,1)S(1)}, u32[]{:S(2)}, u32[]{:S(2)}) collective-permute-start(bf16[128,4096]{1,0:T(8,128)(2,1)S(1)} %pad_maximum_fusion.1), channel_id=1, source_target_pairs={{0,4},{4,0},{8,12},{12,8},{1,5},{5,1},{9,13},{13,9},{2,6},{6,2},{1... | collective-permute-start | bytes 3145736 | tf_op jit(solution)/shard_map/ppermute | solution.py:250
  41.3 10.1 %collective-permute-start.14 = (bf16[128,2048]{1,0:T(8,128)(2,1)S(1)}, bf16[128,2048]{1,0:T(8,128)(2,1)S(1)}, u32[]{:S(2)}, u32[]{:S(2)}) collective-permute-start(bf16[128,2048]{1,0:T(8,128)(2,1)S(1)} %pad_maximum_fusion.2), channel_id=1, source_target_pairs={{0,4},{4,0},{8,12},{12,8},{1,5},{5,1},{9,13},{13,9},{2,6},{6,2},{1... | collective-permute-start | bytes 1572872 | tf_op jit(solution)/shard_map/ppermute | solution.py:250
  42.6 8.0 %collective-permute-start.13 = (bf16[128,1024]{1,0:T(8,128)(2,1)S(1)}, bf16[128,1024]{1,0:T(8,128)(2,1)S(1)}, u32[]{:S(2)}, u32[]{:S(2)}) collective-permute-start(bf16[128,1024]{1,0:T(8,128)(2,1)S(1)} %collective-permute-done.9.refs_7_), channel_id=1, source_target_pairs={{0,8},{4,12},{8,0},{12,4},{1,9},{5,13},{9,1},{13,5},{2,10},{6,14},... | collective-permute-start | bytes 786440 | tf_op jit(solution)/shard_map/ppermute | solution.py:247
  46.9 4.5 %collective-permute-start.19 = (bf16[128,1024]{1,0:T(8,128)(2,1)S(1)}, bf16[128,1024]{1,0:T(8,128)(2,1)S(1)}, u32[]{:S(2)}, u32[]{:S(2)}) collective-permute-start(bf16[128,1024]{1,0:T(8,128)(2,1)S(1)} %collective-permute-done.11.refs_11_), channel_id=1, source_target_pairs={{0,4},{4,0},{8,12},{12,8},{1,5},{5,1},{9,13},{13,9},{2,6},{6,2},{1... | collective-permute-start | bytes 786440 | tf_op jit(solution)/shard_map/ppermute | solution.py:250
  50.6 2.3 %collective-permute-start.17 = (bf16[128,2048]{1,0:T(8,128)(2,1)S(1)}, bf16[128,2048]{1,0:T(8,128)(2,1)S(1)}, u32[]{:S(2)}, u32[]{:S(2)}) collective-permute-start(bf16[128,2048]{1,0:T(8,128)(2,1)S(1)} %pad_maximum_fusion.3), channel_id=1, source_target_pairs={{0,4},{4,0},{8,12},{12,8},{1,5},{5,1},{9,13},{13,9},{2,6},{6,2},{1... | collective-permute-start | bytes 1572872 | tf_op jit(solution)/shard_map/ppermute | solution.py:250
  51.4 2.3 %collective-permute-start.18 = (bf16[128,2048]{1,0:T(8,128)(2,1)S(1)}, bf16[128,2048]{1,0:T(8,128)(2,1)S(1)}, u32[]{:S(2)}, u32[]{:S(2)}) collective-permute-start(bf16[128,2048]{1,0:T(8,128)(2,1)S(1)} %pad_maximum_fusion.4), channel_id=1, source_target_pairs={{0,4},{4,0},{8,12},{12,8},{1,5},{5,1},{9,13},{13,9},{2,6},{6,2},{1... | collective-permute-start | bytes 1572872 | tf_op jit(solution)/shard_map/ppermute | solution.py:250
  51.4 2.6 %collective-permute-start.20 = (bf16[128,1024]{1,0:T(8,128)(2,1)S(1)}, bf16[128,1024]{1,0:T(8,128)(2,1)S(1)}, u32[]{:S(2)}, u32[]{:S(2)}) collective-permute-start(bf16[128,1024]{1,0:T(8,128)(2,1)S(1)} %collective-permute-done.13.refs_15_), channel_id=1, source_target_pairs={{0,4},{4,0},{8,12},{12,8},{1,5},{5,1},{9,13},{13,9},{2,6},{6,2},{1... | collective-permute-start | bytes 786440 | tf_op jit(solution)/shard_map/ppermute | solution.py:250

commit v8 on v7

--- a/solution.py
+++ b/solution.py
@@ -10,7 +10,7 @@
 
 HD = 128
 CORES = 2
-HEADS_PER_TILE = 2
+HEADS_PER_TILE = 8
 EXP2_SCALE = math.log2(math.e) / math.sqrt(HD)
 LEAST_TOTAL, MOST_TOTAL = 1e-20, 1e30
 
@@ -166,32 +166,30 @@
     column = pl.ds(pl.multiple_of(kv_head * HD, HD), HD)
     key, value = held_key.at[:, column], held_value.at[:, column]
     kept = here.kept()
-    span = HEADS_PER_TILE * HD
-
-    def one_tile(tile, carry):
-        least, most = carry
-        columns = pl.ds(pl.multiple_of(tile * span, span), span)
-        query_tile = query[:, columns]
-        query_tile = jnp.concatenate([query_tile[:, h * HD : (h + 1) * HD] for h in range(HEADS_PER_TILE)], axis=0)
-        scores = matmul_nt(query_tile, key[...]) * EXP2_SCALE
-        split = scores.shape[1] - masked
-        tail = scores[:, split:].reshape(HEADS_PER_TILE, tokens, masked) + bias[...][None]
-        tail = tail.reshape(HEADS_PER_TILE * tokens, masked)
-        scores = tail if split == 0 else jnp.concatenate([scores[:, :split], tail], axis=1)
-        weights = jnp.exp2(scores).astype(jnp.bfloat16)
-        values = jnp.concatenate([value[...], ones[...]], axis=1)
-        summed = jnp.dot(weights, values, preferred_element_type=jnp.float32)
-        results = []
-        for i in range(HEADS_PER_TILE):
+    zeros = jnp.zeros((tokens, HD), jnp.float32)
+    least, most = zeros + jnp.inf, zeros
+    rows = ring * tokens
+    for tile in range(group // HEADS_PER_TILE):
+        heads = range(tile * HEADS_PER_TILE, (tile + 1) * HEADS_PER_TILE)
+        query_tile = jnp.concatenate([query[:, h * HD : (h + 1) * HD] for h in heads], axis=0)
+        summed = None
+        for slot in range(here.slots):
+            block = pl.ds(slot * rows, rows)
+            scores = matmul_nt(query_tile, key[block, :]) * EXP2_SCALE
+            if slot == prompt_count:
+                split = rows - masked
+                tail = scores[:, split:].reshape(HEADS_PER_TILE, tokens, masked) + bias[...][None]
+                tail = tail.reshape(HEADS_PER_TILE * tokens, masked)
+                scores = tail if split == 0 else jnp.concatenate([scores[:, :split], tail], axis=1)
+            weights = jnp.exp2(scores).astype(jnp.bfloat16)
+            values = jnp.concatenate([value[block, :], ones[block, :]], axis=1)
+            part = jnp.dot(weights, values, preferred_element_type=jnp.float32)
+            summed = part if summed is None else summed + part
+        for i, h in enumerate(heads):
             part = summed[i * tokens : (i + 1) * tokens]
             total = part[:, HD:]
             least, most = jnp.minimum(least, total), jnp.maximum(most, total)
-            results.append(jnp.where(kept, part[:, :HD] / total, 0.0).astype(out.dtype))
-        out[:, columns] = jnp.concatenate(results, axis=1)
-        return least, most
-
-    zeros = jnp.zeros((tokens, HD), jnp.float32)
-    least, most = lax.fori_loop(0, group // HEADS_PER_TILE, one_tile, (zeros + jnp.inf, zeros))
+            out[:, h * HD : (h + 1) * HD] = jnp.where(kept, part[:, :HD] / total, 0.0).astype(out.dtype)
     safe = (jnp.min(least) > LEAST_TOTAL) & (jnp.max(most) < MOST_TOTAL)
 
     @pl.when(jnp.logical_not(safe))
@@ -206,7 +204,7 @@
     own_spec = pl.BlockSpec((tokens, group * HD), lambda g, *_: (0, g))
     whole = pl.BlockSpec(memory_space=pl.ANY)
     keys = slots * ring * tokens
-    masked = tokens if tokens % HD == 0 else keys
+    masked = tokens if tokens % HD == 0 else ring * tokens
     work = tokens * group * kv_heads * keys
     return pl.pallas_call(
         functools.partial(attend_kernel, sizes, where, groups),
@@ -225,7 +223,7 @@
         ),
         out_shape=jax.ShapeDtypeStruct(query_rows.shape, query_rows.dtype),
         cost_estimate=pl.CostEstimate(flops=6 * work * HD, bytes_accessed=12 << 20, transcendentals=work),
-        compiler_params=pltpu.CompilerParams(vmem_limit_bytes=2 * keys * kv_heads * 2 * HD * 2),
+        compiler_params=pltpu.CompilerParams(vmem_limit_bytes=2 * keys * kv_heads * 2 * HD * 2 + (12 << 20)),
     )(placement, lengths, pltpu.with_memory_space_constraint(query_rows, pltpu.HBM), *arrays)
 
 

time: 208 us -> 205 us (0.986)
  the two profiles are of different devices: /device:TPU:1 before, /device:TPU:0 now
where the time goes in v8:
time: 205 us
  Pallas kernels  151 us (74%)
  waiting for transfers between devices  41 us (20%)
  starting transfers between devices  13 us (6%)
    pallas_call x1, Pallas kernels, attend(): pl.pallas_call(functools.partial(attend_kernel, sizes, where, groups), gr...  151 us
    ppermute x7, waiting for transfers between devices, next_hop(): return lax.ppermute(x, 'head', [(i, (i + 1) % ring) for i in range(ring)])  22 us
    ppermute x7, waiting for transfers between devices, next_chip(): lax.ppermute(x, 'blk', [(i, (i + CORES) % blocks) for i in range(blocks)])  16.6 us
    ppermute x7, starting transfers between devices, next_chip(): lax.ppermute(x, 'blk', [(i, (i + CORES) % blocks) for i in range(blocks)])  6.68 us
    ppermute x7, starting transfers between devices, next_hop(): return lax.ppermute(x, 'head', [(i, (i + 1) % ring) for i in range(ring)])  5.66 us
  transfers between devices with their start and end apart: 21, of which 16 were waited for; matrix products, arithmetic and copies ran while one was open for 0% of the time, Pallas kernels for 0%

profile of v8, /device:TPU:0, one launch (start us, length us, event | category | flops | bytes accessed | tf_op | source)
XLA Modules:
  0.0 205.1 jit_solution(8175296041179044520)
XLA Ops:
  0.0 2.9 %collective-permute-start.1 = (bf16[128,1024]{1,0:T(8,128)(2,1)}, bf16[128,1024]{1,0:T(8,128)(2,1)S(1)}, u32[]{:S(2)}, u32[]{:S(2)}) collective-permute-start(bf16[128,1024]{1,0:T(8,128)(2,1)} %refs_0_.1), channel_id=1, source_target_pairs={{0,8},{4,12},{8,0},{12,4},{1,9},{5,13},{9,1},{13,5},{2,10},{6,14},... | collective-permute-start | bytes 786440 | tf_op jit(solution)/shard_map/ppermute | solution.py:245
  2.9 1.6 collective-permute-start
  4.5 0.5 collective-permute-start.6
  5.1 1.6 collective-permute-start.5
  6.6 3.7 %collective-permute-done.1.refs_8_ = bf16[128,1024]{1,0:T(8,128)(2,1)S(1)} collective-permute-done((bf16[128,1024]{1,0:T(8,128)(2,1)}, bf16[128,1024]{1,0:T(8,128)(2,1)S(1)}, u32[]{:S(2)}, u32[]{:S(2)}) %collective-permute-start.1) | collective-permute-done | bytes 262176 | tf_op jit(solution)/shard_map/ppermute | solution.py:245
  10.4 3.8 %collective-permute-done.refs_1_ = bf16[128,1024]{1,0:T(8,128)(2,1)S(1)} collective-permute-done((bf16[128,1024]{1,0:T(8,128)(2,1)}, bf16[128,1024]{1,0:T(8,128)(2,1)S(1)}, u32[]{:S(2)}, u32[]{:S(2)}) %collective-permute-start) | collective-permute-done | bytes 262176 | tf_op jit(solution)/shard_map/ppermute | solution.py:242
  14.2 0.3 collective-permute-start.3
  14.5 1.5 collective-permute-done.6.refs_12_
  16.0 3.8 %collective-permute-done.5.refs_5_ = bf16[128,1024]{1,0:T(8,128)(2,1)S(1)} collective-permute-done((bf16[128,1024]{1,0:T(8,128)(2,1)}, bf16[128,1024]{1,0:T(8,128)(2,1)S(1)}, u32[]{:S(2)}, u32[]{:S(2)}) %collective-permute-start.5) | collective-permute-done | bytes 262176 | tf_op jit(solution)/shard_map/ppermute | solution.py:242
  19.8 0.3 collective-permute-start.8
  20.1 1.6 collective-permute-done.3.refs_9_
  21.7 3.9 %collective-permute-done.2.refs_2_ = bf16[128,1024]{1,0:T(8,128)(2,1)S(1)} collective-permute-done((bf16[128,1024]{1,0:T(8,128)(2,1)S(1)}, bf16[128,1024]{1,0:T(8,128)(2,1)S(1)}, u32[]{:S(2)}, u32[]{:S(2)}) %collective-permute-start.2) | collective-permute-done | bytes 262176 | tf_op jit(solution)/shard_map/ppermute | solution.py:242
  25.5 0.2 collective-permute-start.10
  25.8 0.1 pad_maximum_fusion
  25.9 0.1 collective-permute-start.15
  26.0 1.4 collective-permute-done.8.refs_13_
  27.4 2.2 %collective-permute-done.7.refs_6_ = bf16[128,1024]{1,0:T(8,128)(2,1)S(1)} collective-permute-done((bf16[128,1024]{1,0:T(8,128)(2,1)S(1)}, bf16[128,1024]{1,0:T(8,128)(2,1)S(1)}, u32[]{:S(2)}, u32[]{:S(2)}) %collective-permute-start.7) | collective-permute-done | bytes 262176 | tf_op jit(solution)/shard_map/ppermute | solution.py:242
  29.7 0.5 collective-permute-start.12
  30.2 0.6 collective-permute-start.9
  30.8 2.3 %collective-permute-done.10.refs_10_ = bf16[128,1024]{1,0:T(8,128)(2,1)S(1)} collective-permute-done((bf16[128,1024]{1,0:T(8,128)(2,1)S(1)}, bf16[128,1024]{1,0:T(8,128)(2,1)S(1)}, u32[]{:S(2)}, u32[]{:S(2)}) %collective-permute-start.10) | collective-permute-done | bytes 262176 | tf_op jit(solution)/shard_map/ppermute | solution.py:245
  33.0 1.9 collective-permute-start.11
  35.0 2.6 %collective-permute-done.12.refs_14_ = bf16[128,1024]{1,0:T(8,128)(2,1)S(1)} collective-permute-done((bf16[128,1024]{1,0:T(8,128)(2,1)S(1)}, bf16[128,1024]{1,0:T(8,128)(2,1)S(1)}, u32[]{:S(2)}, u32[]{:S(2)}) %collective-permute-start.12) | collective-permute-done | bytes 262176 | tf_op jit(solution)/shard_map/ppermute | solution.py:245
  37.7 4.9 %collective-permute-done.9.refs_7_ = bf16[128,1024]{1,0:T(8,128)(2,1)S(1)} collective-permute-done((bf16[128,1024]{1,0:T(8,128)(2,1)S(1)}, bf16[128,1024]{1,0:T(8,128)(2,1)S(1)}, u32[]{:S(2)}, u32[]{:S(2)}) %collective-permute-start.9) | collective-permute-done | bytes 262176 | tf_op jit(solution)/shard_map/ppermute | solution.py:242
  42.5 1.8 collective-permute-start.13
  44.3 3.4 %collective-permute-done.11.refs_11_ = bf16[128,1024]{1,0:T(8,128)(2,1)S(1)} collective-permute-done((bf16[128,1024]{1,0:T(8,128)(2,1)S(1)}, bf16[128,1024]{1,0:T(8,128)(2,1)S(1)}, u32[]{:S(2)}, u32[]{:S(2)}) %collective-permute-start.11) | collective-permute-done | bytes 262176 | tf_op jit(solution)/shard_map/ppermute | solution.py:242
  47.8 3.5 %collective-permute-done.13.refs_15_ = bf16[128,1024]{1,0:T(8,128)(2,1)S(1)} collective-permute-done((bf16[128,1024]{1,0:T(8,128)(2,1)S(1)}, bf16[128,1024]{1,0:T(8,128)(2,1)S(1)}, u32[]{:S(2)}, u32[]{:S(2)}) %collective-permute-start.13) | collective-permute-done | bytes 262176 | tf_op jit(solution)/shard_map/ppermute | solution.py:245
  51.3 0.5 collective-permute-start.18
  51.8 0.1 collective-permute-start.20
  51.9 1.3 collective-permute-done.17.refs_19_
  53.2 0.7 collective-permute-done.18.refs_20_
  54.0 0.4 collective-permute-done.20.refs_22_
  54.3 150.8 %shard_map.55 = bf16[128,8192]{1,0:T(8,128)(2,1)} custom-call(s32[4]{0:T(128)S(1)} %copy-done.2, s32[2]{0:T(128)S(1)} %copy-done.3, bf16[128,8192]{1,0:T(8,128)(2,1)} %query.1, bf16[128,1024]{1,0:T(8,128)(2,1)S(1)} %copy-done, bf16[128,1024]{1,0:T(8,128)(2,1)S(1)} %collective-permute-done.refs_1_, bf16[128,1024]{1,0:T(8,128)(2,1)S(1)} %collective-permute-done.2.refs_2_, ...), custom_call_target="tpu_custom_call" | custom-call | flops 9663676416 | bytes 12582912 | tf_op jit(solution)/shard_map/pallas_call | solution.py:209
  (24 shorter events, 0.3 us)
Async XLA Ops:
  0.0 37.6 %copy-start = (bf16[128,1024]{1,0:T(8,128)(2,1)S(1)}, bf16[128,1024]{1,0:T(8,128)(2,1)}, u32[]{:S(2)}) copy-start(bf16[128,1024]{1,0:T(8,128)(2,1)} %refs_0_.1) | copy-start | bytes 786436
  0.0 37.6 %copy-start.1 = (bf16[128,1024]{1,0:T(8,128)(2,1)S(1)}, bf16[128,1024]{1,0:T(8,128)(2,1)}, u32[]{:S(2)}) copy-start(bf16[128,1024]{1,0:T(8,128)(2,1)} %refs_4_.1) | copy-start | bytes 786436
  0.0 10.3 %collective-permute-start.1 = (bf16[128,1024]{1,0:T(8,128)(2,1)}, bf16[128,1024]{1,0:T(8,128)(2,1)S(1)}, u32[]{:S(2)}, u32[]{:S(2)}) collective-permute-start(bf16[128,1024]{1,0:T(8,128)(2,1)} %refs_0_.1), channel_id=1, source_target_pairs={{0,8},{4,12},{8,0},{12,4},{1,9},{5,13},{9,1},{13,5},{2,10},{6,14},... | collective-permute-start | bytes 786440 | tf_op jit(solution)/shard_map/ppermute | solution.py:245
  2.9 11.2 %collective-permute-start = (bf16[128,1024]{1,0:T(8,128)(2,1)}, bf16[128,1024]{1,0:T(8,128)(2,1)S(1)}, u32[]{:S(2)}, u32[]{:S(2)}) collective-permute-start(bf16[128,1024]{1,0:T(8,128)(2,1)} %refs_0_.1), channel_id=1, source_target_pairs={{0,1},{1,2},{2,3},{3,0},{4,5},{5,6},{6,7},{7,4},{8,9},{9,10},{10,1... | collective-permute-start | bytes 786440 | tf_op jit(solution)/shard_map/ppermute | solution.py:242
  4.5 11.5 %collective-permute-start.6 = (bf16[128,1024]{1,0:T(8,128)(2,1)}, bf16[128,1024]{1,0:T(8,128)(2,1)S(1)}, u32[]{:S(2)}, u32[]{:S(2)}) collective-permute-start(bf16[128,1024]{1,0:T(8,128)(2,1)} %refs_4_.1), channel_id=1, source_target_pairs={{0,8},{4,12},{8,0},{12,4},{1,9},{5,13},{9,1},{13,5},{2,10},{6,14},... | collective-permute-start | bytes 786440 | tf_op jit(solution)/shard_map/ppermute | solution.py:245
  5.1 14.7 %collective-permute-start.5 = (bf16[128,1024]{1,0:T(8,128)(2,1)}, bf16[128,1024]{1,0:T(8,128)(2,1)S(1)}, u32[]{:S(2)}, u32[]{:S(2)}) collective-permute-start(bf16[128,1024]{1,0:T(8,128)(2,1)} %refs_4_.1), channel_id=1, source_target_pairs={{0,1},{1,2},{2,3},{3,0},{4,5},{5,6},{6,7},{7,4},{8,9},{9,10},{10,1... | collective-permute-start | bytes 786440 | tf_op jit(solution)/shard_map/ppermute | solution.py:242
  14.2 7.5 %collective-permute-start.3 = (bf16[128,1024]{1,0:T(8,128)(2,1)S(1)}, bf16[128,1024]{1,0:T(8,128)(2,1)S(1)}, u32[]{:S(2)}, u32[]{:S(2)}) collective-permute-start(bf16[128,1024]{1,0:T(8,128)(2,1)S(1)} %collective-permute-done.refs_1_), channel_id=1, source_target_pairs={{0,8},{4,12},{8,0},{12,4},{1,9},{5,13},{9,1},{13,5},{2,10},{6,14},... | collective-permute-start | bytes 786440 | tf_op jit(solution)/shard_map/ppermute | solution.py:245
  14.5 11.0 %collective-permute-start.2 = (bf16[128,1024]{1,0:T(8,128)(2,1)S(1)}, bf16[128,1024]{1,0:T(8,128)(2,1)S(1)}, u32[]{:S(2)}, u32[]{:S(2)}) collective-permute-start(bf16[128,1024]{1,0:T(8,128)(2,1)S(1)} %collective-permute-done.refs_1_), channel_id=1, source_target_pairs={{0,1},{1,2},{2,3},{3,0},{4,5},{5,6},{6,7},{7,4},{8,9},{9,10},{10,1... | collective-permute-start | bytes 786440 | tf_op jit(solution)/shard_map/ppermute | solution.py:242
  19.8 7.6 %collective-permute-start.8 = (bf16[128,1024]{1,0:T(8,128)(2,1)S(1)}, bf16[128,1024]{1,0:T(8,128)(2,1)S(1)}, u32[]{:S(2)}, u32[]{:S(2)}) collective-permute-start(bf16[128,1024]{1,0:T(8,128)(2,1)S(1)} %collective-permute-done.5.refs_5_), channel_id=1, source_target_pairs={{0,8},{4,12},{8,0},{12,4},{1,9},{5,13},{9,1},{13,5},{2,10},{6,14},... | collective-permute-start | bytes 786440 | tf_op jit(solution)/shard_map/ppermute | solution.py:245
  20.1 9.6 %collective-permute-start.7 = (bf16[128,1024]{1,0:T(8,128)(2,1)S(1)}, bf16[128,1024]{1,0:T(8,128)(2,1)S(1)}, u32[]{:S(2)}, u32[]{:S(2)}) collective-permute-start(bf16[128,1024]{1,0:T(8,128)(2,1)S(1)} %collective-permute-done.5.refs_5_), channel_id=1, source_target_pairs={{0,1},{1,2},{2,3},{3,0},{4,5},{5,6},{6,7},{7,4},{8,9},{9,10},{10,1... | collective-permute-start | bytes 786440 | tf_op jit(solution)/shard_map/ppermute | solution.py:242
  25.5 7.5 %collective-permute-start.10 = (bf16[128,1024]{1,0:T(8,128)(2,1)S(1)}, bf16[128,1024]{1,0:T(8,128)(2,1)S(1)}, u32[]{:S(2)}, u32[]{:S(2)}) collective-permute-start(bf16[128,1024]{1,0:T(8,128)(2,1)S(1)} %collective-permute-done.2.refs_2_), channel_id=1, source_target_pairs={{0,8},{4,12},{8,0},{12,4},{1,9},{5,13},{9,1},{13,5},{2,10},{6,14},... | collective-permute-start | bytes 786440 | tf_op jit(solution)/shard_map/ppermute | solution.py:245
  25.9 28.5 %copy-start.2 = (s32[4]{0:T(128)S(1)}, s32[4]{0:T(128)}, u32[]{:S(2)}) copy-start(s32[4]{0:T(128)} %placement.1) | copy-start | bytes 52
  25.9 28.5 %copy-start.3 = (s32[2]{0:T(128)S(1)}, s32[2]{0:T(128)}, u32[]{:S(2)}) copy-start(s32[2]{0:T(128)} %lengths.1) | copy-start | bytes 28
  25.9 26.0 %collective-permute-start.15 = (bf16[128,4096]{1,0:T(8,128)(2,1)S(1)}, bf16[128,4096]{1,0:T(8,128)(2,1)S(1)}, u32[]{:S(2)}, u32[]{:S(2)}) collective-permute-start(bf16[128,4096]{1,0:T(8,128)(2,1)S(1)} %pad_maximum_fusion), channel_id=1, source_target_pairs={{0,4},{4,0},{8,12},{12,8},{1,5},{5,1},{9,13},{13,9},{2,6},{6,2},{1... | collective-permute-start | bytes 3145736 | tf_op jit(solution)/shard_map/ppermute | solution.py:248
  26.0 16.6 %collective-permute-start.4 = (bf16[128,1024]{1,0:T(8,128)(2,1)S(1)}, bf16[128,1024]{1,0:T(8,128)(2,1)S(1)}, u32[]{:S(2)}, u32[]{:S(2)}) collective-permute-start(bf16[128,1024]{1,0:T(8,128)(2,1)S(1)} %collective-permute-done.2.refs_2_), channel_id=1, source_target_pairs={{0,1},{1,2},{2,3},{3,0},{4,5},{5,6},{6,7},{7,4},{8,9},{9,10},{10,1... | collective-permute-start | bytes 786440 | tf_op jit(solution)/shard_map/ppermute | solution.py:242
  29.7 7.9 %collective-permute-start.12 = (bf16[128,1024]{1,0:T(8,128)(2,1)S(1)}, bf16[128,1024]{1,0:T(8,128)(2,1)S(1)}, u32[]{:S(2)}, u32[]{:S(2)}) collective-permute-start(bf16[128,1024]{1,0:T(8,128)(2,1)S(1)} %collective-permute-done.7.refs_6_), channel_id=1, source_target_pairs={{0,8},{4,12},{8,0},{12,4},{1,9},{5,13},{9,1},{13,5},{2,10},{6,14},... | collective-permute-start | bytes 786440 | tf_op jit(solution)/shard_map/ppermute | solution.py:245
  30.2 12.3 %collective-permute-start.9 = (bf16[128,1024]{1,0:T(8,128)(2,1)S(1)}, bf16[128,1024]{1,0:T(8,128)(2,1)S(1)}, u32[]{:S(2)}, u32[]{:S(2)}) collective-permute-start(bf16[128,1024]{1,0:T(8,128)(2,1)S(1)} %collective-permute-done.7.refs_6_), channel_id=1, source_target_pairs={{0,1},{1,2},{2,3},{3,0},{4,5},{5,6},{6,7},{7,4},{8,9},{9,10},{10,1... | collective-permute-start | bytes 786440 | tf_op jit(solution)/shard_map/ppermute | solution.py:242
  33.0 14.7 %collective-permute-start.11 = (bf16[128,1024]{1,0:T(8,128)(2,1)S(1)}, bf16[128,1024]{1,0:T(8,128)(2,1)S(1)}, u32[]{:S(2)}, u32[]{:S(2)}) collective-permute-start(bf16[128,1024]{1,0:T(8,128)(2,1)S(1)} %collective-permute-done.10.refs_10_), channel_id=1, source_target_pairs={{0,1},{1,2},{2,3},{3,0},{4,5},{5,6},{6,7},{7,4},{8,9},{9,10},{10,1... | collective-permute-start | bytes 786440 | tf_op jit(solution)/shard_map/ppermute | solution.py:242
  37.6 16.3 %collective-permute-start.16 = (bf16[128,4096]{1,0:T(8,128)(2,1)S(1)}, bf16[128,4096]{1,0:T(8,128)(2,1)S(1)}, u32[]{:S(2)}, u32[]{:S(2)}) collective-permute-start(bf16[128,4096]{1,0:T(8,128)(2,1)S(1)} %pad_maximum_fusion.1), channel_id=1, source_target_pairs={{0,4},{4,0},{8,12},{12,8},{1,5},{5,1},{9,13},{13,9},{2,6},{6,2},{1... | collective-permute-start | bytes 3145736 | tf_op jit(solution)/shard_map/ppermute | solution.py:248
  42.5 9.3 %collective-permute-start.14 = (bf16[128,2048]{1,0:T(8,128)(2,1)S(1)}, bf16[128,2048]{1,0:T(8,128)(2,1)S(1)}, u32[]{:S(2)}, u32[]{:S(2)}) collective-permute-start(bf16[128,2048]{1,0:T(8,128)(2,1)S(1)} %pad_maximum_fusion.2), channel_id=1, source_target_pairs={{0,4},{4,0},{8,12},{12,8},{1,5},{5,1},{9,13},{13,9},{2,6},{6,2},{1... | collective-permute-start | bytes 1572872 | tf_op jit(solution)/shard_map/ppermute | solution.py:248
  42.5 8.8 %collective-permute-start.13 = (bf16[128,1024]{1,0:T(8,128)(2,1)S(1)}, bf16[128,1024]{1,0:T(8,128)(2,1)S(1)}, u32[]{:S(2)}, u32[]{:S(2)}) collective-permute-start(bf16[128,1024]{1,0:T(8,128)(2,1)S(1)} %collective-permute-done.9.refs_7_), channel_id=1, source_target_pairs={{0,8},{4,12},{8,0},{12,4},{1,9},{5,13},{9,1},{13,5},{2,10},{6,14},... | collective-permute-start | bytes 786440 | tf_op jit(solution)/shard_map/ppermute | solution.py:245
  47.7 3.6 %collective-permute-start.19 = (bf16[128,1024]{1,0:T(8,128)(2,1)S(1)}, bf16[128,1024]{1,0:T(8,128)(2,1)S(1)}, u32[]{:S(2)}, u32[]{:S(2)}) collective-permute-start(bf16[128,1024]{1,0:T(8,128)(2,1)S(1)} %collective-permute-done.11.refs_11_), channel_id=1, source_target_pairs={{0,4},{4,0},{8,12},{12,8},{1,5},{5,1},{9,13},{13,9},{2,6},{6,2},{1... | collective-permute-start | bytes 786440 | tf_op jit(solution)/shard_map/ppermute | solution.py:248
  51.3 1.9 collective-permute-start.17
  51.3 2.7 %collective-permute-start.18 = (bf16[128,2048]{1,0:T(8,128)(2,1)S(1)}, bf16[128,2048]{1,0:T(8,128)(2,1)S(1)}, u32[]{:S(2)}, u32[]{:S(2)}) collective-permute-start(bf16[128,2048]{1,0:T(8,128)(2,1)S(1)} %pad_maximum_fusion.4), channel_id=1, source_target_pairs={{0,4},{4,0},{8,12},{12,8},{1,5},{5,1},{9,13},{13,9},{2,6},{6,2},{1... | collective-permute-start | bytes 1572872 | tf_op jit(solution)/shard_map/ppermute | solution.py:248
  51.8 2.5 %collective-permute-start.20 = (bf16[128,1024]{1,0:T(8,128)(2,1)S(1)}, bf16[128,1024]{1,0:T(8,128)(2,1)S(1)}, u32[]{:S(2)}, u32[]{:S(2)}) collective-permute-start(bf16[128,1024]{1,0:T(8,128)(2,1)S(1)} %collective-permute-done.13.refs_15_), channel_id=1, source_target_pairs={{0,4},{4,0},{8,12},{12,8},{1,5},{5,1},{9,13},{13,9},{2,6},{6,2},{1... | collective-permute-start | bytes 786440 | tf_op jit(solution)/shard_map/ppermute | solution.py:248

commit v9 on v7

v9 whole, which is shorter than its diff:
```python
import functools
import math

import jax
import jax.numpy as jnp
from jax import lax
from jax.experimental import pallas as pl
from jax.experimental.pallas import tpu as pltpu
from jax.sharding import PartitionSpec as P

HD = 128
CORES = 2
HEADS_PER_TILE = 2
RESIDENT_BYTES = 16 << 20
EXP2_SCALE = math.log2(math.e) / math.sqrt(HD)
LEAST_TOTAL, MOST_TOTAL = 1e-20, 1e30


def matmul_nt(a, b):
    return lax.dot_general(a, b, (((1,), (1,)), ((), ())), preferred_element_type=jnp.float32)


class Place:
    def __init__(self, sizes, placement, lengths):
        self.prompt_count, self.chips, self.ring, self.tokens = sizes
        self.blocks, self.slots = self.chips * CORES, self.prompt_count + 1
        self.index, self.head = lax.axis_index("blk"), lax.axis_index("head")
        self.placement, self.lengths = placement, lengths
        self.block = placement[self.index]

    def source(self, slot):
        found = self.index
        for b in range(self.blocks):
            found = jnp.where(self.placement[b] == slot, b, found)
        found = jnp.where(slot == self.prompt_count, self.index, found)
        back = lax.shift_right_logical(self.index, 1) - lax.shift_right_logical(found, 1)
        return jnp.where(back < 0, back + self.chips, back) * CORES + ((self.index ^ found) & 1)

    def first_key(self, slot):
        own = (self.ring - 1 - self.head) * self.tokens
        return jnp.where(slot == self.prompt_count, own, jnp.where(self.block > slot, 0, self.ring * self.tokens))

    def kept(self):
        keep = jnp.int32(self.ring * self.tokens)
        for response in range(self.prompt_count):
            keep = jnp.where(self.block == self.prompt_count + response, self.lengths[response], keep)
        offsets = self.head * self.tokens + lax.broadcasted_iota(jnp.int32, (self.tokens, 1), 0)
        return offsets < keep


def exact(here, query, key, value, out):
    slots, tokens, rows = here.prompt_count + 1, here.tokens, here.ring * here.tokens
    key_row = lax.broadcasted_iota(jnp.int32, (tokens, rows), 1)
    newest_own = rows - tokens + lax.broadcasted_iota(jnp.int32, (tokens, rows), 0)

    def one_head(head, carry):
        columns = pl.ds(pl.multiple_of(head * HD, HD), HD)
        query_one = query[:, columns]

        def part(ref, slot):
            return ref[pl.ds(pl.multiple_of(slot * rows, rows), rows), :]

        def score(slot):
            newest = jnp.where(slot == here.prompt_count, newest_own, rows)
            seen = (key_row >= here.first_key(slot)) & (key_row <= newest)
            return jnp.where(seen, matmul_nt(query_one, part(key, slot)), -jnp.inf)

        row_max = lax.fori_loop(
            0,
            slots,
            lambda j, best: jnp.maximum(best, jnp.max(score(j), axis=1, keepdims=True)),
            jnp.full((tokens, 1), -jnp.inf, jnp.float32),
        )

        def add(slot, carry):
            total, summed = carry
            weights = jnp.exp2((score(slot) - row_max) * EXP2_SCALE)
            total += jnp.sum(weights, axis=1, keepdims=True)
            weights = weights.astype(jnp.bfloat16)
            return total, summed + jnp.dot(weights, part(value, slot), preferred_element_type=jnp.float32)

        zeros = jnp.zeros((tokens, 1), jnp.float32), jnp.zeros((tokens, HD), jnp.float32)
        total, summed = lax.fori_loop(0, slots, add, zeros)
        out[:, columns] = jnp.where(here.kept(), summed / total, 0.0).astype(out.dtype)
        return carry

    lax.fori_loop(0, query.shape[1] // HD, one_head, 0)


def attend_kernel(sizes, where, resident, placement, lengths, query_all, *refs):
    prompt_count, chips, ring, tokens = sizes
    here = Place(sizes, placement, lengths)
    arrays, refs = refs[:-9], refs[-9:]
    out_all, query_held, out_held, held_key, held_value, ones, bias, sems, fetch_sem = refs
    width = held_key.shape[1]
    kv_heads = width // HD
    span = query_all.shape[1] // kv_heads
    group = span // HD
    masked = bias.shape[1]

    def heads_of(kv_head):
        return pl.ds(pl.multiple_of(kv_head * span, span), span)

    def query_copy(kv_head):
        columns = heads_of(kv_head)
        return pltpu.make_async_copy(query_all.at[:, columns], query_held.at[:, columns], sems.at[0, kv_head])

    def out_copy(kv_head):
        columns = heads_of(kv_head)
        return pltpu.make_async_copy(out_held.at[:, columns], out_all.at[:, columns], sems.at[1, kv_head])

    for kv_head in range(kv_heads):
        query_copy(kv_head).start()

    def take(slot, carry):
        wanted = here.source(slot)
        for hop in range(ring):
            rows = pl.ds(pl.multiple_of((slot * ring + ring - 1 - hop) * tokens, tokens), tokens)
            seen = (ring - 1 - hop) * tokens >= here.first_key(slot)
            count = jnp.where(seen, 1.0, 0.0)
            ones[rows] = jnp.full((tokens, HD), count, jnp.float32).astype(ones.dtype)
            for kind, held in enumerate((held_key, held_value)):

                @pl.when(jnp.logical_not(seen))
                def _():
                    held[rows] = jnp.zeros((tokens, width), held.dtype)

                for source in range(here.blocks):
                    array, column = where[kind, source, hop]

                    @pl.when(seen & (wanted == source))
                    def _():
                        piece = arrays[array].at[:, column : column + width]
                        if resident:
                            held[rows] = piece[...]
                        else:
                            copy = pltpu.make_async_copy(piece, held.at[rows], fetch_sem)
                            copy.start()
                            copy.wait()

        return carry

    lax.fori_loop(0, here.slots, take, 0)
    own = lax.broadcasted_iota(jnp.int32, (tokens, masked), 0)
    key_row = lax.broadcasted_iota(jnp.int32, (tokens, masked), 1) - (masked - tokens)
    bias[...] = jnp.where(key_row <= own, 0.0, -jnp.inf)
    kept = here.kept()

    def of_head(kv_head):
        column = pl.ds(pl.multiple_of(kv_head * HD, HD), HD)
        columns = heads_of(kv_head)
        return query_held.at[:, columns], held_key.at[:, column], held_value.at[:, column], out_held.at[:, columns]

    def one_kv_head(kv_head, carry):
        least, most = carry
        query, key, value, out = of_head(kv_head)
        query_copy(kv_head).wait()
        keys, values = key[...], jnp.concatenate([value[...], ones[...]], axis=1)
        for tile in range(group // HEADS_PER_TILE):
            heads = range(tile * HEADS_PER_TILE, (tile + 1) * HEADS_PER_TILE)
            query_tile = jnp.concatenate([query[:, h * HD : (h + 1) * HD] for h in heads], axis=0)
            scores = matmul_nt(query_tile, keys) * EXP2_SCALE
            split = scores.shape[1] - masked
            tail = scores[:, split:].reshape(HEADS_PER_TILE, tokens, masked) + bias[...][None]
            tail = tail.reshape(HEADS_PER_TILE * tokens, masked)
            scores = tail if split == 0 else jnp.concatenate([scores[:, :split], tail], axis=1)
            weights = jnp.exp2(scores).astype(jnp.bfloat16)
            summed = jnp.dot(weights, values, preferred_element_type=jnp.float32)
            for i, h in enumerate(heads):
                part = summed[i * tokens : (i + 1) * tokens]
                total = part[:, HD:]
                least, most = jnp.minimum(least, total), jnp.maximum(most, total)
                out[:, h * HD : (h + 1) * HD] = jnp.where(kept, part[:, :HD] / total, 0.0).astype(out.dtype)
        out_copy(kv_head).start()
        return least, most

    zeros = jnp.zeros((tokens, HD), jnp.float32)
    least, most = lax.fori_loop(0, kv_heads, one_kv_head, (zeros + jnp.inf, zeros))
    safe = (jnp.min(least) > LEAST_TOTAL) & (jnp.max(most) < MOST_TOTAL)
    for kv_head in range(kv_heads):
        out_copy(kv_head).wait()

    @pl.when(jnp.logical_not(safe))
    def _():
        def again(kv_head, carry):
            query, key, value, out = of_head(kv_head)
            exact(here, query, key, value, out)
            out_copy(kv_head).start()
            out_copy(kv_head).wait()
            return carry

        lax.fori_loop(0, kv_heads, again, 0)


def attend(placement, lengths, query_rows, arrays, where, sizes, kv_heads):
    prompt_count, chips, ring, tokens = sizes
    slots = prompt_count + 1
    width = kv_heads * HD
    keys = slots * ring * tokens
    masked = tokens if tokens % HD == 0 else keys
    work = query_rows.size // HD * keys
    resident = sum(x.size * x.dtype.itemsize for x in arrays) <= RESIDENT_BYTES
    scalar, whole = pl.BlockSpec(memory_space=pltpu.SMEM), pl.BlockSpec(memory_space=pl.ANY)
    piece = pl.BlockSpec(memory_space=pltpu.VMEM) if resident else whole
    return pl.pallas_call(
        functools.partial(attend_kernel, sizes, where, resident),
        in_specs=[scalar, scalar, whole] + [piece] * len(arrays),
        out_specs=whole,
        scratch_shapes=[
            pltpu.VMEM(query_rows.shape, query_rows.dtype),
            pltpu.VMEM(query_rows.shape, query_rows.dtype),
            pltpu.VMEM((keys, width), jnp.bfloat16),
            pltpu.VMEM((keys, width), jnp.bfloat16),
            pltpu.VMEM((keys, HD), jnp.bfloat16),
            pltpu.VMEM((tokens, masked), jnp.float32),
            pltpu.SemaphoreType.DMA((2, kv_heads)),
            pltpu.SemaphoreType.DMA,
        ],
        out_shape=jax.ShapeDtypeStruct(query_rows.shape, query_rows.dtype),
        cost_estimate=pl.CostEstimate(flops=6 * work * HD, bytes_accessed=12 << 20, transcendentals=work),
        compiler_params=pltpu.CompilerParams(vmem_limit_bytes=2 * keys * width * 2 + (14 << 20)),
    )(placement, lengths, pltpu.with_memory_space_constraint(query_rows, pltpu.HBM), *arrays)


def after(x, *others):
    return lax.optimization_barrier((x, *others))[0]


def shards(query_rows, key_rows, value_rows, placement, lengths):
    blocks, ring = lax.axis_size("blk"), lax.axis_size("head")
    chips = blocks // CORES
    sizes = (blocks // 2, chips, ring, query_rows.shape[0])
    width = key_rows.shape[1]
    kv_heads = width // HD

    def next_hop(x):
        return lax.ppermute(x, "head", [(i, (i + 1) % ring) for i in range(ring)])

    def next_chip(x):
        return lax.ppermute(x, "blk", [(i, (i + CORES) % blocks) for i in range(blocks)])

    def other_core(x):
        return lax.ppermute(x, "blk", [(i, i ^ 1) for i in range(blocks)])

    columns, acrosses = [[key_rows], [value_rows]], [[], []]
    for hop in range(ring):
        for c in range(2):
            column, across = columns[c], acrosses[c]
            x = column[hop]
            if hop > 0:
                x = after(x, across[hop - 1])
            if hop < ring - 1:
                column.append(next_hop(x))
            if hop < ring - 1 or c == 1:
                across.append(next_chip(x))
            else:
                across.append(next_hop(after(across[-1], x)))
    planes = [columns, acrosses]
    bundles = [[(0, c, hop) for c in range(2)] + [(1, c, hop - 1) for c in range(2) if hop] for hop in range(ring - 1)]
    bundles += [[(0, c, ring - 1), (1, c, ring - 2)] for c in range(2)] + [[(1, c, ring - 1)] for c in range(2)]
    for back in range(2, chips):
        planes.append([[next_chip(x) for x in part] for part in planes[-1]])
        bundles.append([(back, c, hop) for hop in range(ring) for c in range(2)])
    arrays, where = [], {}
    for back, plane in enumerate(planes):
        for c in range(2):
            for hop in range(ring):
                where[c, back * CORES, hop] = len(arrays), 0
                arrays.append(plane[c][hop])
    for bundle in bundles:
        for place, (back, c, hop) in enumerate(bundle):
            where[c, back * CORES + 1, hop] = len(arrays), place * width
        packed = jnp.concatenate([planes[back][c][hop] for back, c, hop in bundle], axis=1)
        for c in range(2):
            if bundle == bundles[ring - 1 + c]:
                packed = after(packed, planes[1][c][ring - 1])
        if bundle == bundles[ring + 2]:
            packed = after(packed, arrays[-1])
        arrays.append(other_core(packed))
    return attend(placement, lengths, query_rows, arrays, where, sizes, kv_heads)


def solution(mesh):
    rows = P(("grp", "blk", "head"), None)
    return jax.shard_map(
        shards,
        mesh=mesh,
        in_specs=(rows, rows, rows, P("grp"), P("grp")),
        out_specs=rows,
        check_vma=False,
    )
```

time: 208 us -> 203 us (0.976)
  the two profiles are of different devices: /device:TPU:1 before, /device:TPU:0 now
where the time goes in v9:
time: 203 us
  Pallas kernels  149 us (73%)
  waiting for transfers between devices  41 us (20%)
  starting transfers between devices  13 us (6%)
    pallas_call x1, Pallas kernels, attend(): pl.pallas_call(functools.partial(attend_kernel, sizes, where, resident),...  149 us
    ppermute x7, waiting for transfers between devices, next_hop(): return lax.ppermute(x, 'head', [(i, (i + 1) % ring) for i in range(ring)])  22 us
    ppermute x7, waiting for transfers between devices, next_chip(): lax.ppermute(x, 'blk', [(i, (i + CORES) % blocks) for i in range(blocks)])  16.6 us
    ppermute x7, starting transfers between devices, next_chip(): lax.ppermute(x, 'blk', [(i, (i + CORES) % blocks) for i in range(blocks)])  6.68 us
    ppermute x7, starting transfers between devices, next_hop(): return lax.ppermute(x, 'head', [(i, (i + 1) % ring) for i in range(ring)])  5.66 us
  transfers between devices with their start and end apart: 21, of which 16 were waited for; matrix products, arithmetic and copies ran while one was open for 0% of the time, Pallas kernels for 0%

profile of v9, /device:TPU:0, one launch (start us, length us, event | category | flops | bytes accessed | tf_op | source)
XLA Modules:
  0.0 202.9 jit_solution(3085684849413864613)
XLA Ops:
  0.0 2.9 %collective-permute-start.1 = (bf16[128,1024]{1,0:T(8,128)(2,1)}, bf16[128,1024]{1,0:T(8,128)(2,1)S(1)}, u32[]{:S(2)}, u32[]{:S(2)}) collective-permute-start(bf16[128,1024]{1,0:T(8,128)(2,1)} %refs_0_.1), channel_id=1, source_target_pairs={{0,8},{4,12},{8,0},{12,4},{1,9},{5,13},{9,1},{13,5},{2,10},{6,14},... | collective-permute-start | bytes 786440 | tf_op jit(solution)/shard_map/ppermute | solution.py:240
  2.9 1.6 collective-permute-start
  4.5 0.5 collective-permute-start.6
  5.1 1.6 collective-permute-start.5
  6.6 3.7 %collective-permute-done.1.refs_8_ = bf16[128,1024]{1,0:T(8,128)(2,1)S(1)} collective-permute-done((bf16[128,1024]{1,0:T(8,128)(2,1)}, bf16[128,1024]{1,0:T(8,128)(2,1)S(1)}, u32[]{:S(2)}, u32[]{:S(2)}) %collective-permute-start.1) | collective-permute-done | bytes 262176 | tf_op jit(solution)/shard_map/ppermute | solution.py:240
  10.4 3.8 %collective-permute-done.refs_1_ = bf16[128,1024]{1,0:T(8,128)(2,1)S(1)} collective-permute-done((bf16[128,1024]{1,0:T(8,128)(2,1)}, bf16[128,1024]{1,0:T(8,128)(2,1)S(1)}, u32[]{:S(2)}, u32[]{:S(2)}) %collective-permute-start) | collective-permute-done | bytes 262176 | tf_op jit(solution)/shard_map/ppermute | solution.py:237
  14.2 0.3 collective-permute-start.3
  14.5 1.5 collective-permute-done.6.refs_12_
  16.0 3.8 %collective-permute-done.5.refs_5_ = bf16[128,1024]{1,0:T(8,128)(2,1)S(1)} collective-permute-done((bf16[128,1024]{1,0:T(8,128)(2,1)}, bf16[128,1024]{1,0:T(8,128)(2,1)S(1)}, u32[]{:S(2)}, u32[]{:S(2)}) %collective-permute-start.5) | collective-permute-done | bytes 262176 | tf_op jit(solution)/shard_map/ppermute | solution.py:237
  19.8 0.3 collective-permute-start.8
  20.1 1.6 collective-permute-done.3.refs_9_
  21.7 3.9 %collective-permute-done.2.refs_2_ = bf16[128,1024]{1,0:T(8,128)(2,1)S(1)} collective-permute-done((bf16[128,1024]{1,0:T(8,128)(2,1)S(1)}, bf16[128,1024]{1,0:T(8,128)(2,1)S(1)}, u32[]{:S(2)}, u32[]{:S(2)}) %collective-permute-start.2) | collective-permute-done | bytes 262176 | tf_op jit(solution)/shard_map/ppermute | solution.py:237
  25.5 0.2 collective-permute-start.10
  25.8 0.1 pad_maximum_fusion
  25.9 0.1 collective-permute-start.15
  26.0 1.4 collective-permute-done.8.refs_13_
  27.4 2.2 %collective-permute-done.7.refs_6_ = bf16[128,1024]{1,0:T(8,128)(2,1)S(1)} collective-permute-done((bf16[128,1024]{1,0:T(8,128)(2,1)S(1)}, bf16[128,1024]{1,0:T(8,128)(2,1)S(1)}, u32[]{:S(2)}, u32[]{:S(2)}) %collective-permute-start.7) | collective-permute-done | bytes 262176 | tf_op jit(solution)/shard_map/ppermute | solution.py:237
  29.7 0.5 collective-permute-start.12
  30.2 0.6 collective-permute-start.9
  30.8 2.3 %collective-permute-done.10.refs_10_ = bf16[128,1024]{1,0:T(8,128)(2,1)S(1)} collective-permute-done((bf16[128,1024]{1,0:T(8,128)(2,1)S(1)}, bf16[128,1024]{1,0:T(8,128)(2,1)S(1)}, u32[]{:S(2)}, u32[]{:S(2)}) %collective-permute-start.10) | collective-permute-done | bytes 262176 | tf_op jit(solution)/shard_map/ppermute | solution.py:240
  33.0 1.9 collective-permute-start.11
  35.0 2.6 %collective-permute-done.12.refs_14_ = bf16[128,1024]{1,0:T(8,128)(2,1)S(1)} collective-permute-done((bf16[128,1024]{1,0:T(8,128)(2,1)S(1)}, bf16[128,1024]{1,0:T(8,128)(2,1)S(1)}, u32[]{:S(2)}, u32[]{:S(2)}) %collective-permute-start.12) | collective-permute-done | bytes 262176 | tf_op jit(solution)/shard_map/ppermute | solution.py:240
  37.7 4.9 %collective-permute-done.9.refs_7_ = bf16[128,1024]{1,0:T(8,128)(2,1)S(1)} collective-permute-done((bf16[128,1024]{1,0:T(8,128)(2,1)S(1)}, bf16[128,1024]{1,0:T(8,128)(2,1)S(1)}, u32[]{:S(2)}, u32[]{:S(2)}) %collective-permute-start.9) | collective-permute-done | bytes 262176 | tf_op jit(solution)/shard_map/ppermute | solution.py:237
  42.5 1.8 collective-permute-start.13
  44.3 3.4 %collective-permute-done.11.refs_11_ = bf16[128,1024]{1,0:T(8,128)(2,1)S(1)} collective-permute-done((bf16[128,1024]{1,0:T(8,128)(2,1)S(1)}, bf16[128,1024]{1,0:T(8,128)(2,1)S(1)}, u32[]{:S(2)}, u32[]{:S(2)}) %collective-permute-start.11) | collective-permute-done | bytes 262176 | tf_op jit(solution)/shard_map/ppermute | solution.py:237
  47.8 3.5 %collective-permute-done.13.refs_15_ = bf16[128,1024]{1,0:T(8,128)(2,1)S(1)} collective-permute-done((bf16[128,1024]{1,0:T(8,128)(2,1)S(1)}, bf16[128,1024]{1,0:T(8,128)(2,1)S(1)}, u32[]{:S(2)}, u32[]{:S(2)}) %collective-permute-start.13) | collective-permute-done | bytes 262176 | tf_op jit(solution)/shard_map/ppermute | solution.py:240
  51.3 0.5 collective-permute-start.18
  51.8 0.1 collective-permute-start.20
  51.9 1.3 collective-permute-done.17.refs_19_
  53.2 0.7 collective-permute-done.18.refs_20_
  54.0 0.4 collective-permute-done.20.refs_22_
  54.3 148.6 %shard_map.55 = bf16[128,8192]{1,0:T(8,128)(2,1)} custom-call(s32[4]{0:T(128)S(1)} %copy-done.2, s32[2]{0:T(128)S(1)} %copy-done.3, bf16[128,8192]{1,0:T(8,128)(2,1)} %query_all.1, bf16[128,1024]{1,0:T(8,128)(2,1)S(1)} %copy-done, bf16[128,1024]{1,0:T(8,128)(2,1)S(1)} %collective-permute-done.refs_1_, bf16[128,1024]{1,0:T(8,128)(2,1)S(1)} %collective-permute-done.2.refs_2_, ...), custom_call_target="tpu_custom_call" | custom-call | flops 9663676416 | bytes 12582912 | tf_op jit(solution)/shard_map/pallas_call | solution.py:205
  (24 shorter events, 0.3 us)
Async XLA Ops:
  0.0 37.6 %copy-start = (bf16[128,1024]{1,0:T(8,128)(2,1)S(1)}, bf16[128,1024]{1,0:T(8,128)(2,1)}, u32[]{:S(2)}) copy-start(bf16[128,1024]{1,0:T(8,128)(2,1)} %refs_0_.1) | copy-start | bytes 786436
  0.0 37.6 %copy-start.1 = (bf16[128,1024]{1,0:T(8,128)(2,1)S(1)}, bf16[128,1024]{1,0:T(8,128)(2,1)}, u32[]{:S(2)}) copy-start(bf16[128,1024]{1,0:T(8,128)(2,1)} %refs_4_.1) | copy-start | bytes 786436
  0.0 10.3 %collective-permute-start.1 = (bf16[128,1024]{1,0:T(8,128)(2,1)}, bf16[128,1024]{1,0:T(8,128)(2,1)S(1)}, u32[]{:S(2)}, u32[]{:S(2)}) collective-permute-start(bf16[128,1024]{1,0:T(8,128)(2,1)} %refs_0_.1), channel_id=1, source_target_pairs={{0,8},{4,12},{8,0},{12,4},{1,9},{5,13},{9,1},{13,5},{2,10},{6,14},... | collective-permute-start | bytes 786440 | tf_op jit(solution)/shard_map/ppermute | solution.py:240
  2.9 11.2 %collective-permute-start = (bf16[128,1024]{1,0:T(8,128)(2,1)}, bf16[128,1024]{1,0:T(8,128)(2,1)S(1)}, u32[]{:S(2)}, u32[]{:S(2)}) collective-permute-start(bf16[128,1024]{1,0:T(8,128)(2,1)} %refs_0_.1), channel_id=1, source_target_pairs={{0,1},{1,2},{2,3},{3,0},{4,5},{5,6},{6,7},{7,4},{8,9},{9,10},{10,1... | collective-permute-start | bytes 786440 | tf_op jit(solution)/shard_map/ppermute | solution.py:237
  4.5 11.5 %collective-permute-start.6 = (bf16[128,1024]{1,0:T(8,128)(2,1)}, bf16[128,1024]{1,0:T(8,128)(2,1)S(1)}, u32[]{:S(2)}, u32[]{:S(2)}) collective-permute-start(bf16[128,1024]{1,0:T(8,128)(2,1)} %refs_4_.1), channel_id=1, source_target_pairs={{0,8},{4,12},{8,0},{12,4},{1,9},{5,13},{9,1},{13,5},{2,10},{6,14},... | collective-permute-start | bytes 786440 | tf_op jit(solution)/shard_map/ppermute | solution.py:240
  5.1 14.7 %collective-permute-start.5 = (bf16[128,1024]{1,0:T(8,128)(2,1)}, bf16[128,1024]{1,0:T(8,128)(2,1)S(1)}, u32[]{:S(2)}, u32[]{:S(2)}) collective-permute-start(bf16[128,1024]{1,0:T(8,128)(2,1)} %refs_4_.1), channel_id=1, source_target_pairs={{0,1},{1,2},{2,3},{3,0},{4,5},{5,6},{6,7},{7,4},{8,9},{9,10},{10,1... | collective-permute-start | bytes 786440 | tf_op jit(solution)/shard_map/ppermute | solution.py:237
  14.2 7.5 %collective-permute-start.3 = (bf16[128,1024]{1,0:T(8,128)(2,1)S(1)}, bf16[128,1024]{1,0:T(8,128)(2,1)S(1)}, u32[]{:S(2)}, u32[]{:S(2)}) collective-permute-start(bf16[128,1024]{1,0:T(8,128)(2,1)S(1)} %collective-permute-done.refs_1_), channel_id=1, source_target_pairs={{0,8},{4,12},{8,0},{12,4},{1,9},{5,13},{9,1},{13,5},{2,10},{6,14},... | collective-permute-start | bytes 786440 | tf_op jit(solution)/shard_map/ppermute | solution.py:240
  14.5 11.0 %collective-permute-start.2 = (bf16[128,1024]{1,0:T(8,128)(2,1)S(1)}, bf16[128,1024]{1,0:T(8,128)(2,1)S(1)}, u32[]{:S(2)}, u32[]{:S(2)}) collective-permute-start(bf16[128,1024]{1,0:T(8,128)(2,1)S(1)} %collective-permute-done.refs_1_), channel_id=1, source_target_pairs={{0,1},{1,2},{2,3},{3,0},{4,5},{5,6},{6,7},{7,4},{8,9},{9,10},{10,1... | collective-permute-start | bytes 786440 | tf_op jit(solution)/shard_map/ppermute | solution.py:237
  19.8 7.6 %collective-permute-start.8 = (bf16[128,1024]{1,0:T(8,128)(2,1)S(1)}, bf16[128,1024]{1,0:T(8,128)(2,1)S(1)}, u32[]{:S(2)}, u32[]{:S(2)}) collective-permute-start(bf16[128,1024]{1,0:T(8,128)(2,1)S(1)} %collective-permute-done.5.refs_5_), channel_id=1, source_target_pairs={{0,8},{4,12},{8,0},{12,4},{1,9},{5,13},{9,1},{13,5},{2,10},{6,14},... | collective-permute-start | bytes 786440 | tf_op jit(solution)/shard_map/ppermute | solution.py:240
  20.1 9.6 %collective-permute-start.7 = (bf16[128,1024]{1,0:T(8,128)(2,1)S(1)}, bf16[128,1024]{1,0:T(8,128)(2,1)S(1)}, u32[]{:S(2)}, u32[]{:S(2)}) collective-permute-start(bf16[128,1024]{1,0:T(8,128)(2,1)S(1)} %collective-permute-done.5.refs_5_), channel_id=1, source_target_pairs={{0,1},{1,2},{2,3},{3,0},{4,5},{5,6},{6,7},{7,4},{8,9},{9,10},{10,1... | collective-permute-start | bytes 786440 | tf_op jit(solution)/shard_map/ppermute | solution.py:237
  25.5 7.5 %collective-permute-start.10 = (bf16[128,1024]{1,0:T(8,128)(2,1)S(1)}, bf16[128,1024]{1,0:T(8,128)(2,1)S(1)}, u32[]{:S(2)}, u32[]{:S(2)}) collective-permute-start(bf16[128,1024]{1,0:T(8,128)(2,1)S(1)} %collective-permute-done.2.refs_2_), channel_id=1, source_target_pairs={{0,8},{4,12},{8,0},{12,4},{1,9},{5,13},{9,1},{13,5},{2,10},{6,14},... | collective-permute-start | bytes 786440 | tf_op jit(solution)/shard_map/ppermute | solution.py:240
  25.9 28.5 %copy-start.2 = (s32[4]{0:T(128)S(1)}, s32[4]{0:T(128)}, u32[]{:S(2)}) copy-start(s32[4]{0:T(128)} %placement.1) | copy-start | bytes 52
  25.9 28.5 %copy-start.3 = (s32[2]{0:T(128)S(1)}, s32[2]{0:T(128)}, u32[]{:S(2)}) copy-start(s32[2]{0:T(128)} %lengths.1) | copy-start | bytes 28
  25.9 26.0 %collective-permute-start.15 = (bf16[128,4096]{1,0:T(8,128)(2,1)S(1)}, bf16[128,4096]{1,0:T(8,128)(2,1)S(1)}, u32[]{:S(2)}, u32[]{:S(2)}) collective-permute-start(bf16[128,4096]{1,0:T(8,128)(2,1)S(1)} %pad_maximum_fusion), channel_id=1, source_target_pairs={{0,4},{4,0},{8,12},{12,8},{1,5},{5,1},{9,13},{13,9},{2,6},{6,2},{1... | collective-permute-start | bytes 3145736 | tf_op jit(solution)/shard_map/ppermute | solution.py:243
  26.0 16.6 %collective-permute-start.4 = (bf16[128,1024]{1,0:T(8,128)(2,1)S(1)}, bf16[128,1024]{1,0:T(8,128)(2,1)S(1)}, u32[]{:S(2)}, u32[]{:S(2)}) collective-permute-start(bf16[128,1024]{1,0:T(8,128)(2,1)S(1)} %collective-permute-done.2.refs_2_), channel_id=1, source_target_pairs={{0,1},{1,2},{2,3},{3,0},{4,5},{5,6},{6,7},{7,4},{8,9},{9,10},{10,1... | collective-permute-start | bytes 786440 | tf_op jit(solution)/shard_map/ppermute | solution.py:237
  29.7 7.9 %collective-permute-start.12 = (bf16[128,1024]{1,0:T(8,128)(2,1)S(1)}, bf16[128,1024]{1,0:T(8,128)(2,1)S(1)}, u32[]{:S(2)}, u32[]{:S(2)}) collective-permute-start(bf16[128,1024]{1,0:T(8,128)(2,1)S(1)} %collective-permute-done.7.refs_6_), channel_id=1, source_target_pairs={{0,8},{4,12},{8,0},{12,4},{1,9},{5,13},{9,1},{13,5},{2,10},{6,14},... | collective-permute-start | bytes 786440 | tf_op jit(solution)/shard_map/ppermute | solution.py:240
  30.2 12.3 %collective-permute-start.9 = (bf16[128,1024]{1,0:T(8,128)(2,1)S(1)}, bf16[128,1024]{1,0:T(8,128)(2,1)S(1)}, u32[]{:S(2)}, u32[]{:S(2)}) collective-permute-start(bf16[128,1024]{1,0:T(8,128)(2,1)S(1)} %collective-permute-done.7.refs_6_), channel_id=1, source_target_pairs={{0,1},{1,2},{2,3},{3,0},{4,5},{5,6},{6,7},{7,4},{8,9},{9,10},{10,1... | collective-permute-start | bytes 786440 | tf_op jit(solution)/shard_map/ppermute | solution.py:237
  33.0 14.7 %collective-permute-start.11 = (bf16[128,1024]{1,0:T(8,128)(2,1)S(1)}, bf16[128,1024]{1,0:T(8,128)(2,1)S(1)}, u32[]{:S(2)}, u32[]{:S(2)}) collective-permute-start(bf16[128,1024]{1,0:T(8,128)(2,1)S(1)} %collective-permute-done.10.refs_10_), channel_id=1, source_target_pairs={{0,1},{1,2},{2,3},{3,0},{4,5},{5,6},{6,7},{7,4},{8,9},{9,10},{10,1... | collective-permute-start | bytes 786440 | tf_op jit(solution)/shard_map/ppermute | solution.py:237
  37.6 16.3 %collective-permute-start.16 = (bf16[128,4096]{1,0:T(8,128)(2,1)S(1)}, bf16[128,4096]{1,0:T(8,128)(2,1)S(1)}, u32[]{:S(2)}, u32[]{:S(2)}) collective-permute-start(bf16[128,4096]{1,0:T(8,128)(2,1)S(1)} %pad_maximum_fusion.1), channel_id=1, source_target_pairs={{0,4},{4,0},{8,12},{12,8},{1,5},{5,1},{9,13},{13,9},{2,6},{6,2},{1... | collective-permute-start | bytes 3145736 | tf_op jit(solution)/shard_map/ppermute | solution.py:243
  42.5 9.3 %collective-permute-start.14 = (bf16[128,2048]{1,0:T(8,128)(2,1)S(1)}, bf16[128,2048]{1,0:T(8,128)(2,1)S(1)}, u32[]{:S(2)}, u32[]{:S(2)}) collective-permute-start(bf16[128,2048]{1,0:T(8,128)(2,1)S(1)} %pad_maximum_fusion.2), channel_id=1, source_target_pairs={{0,4},{4,0},{8,12},{12,8},{1,5},{5,1},{9,13},{13,9},{2,6},{6,2},{1... | collective-permute-start | bytes 1572872 | tf_op jit(solution)/shard_map/ppermute | solution.py:243
  42.5 8.8 %collective-permute-start.13 = (bf16[128,1024]{1,0:T(8,128)(2,1)S(1)}, bf16[128,1024]{1,0:T(8,128)(2,1)S(1)}, u32[]{:S(2)}, u32[]{:S(2)}) collective-permute-start(bf16[128,1024]{1,0:T(8,128)(2,1)S(1)} %collective-permute-done.9.refs_7_), channel_id=1, source_target_pairs={{0,8},{4,12},{8,0},{12,4},{1,9},{5,13},{9,1},{13,5},{2,10},{6,14},... | collective-permute-start | bytes 786440 | tf_op jit(solution)/shard_map/ppermute | solution.py:240
  47.7 3.6 %collective-permute-start.19 = (bf16[128,1024]{1,0:T(8,128)(2,1)S(1)}, bf16[128,1024]{1,0:T(8,128)(2,1)S(1)}, u32[]{:S(2)}, u32[]{:S(2)}) collective-permute-start(bf16[128,1024]{1,0:T(8,128)(2,1)S(1)} %collective-permute-done.11.refs_11_), channel_id=1, source_target_pairs={{0,4},{4,0},{8,12},{12,8},{1,5},{5,1},{9,13},{13,9},{2,6},{6,2},{1... | collective-permute-start | bytes 786440 | tf_op jit(solution)/shard_map/ppermute | solution.py:243
  51.3 1.9 collective-permute-start.17
  51.3 2.7 %collective-permute-start.18 = (bf16[128,2048]{1,0:T(8,128)(2,1)S(1)}, bf16[128,2048]{1,0:T(8,128)(2,1)S(1)}, u32[]{:S(2)}, u32[]{:S(2)}) collective-permute-start(bf16[128,2048]{1,0:T(8,128)(2,1)S(1)} %pad_maximum_fusion.4), channel_id=1, source_target_pairs={{0,4},{4,0},{8,12},{12,8},{1,5},{5,1},{9,13},{13,9},{2,6},{6,2},{1... | collective-permute-start | bytes 1572872 | tf_op jit(solution)/shard_map/ppermute | solution.py:243
  51.8 2.5 %collective-permute-start.20 = (bf16[128,1024]{1,0:T(8,128)(2,1)S(1)}, bf16[128,1024]{1,0:T(8,128)(2,1)S(1)}, u32[]{:S(2)}, u32[]{:S(2)}) collective-permute-start(bf16[128,1024]{1,0:T(8,128)(2,1)S(1)} %collective-permute-done.13.refs_15_), channel_id=1, source_target_pairs={{0,4},{4,0},{8,12},{12,8},{1,5},{5,1},{9,13},{13,9},{2,6},{6,2},{1... | collective-permute-start | bytes 786440 | tf_op jit(solution)/shard_map/ppermute | solution.py:243

commit v10 on v9

--- a/solution.py
+++ b/solution.py
@@ -244,17 +244,11 @@
 
     columns, acrosses = [[key_rows], [value_rows]], [[], []]
     for hop in range(ring):
-        for c in range(2):
-            column, across = columns[c], acrosses[c]
-            x = column[hop]
-            if hop > 0:
-                x = after(x, across[hop - 1])
+        for column, across in zip(columns, acrosses):
+            x = after(column[hop], across[hop - 1]) if hop else column[hop]
+            across.append(next_chip(x))
             if hop < ring - 1:
                 column.append(next_hop(x))
-            if hop < ring - 1 or c == 1:
-                across.append(next_chip(x))
-            else:
-                across.append(next_hop(after(across[-1], x)))
     planes = [columns, acrosses]
     bundles = [[(0, c, hop) for c in range(2)] + [(1, c, hop - 1) for c in range(2) if hop] for hop in range(ring - 1)]
     bundles += [[(0, c, ring - 1), (1, c, ring - 2)] for c in range(2)] + [[(1, c, ring - 1)] for c in range(2)]

time: 203 us -> 201 us (level)
  starting transfers between devices: 13 us -> 9.53 us
    ppermute x7 -> x6, starting transfers between devices: 5.66 us -> 3.16 us  [next_hop(): return lax.ppermute(x, 'head', [(i, (i + 1) % ring) for i in range(ring)])]
    ppermute x7 -> x8, waiting for transfers between devices: 16.6 us -> 18.4 us  [next_chip(): lax.ppermute(x, 'blk', [(i, (i + CORES) % blocks) for i in range(blocks)])]
    ppermute x7 -> x8, starting transfers between devices: 6.68 us -> 5.63 us  [next_chip(): lax.ppermute(x, 'blk', [(i, (i + CORES) % blocks) for i in range(blocks)])]
    ppermute x7 -> x6, waiting for transfers between devices: 22 us -> 21.2 us  [next_hop(): return lax.ppermute(x, 'head', [(i, (i + 1) % ring) for i in range(ring)])]
  transfers between devices with their start and end apart: 21 -> 21, of which waited for: 16 -> 17; matrix products, arithmetic and copies ran while one was open for 0% -> 0% of each run, Pallas kernels for 0% -> 0%
where the time goes in v10:
time: 201 us; the launch traced here: 200 us
  Pallas kernels  149 us (74%)
  waiting for transfers between devices  42 us (21%)
  starting transfers between devices  9.53 us (5%)
    pallas_call x1, Pallas kernels, attend(): pl.pallas_call(functools.partial(attend_kernel, sizes, where, resident),...  149 us
    ppermute x6, waiting for transfers between devices, next_hop(): return lax.ppermute(x, 'head', [(i, (i + 1) % ring) for i in range(ring)])  21.2 us
    ppermute x8, waiting for transfers between devices, next_chip(): lax.ppermute(x, 'blk', [(i, (i + CORES) % blocks) for i in range(blocks)])  18.4 us
    ppermute x8, starting transfers between devices, next_chip(): lax.ppermute(x, 'blk', [(i, (i + CORES) % blocks) for i in range(blocks)])  5.63 us
  transfers between devices with their start and end apart: 21, of which 17 were waited for; matrix products, arithmetic and copies ran while one was open for 0% of the time, Pallas kernels for 0%

profile of v10, /device:TPU:0, one launch (start us, length us, event | category | flops | bytes accessed | tf_op | source)
XLA Modules:
  0.0 200.4 jit_solution(1942687617850868044)
XLA Ops:
  0.0 2.9 %collective-permute-start.1 = (bf16[128,1024]{1,0:T(8,128)(2,1)}, bf16[128,1024]{1,0:T(8,128)(2,1)S(1)}, u32[]{:S(2)}, u32[]{:S(2)}) collective-permute-start(bf16[128,1024]{1,0:T(8,128)(2,1)} %refs_0_.1), channel_id=1, source_target_pairs={{0,8},{4,12},{8,0},{12,4},{1,9},{5,13},{9,1},{13,5},{2,10},{6,14},... | collective-permute-start | bytes 786440 | tf_op jit(solution)/shard_map/ppermute | solution.py:240
  2.9 1.6 collective-permute-start
  4.5 0.5 collective-permute-start.6
  5.1 1.6 collective-permute-start.5
  6.6 3.7 %collective-permute-done.1.refs_8_ = bf16[128,1024]{1,0:T(8,128)(2,1)S(1)} collective-permute-done((bf16[128,1024]{1,0:T(8,128)(2,1)}, bf16[128,1024]{1,0:T(8,128)(2,1)S(1)}, u32[]{:S(2)}, u32[]{:S(2)}) %collective-permute-start.1) | collective-permute-done | bytes 262176 | tf_op jit(solution)/shard_map/ppermute | solution.py:240
  10.4 3.8 %collective-permute-done.refs_1_ = bf16[128,1024]{1,0:T(8,128)(2,1)S(1)} collective-permute-done((bf16[128,1024]{1,0:T(8,128)(2,1)}, bf16[128,1024]{1,0:T(8,128)(2,1)S(1)}, u32[]{:S(2)}, u32[]{:S(2)}) %collective-permute-start) | collective-permute-done | bytes 262176 | tf_op jit(solution)/shard_map/ppermute | solution.py:237
  14.2 0.3 collective-permute-start.3
  14.5 1.5 collective-permute-done.6.refs_12_
  16.0 3.8 %collective-permute-done.5.refs_5_ = bf16[128,1024]{1,0:T(8,128)(2,1)S(1)} collective-permute-done((bf16[128,1024]{1,0:T(8,128)(2,1)}, bf16[128,1024]{1,0:T(8,128)(2,1)S(1)}, u32[]{:S(2)}, u32[]{:S(2)}) %collective-permute-start.5) | collective-permute-done | bytes 262176 | tf_op jit(solution)/shard_map/ppermute | solution.py:237
  19.8 0.3 collective-permute-start.8
  20.1 1.6 collective-permute-done.3.refs_9_
  21.7 3.9 %collective-permute-done.2.refs_2_ = bf16[128,1024]{1,0:T(8,128)(2,1)S(1)} collective-permute-done((bf16[128,1024]{1,0:T(8,128)(2,1)S(1)}, bf16[128,1024]{1,0:T(8,128)(2,1)S(1)}, u32[]{:S(2)}, u32[]{:S(2)}) %collective-permute-start.2) | collective-permute-done | bytes 262176 | tf_op jit(solution)/shard_map/ppermute | solution.py:237
  25.5 0.2 collective-permute-start.10
  25.9 0.1 collective-permute-start.15
  26.0 1.5 collective-permute-done.8.refs_13_
  27.4 3.7 %collective-permute-done.7.refs_6_ = bf16[128,1024]{1,0:T(8,128)(2,1)S(1)} collective-permute-done((bf16[128,1024]{1,0:T(8,128)(2,1)S(1)}, bf16[128,1024]{1,0:T(8,128)(2,1)S(1)}, u32[]{:S(2)}, u32[]{:S(2)}) %collective-permute-start.7) | collective-permute-done | bytes 262176 | tf_op jit(solution)/shard_map/ppermute | solution.py:237
  31.2 0.4 collective-permute-start.12
  31.5 1.5 collective-permute-done.10.refs_10_
  33.0 3.7 %collective-permute-done.4.refs_3_ = bf16[128,1024]{1,0:T(8,128)(2,1)S(1)} collective-permute-done((bf16[128,1024]{1,0:T(8,128)(2,1)S(1)}, bf16[128,1024]{1,0:T(8,128)(2,1)S(1)}, u32[]{:S(2)}, u32[]{:S(2)}) %collective-permute-start.4) | collective-permute-done | bytes 262176 | tf_op jit(solution)/shard_map/ppermute | solution.py:237
  36.8 0.4 collective-permute-start.11
  37.2 0.1 collective-permute-start.16
  37.4 1.3 collective-permute-done.12.refs_14_
  38.7 2.2 %collective-permute-done.9.refs_7_ = bf16[128,1024]{1,0:T(8,128)(2,1)S(1)} collective-permute-done((bf16[128,1024]{1,0:T(8,128)(2,1)S(1)}, bf16[128,1024]{1,0:T(8,128)(2,1)S(1)}, u32[]{:S(2)}, u32[]{:S(2)}) %collective-permute-start.9) | collective-permute-done | bytes 262176 | tf_op jit(solution)/shard_map/ppermute | solution.py:237
  40.9 0.5 collective-permute-start.13
  41.4 2.8 %collective-permute-done.11.refs_11_ = bf16[128,1024]{1,0:T(8,128)(2,1)S(1)} collective-permute-done((bf16[128,1024]{1,0:T(8,128)(2,1)S(1)}, bf16[128,1024]{1,0:T(8,128)(2,1)S(1)}, u32[]{:S(2)}, u32[]{:S(2)}) %collective-permute-start.11) | collective-permute-done | bytes 262176 | tf_op jit(solution)/shard_map/ppermute | solution.py:240
  44.4 4.5 %collective-permute-done.13.refs_15_ = bf16[128,1024]{1,0:T(8,128)(2,1)S(1)} collective-permute-done((bf16[128,1024]{1,0:T(8,128)(2,1)S(1)}, bf16[128,1024]{1,0:T(8,128)(2,1)S(1)}, u32[]{:S(2)}, u32[]{:S(2)}) %collective-permute-start.13) | collective-permute-done | bytes 262176 | tf_op jit(solution)/shard_map/ppermute | solution.py:240
  48.9 0.5 collective-permute-start.18
  49.4 0.1 collective-permute-start.20
  49.4 1.3 collective-permute-done.17.refs_19_
  50.8 0.7 collective-permute-done.18.refs_20_
  51.5 0.4 collective-permute-done.20.refs_22_
  51.9 148.5 %shard_map.55 = bf16[128,8192]{1,0:T(8,128)(2,1)} custom-call(s32[4]{0:T(128)S(1)} %copy-done.2, s32[2]{0:T(128)S(1)} %copy-done.3, bf16[128,8192]{1,0:T(8,128)(2,1)} %query_all.1, bf16[128,1024]{1,0:T(8,128)(2,1)S(1)} %copy-done, bf16[128,1024]{1,0:T(8,128)(2,1)S(1)} %collective-permute-done.refs_1_, bf16[128,1024]{1,0:T(8,128)(2,1)S(1)} %collective-permute-done.2.refs_2_, ...), custom_call_target="tpu_custom_call" | custom-call | flops 9663676416 | bytes 12582912 | tf_op jit(solution)/shard_map/pallas_call | solution.py:205
  (24 shorter events, 0.3 us)
Async XLA Ops:
  0.0 37.3 %copy-start = (bf16[128,1024]{1,0:T(8,128)(2,1)S(1)}, bf16[128,1024]{1,0:T(8,128)(2,1)}, u32[]{:S(2)}) copy-start(bf16[128,1024]{1,0:T(8,128)(2,1)} %refs_0_.1) | copy-start | bytes 786436
  0.0 37.3 %copy-start.1 = (bf16[128,1024]{1,0:T(8,128)(2,1)S(1)}, bf16[128,1024]{1,0:T(8,128)(2,1)}, u32[]{:S(2)}) copy-start(bf16[128,1024]{1,0:T(8,128)(2,1)} %refs_4_.1) | copy-start | bytes 786436
  0.0 10.3 %collective-permute-start.1 = (bf16[128,1024]{1,0:T(8,128)(2,1)}, bf16[128,1024]{1,0:T(8,128)(2,1)S(1)}, u32[]{:S(2)}, u32[]{:S(2)}) collective-permute-start(bf16[128,1024]{1,0:T(8,128)(2,1)} %refs_0_.1), channel_id=1, source_target_pairs={{0,8},{4,12},{8,0},{12,4},{1,9},{5,13},{9,1},{13,5},{2,10},{6,14},... | collective-permute-start | bytes 786440 | tf_op jit(solution)/shard_map/ppermute | solution.py:240
  2.9 11.2 %collective-permute-start = (bf16[128,1024]{1,0:T(8,128)(2,1)}, bf16[128,1024]{1,0:T(8,128)(2,1)S(1)}, u32[]{:S(2)}, u32[]{:S(2)}) collective-permute-start(bf16[128,1024]{1,0:T(8,128)(2,1)} %refs_0_.1), channel_id=1, source_target_pairs={{0,1},{1,2},{2,3},{3,0},{4,5},{5,6},{6,7},{7,4},{8,9},{9,10},{10,1... | collective-permute-start | bytes 786440 | tf_op jit(solution)/shard_map/ppermute | solution.py:237
  4.5 11.5 %collective-permute-start.6 = (bf16[128,1024]{1,0:T(8,128)(2,1)}, bf16[128,1024]{1,0:T(8,128)(2,1)S(1)}, u32[]{:S(2)}, u32[]{:S(2)}) collective-permute-start(bf16[128,1024]{1,0:T(8,128)(2,1)} %refs_4_.1), channel_id=1, source_target_pairs={{0,8},{4,12},{8,0},{12,4},{1,9},{5,13},{9,1},{13,5},{2,10},{6,14},... | collective-permute-start | bytes 786440 | tf_op jit(solution)/shard_map/ppermute | solution.py:240
  5.1 14.7 %collective-permute-start.5 = (bf16[128,1024]{1,0:T(8,128)(2,1)}, bf16[128,1024]{1,0:T(8,128)(2,1)S(1)}, u32[]{:S(2)}, u32[]{:S(2)}) collective-permute-start(bf16[128,1024]{1,0:T(8,128)(2,1)} %refs_4_.1), channel_id=1, source_target_pairs={{0,1},{1,2},{2,3},{3,0},{4,5},{5,6},{6,7},{7,4},{8,9},{9,10},{10,1... | collective-permute-start | bytes 786440 | tf_op jit(solution)/shard_map/ppermute | solution.py:237
  14.2 7.5 %collective-permute-start.3 = (bf16[128,1024]{1,0:T(8,128)(2,1)S(1)}, bf16[128,1024]{1,0:T(8,128)(2,1)S(1)}, u32[]{:S(2)}, u32[]{:S(2)}) collective-permute-start(bf16[128,1024]{1,0:T(8,128)(2,1)S(1)} %collective-permute-done.refs_1_), channel_id=1, source_target_pairs={{0,8},{4,12},{8,0},{12,4},{1,9},{5,13},{9,1},{13,5},{2,10},{6,14},... | collective-permute-start | bytes 786440 | tf_op jit(solution)/shard_map/ppermute | solution.py:240
  14.5 11.0 %collective-permute-start.2 = (bf16[128,1024]{1,0:T(8,128)(2,1)S(1)}, bf16[128,1024]{1,0:T(8,128)(2,1)S(1)}, u32[]{:S(2)}, u32[]{:S(2)}) collective-permute-start(bf16[128,1024]{1,0:T(8,128)(2,1)S(1)} %collective-permute-done.refs_1_), channel_id=1, source_target_pairs={{0,1},{1,2},{2,3},{3,0},{4,5},{5,6},{6,7},{7,4},{8,9},{9,10},{10,1... | collective-permute-start | bytes 786440 | tf_op jit(solution)/shard_map/ppermute | solution.py:237
  19.8 7.6 %collective-permute-start.8 = (bf16[128,1024]{1,0:T(8,128)(2,1)S(1)}, bf16[128,1024]{1,0:T(8,128)(2,1)S(1)}, u32[]{:S(2)}, u32[]{:S(2)}) collective-permute-start(bf16[128,1024]{1,0:T(8,128)(2,1)S(1)} %collective-permute-done.5.refs_5_), channel_id=1, source_target_pairs={{0,8},{4,12},{8,0},{12,4},{1,9},{5,13},{9,1},{13,5},{2,10},{6,14},... | collective-permute-start | bytes 786440 | tf_op jit(solution)/shard_map/ppermute | solution.py:240
  20.1 11.0 %collective-permute-start.7 = (bf16[128,1024]{1,0:T(8,128)(2,1)S(1)}, bf16[128,1024]{1,0:T(8,128)(2,1)S(1)}, u32[]{:S(2)}, u32[]{:S(2)}) collective-permute-start(bf16[128,1024]{1,0:T(8,128)(2,1)S(1)} %collective-permute-done.5.refs_5_), channel_id=1, source_target_pairs={{0,1},{1,2},{2,3},{3,0},{4,5},{5,6},{6,7},{7,4},{8,9},{9,10},{10,1... | collective-permute-start | bytes 786440 | tf_op jit(solution)/shard_map/ppermute | solution.py:237
  25.5 7.5 %collective-permute-start.10 = (bf16[128,1024]{1,0:T(8,128)(2,1)S(1)}, bf16[128,1024]{1,0:T(8,128)(2,1)S(1)}, u32[]{:S(2)}, u32[]{:S(2)}) collective-permute-start(bf16[128,1024]{1,0:T(8,128)(2,1)S(1)} %collective-permute-done.2.refs_2_), channel_id=1, source_target_pairs={{0,8},{4,12},{8,0},{12,4},{1,9},{5,13},{9,1},{13,5},{2,10},{6,14},... | collective-permute-start | bytes 786440 | tf_op jit(solution)/shard_map/ppermute | solution.py:240
  25.8 11.0 %collective-permute-start.4 = (bf16[128,1024]{1,0:T(8,128)(2,1)S(1)}, bf16[128,1024]{1,0:T(8,128)(2,1)S(1)}, u32[]{:S(2)}, u32[]{:S(2)}) collective-permute-start(bf16[128,1024]{1,0:T(8,128)(2,1)S(1)} %collective-permute-done.2.refs_2_), channel_id=1, source_target_pairs={{0,1},{1,2},{2,3},{3,0},{4,5},{5,6},{6,7},{7,4},{8,9},{9,10},{10,1... | collective-permute-start | bytes 786440 | tf_op jit(solution)/shard_map/ppermute | solution.py:237
  25.9 26.0 %copy-start.2 = (s32[4]{0:T(128)S(1)}, s32[4]{0:T(128)}, u32[]{:S(2)}) copy-start(s32[4]{0:T(128)} %placement.1) | copy-start | bytes 52
  25.9 26.0 %copy-start.3 = (s32[2]{0:T(128)S(1)}, s32[2]{0:T(128)}, u32[]{:S(2)}) copy-start(s32[2]{0:T(128)} %lengths.1) | copy-start | bytes 28
  25.9 23.6 %collective-permute-start.15 = (bf16[128,4096]{1,0:T(8,128)(2,1)S(1)}, bf16[128,4096]{1,0:T(8,128)(2,1)S(1)}, u32[]{:S(2)}, u32[]{:S(2)}) collective-permute-start(bf16[128,4096]{1,0:T(8,128)(2,1)S(1)} %pad_maximum_fusion), channel_id=1, source_target_pairs={{0,4},{4,0},{8,12},{12,8},{1,5},{5,1},{9,13},{13,9},{2,6},{6,2},{1... | collective-permute-start | bytes 3145736 | tf_op jit(solution)/shard_map/ppermute | solution.py:243
  31.2 7.5 %collective-permute-start.12 = (bf16[128,1024]{1,0:T(8,128)(2,1)S(1)}, bf16[128,1024]{1,0:T(8,128)(2,1)S(1)}, u32[]{:S(2)}, u32[]{:S(2)}) collective-permute-start(bf16[128,1024]{1,0:T(8,128)(2,1)S(1)} %collective-permute-done.7.refs_6_), channel_id=1, source_target_pairs={{0,8},{4,12},{8,0},{12,4},{1,9},{5,13},{9,1},{13,5},{2,10},{6,14},... | collective-permute-start | bytes 786440 | tf_op jit(solution)/shard_map/ppermute | solution.py:240
  31.5 9.4 %collective-permute-start.9 = (bf16[128,1024]{1,0:T(8,128)(2,1)S(1)}, bf16[128,1024]{1,0:T(8,128)(2,1)S(1)}, u32[]{:S(2)}, u32[]{:S(2)}) collective-permute-start(bf16[128,1024]{1,0:T(8,128)(2,1)S(1)} %collective-permute-done.7.refs_6_), channel_id=1, source_target_pairs={{0,1},{1,2},{2,3},{3,0},{4,5},{5,6},{6,7},{7,4},{8,9},{9,10},{10,1... | collective-permute-start | bytes 786440 | tf_op jit(solution)/shard_map/ppermute | solution.py:237
  36.8 7.5 %collective-permute-start.11 = (bf16[128,1024]{1,0:T(8,128)(2,1)S(1)}, bf16[128,1024]{1,0:T(8,128)(2,1)S(1)}, u32[]{:S(2)}, u32[]{:S(2)}) collective-permute-start(bf16[128,1024]{1,0:T(8,128)(2,1)S(1)} %collective-permute-done.4.refs_3_), channel_id=1, source_target_pairs={{0,8},{4,12},{8,0},{12,4},{1,9},{5,13},{9,1},{13,5},{2,10},{6,14},... | collective-permute-start | bytes 786440 | tf_op jit(solution)/shard_map/ppermute | solution.py:240
  37.2 14.3 %collective-permute-start.16 = (bf16[128,4096]{1,0:T(8,128)(2,1)S(1)}, bf16[128,4096]{1,0:T(8,128)(2,1)S(1)}, u32[]{:S(2)}, u32[]{:S(2)}) collective-permute-start(bf16[128,4096]{1,0:T(8,128)(2,1)S(1)} %pad_maximum_fusion.1), channel_id=1, source_target_pairs={{0,4},{4,0},{8,12},{12,8},{1,5},{5,1},{9,13},{13,9},{2,6},{6,2},{1... | collective-permute-start | bytes 3145736 | tf_op jit(solution)/shard_map/ppermute | solution.py:243
  38.7 10.7 %collective-permute-start.14 = (bf16[128,2048]{1,0:T(8,128)(2,1)S(1)}, bf16[128,2048]{1,0:T(8,128)(2,1)S(1)}, u32[]{:S(2)}, u32[]{:S(2)}) collective-permute-start(bf16[128,2048]{1,0:T(8,128)(2,1)S(1)} %pad_maximum_fusion.2), channel_id=1, source_target_pairs={{0,4},{4,0},{8,12},{12,8},{1,5},{5,1},{9,13},{13,9},{2,6},{6,2},{1... | collective-permute-start | bytes 1572872 | tf_op jit(solution)/shard_map/ppermute | solution.py:243
  40.9 7.9 %collective-permute-start.13 = (bf16[128,1024]{1,0:T(8,128)(2,1)S(1)}, bf16[128,1024]{1,0:T(8,128)(2,1)S(1)}, u32[]{:S(2)}, u32[]{:S(2)}) collective-permute-start(bf16[128,1024]{1,0:T(8,128)(2,1)S(1)} %collective-permute-done.9.refs_7_), channel_id=1, source_target_pairs={{0,8},{4,12},{8,0},{12,4},{1,9},{5,13},{9,1},{13,5},{2,10},{6,14},... | collective-permute-start | bytes 786440 | tf_op jit(solution)/shard_map/ppermute | solution.py:240
  44.3 4.6 %collective-permute-start.19 = (bf16[128,1024]{1,0:T(8,128)(2,1)S(1)}, bf16[128,1024]{1,0:T(8,128)(2,1)S(1)}, u32[]{:S(2)}, u32[]{:S(2)}) collective-permute-start(bf16[128,1024]{1,0:T(8,128)(2,1)S(1)} %collective-permute-done.11.refs_11_), channel_id=1, source_target_pairs={{0,4},{4,0},{8,12},{12,8},{1,5},{5,1},{9,13},{13,9},{2,6},{6,2},{1... | collective-permute-start | bytes 786440 | tf_op jit(solution)/shard_map/ppermute | solution.py:243
  48.8 1.9 collective-permute-start.17
  48.9 2.7 %collective-permute-start.18 = (bf16[128,2048]{1,0:T(8,128)(2,1)S(1)}, bf16[128,2048]{1,0:T(8,128)(2,1)S(1)}, u32[]{:S(2)}, u32[]{:S(2)}) collective-permute-start(bf16[128,2048]{1,0:T(8,128)(2,1)S(1)} %pad_maximum_fusion.4), channel_id=1, source_target_pairs={{0,4},{4,0},{8,12},{12,8},{1,5},{5,1},{9,13},{13,9},{2,6},{6,2},{1... | collective-permute-start | bytes 1572872 | tf_op jit(solution)/shard_map/ppermute | solution.py:243
  49.4 2.5 %collective-permute-start.20 = (bf16[128,1024]{1,0:T(8,128)(2,1)S(1)}, bf16[128,1024]{1,0:T(8,128)(2,1)S(1)}, u32[]{:S(2)}, u32[]{:S(2)}) collective-permute-start(bf16[128,1024]{1,0:T(8,128)(2,1)S(1)} %collective-permute-done.13.refs_15_), channel_id=1, source_target_pairs={{0,4},{4,0},{8,12},{12,8},{1,5},{5,1},{9,13},{13,9},{2,6},{6,2},{1... | collective-permute-start | bytes 786440 | tf_op jit(solution)/shard_map/ppermute | solution.py:243

commit v11 on v10

v11 whole, which is shorter than its diff:
```python
import functools
import math

import jax
import jax.numpy as jnp
from jax import lax
from jax.experimental import pallas as pl
from jax.experimental.pallas import tpu as pltpu
from jax.sharding import PartitionSpec as P

HD = 128
CORES = 2
HEADS_PER_TILE = 2
EXP2_SCALE = math.log2(math.e) / math.sqrt(HD)
LEAST_TOTAL, MOST_TOTAL = 1e-20, 1e30


def matmul_nt(a, b):
    return lax.dot_general(a, b, (((1,), (1,)), ((), ())), preferred_element_type=jnp.float32)


class Place:
    def __init__(self, sizes, placement, lengths):
        self.prompt_count, self.chips, self.ring, self.tokens = sizes
        self.blocks, self.slots = self.chips * CORES, self.prompt_count + 1
        self.index, self.head = lax.axis_index("blk"), lax.axis_index("head")
        self.placement, self.lengths = placement, lengths
        self.block = placement[self.index]

    def source(self, slot):
        found = self.index
        for b in range(self.blocks):
            found = jnp.where(self.placement[b] == slot, b, found)
        found = jnp.where(slot == self.prompt_count, self.index, found)
        back = lax.shift_right_logical(self.index, 1) - lax.shift_right_logical(found, 1)
        return jnp.where(back < 0, back + self.chips, back) * CORES + ((self.index ^ found) & 1)

    def first_key(self, slot):
        own = (self.ring - 1 - self.head) * self.tokens
        return jnp.where(slot == self.prompt_count, own, jnp.where(self.block > slot, 0, self.ring * self.tokens))

    def kept(self):
        keep = jnp.int32(self.ring * self.tokens)
        for response in range(self.prompt_count):
            keep = jnp.where(self.block == self.prompt_count + response, self.lengths[response], keep)
        offsets = self.head * self.tokens + lax.broadcasted_iota(jnp.int32, (self.tokens, 1), 0)
        return offsets < keep


def exact(here, query, key, value, out):
    slots, tokens, rows = here.prompt_count + 1, here.tokens, here.ring * here.tokens
    key_row = lax.broadcasted_iota(jnp.int32, (tokens, rows), 1)
    newest_own = rows - tokens + lax.broadcasted_iota(jnp.int32, (tokens, rows), 0)

    def one_head(head, carry):
        columns = pl.ds(pl.multiple_of(head * HD, HD), HD)
        query_one = query[:, columns]

        def part(ref, slot):
            return ref[pl.ds(pl.multiple_of(slot * rows, rows), rows), :]

        def score(slot):
            newest = jnp.where(slot == here.prompt_count, newest_own, rows)
            seen = (key_row >= here.first_key(slot)) & (key_row <= newest)
            return jnp.where(seen, matmul_nt(query_one, part(key, slot)), -jnp.inf)

        row_max = lax.fori_loop(
            0,
            slots,
            lambda j, best: jnp.maximum(best, jnp.max(score(j), axis=1, keepdims=True)),
            jnp.full((tokens, 1), -jnp.inf, jnp.float32),
        )

        def add(slot, carry):
            total, summed = carry
            weights = jnp.exp2((score(slot) - row_max) * EXP2_SCALE)
            total += jnp.sum(weights, axis=1, keepdims=True)
            weights = weights.astype(jnp.bfloat16)
            return total, summed + jnp.dot(weights, part(value, slot), preferred_element_type=jnp.float32)

        zeros = jnp.zeros((tokens, 1), jnp.float32), jnp.zeros((tokens, HD), jnp.float32)
        total, summed = lax.fori_loop(0, slots, add, zeros)
        out[:, columns] = jnp.where(here.kept(), summed / total, 0.0).astype(out.dtype)
        return carry

    lax.fori_loop(0, query.shape[1] // HD, one_head, 0)


def fold_kernel(sizes, places, hops, counts, placement, lengths, query_all, *refs):
    prompt_count, chips, ring, tokens = sizes
    here = Place(sizes, placement, lengths)
    first, last = hops[0] == 0, hops[-1] == ring - 1
    refs = list(refs)
    arrays, state, stored = ([refs.pop(0) for _ in range(count)] for count in counts)
    out_all, held_key, held_value, ones, bias = refs[:5]
    width = held_key.shape[1]
    kv_heads = width // HD
    span = query_all.shape[1] // kv_heads
    group = span // HD
    masked = bias.shape[1]

    def heads_of(kv_head, size):
        return pl.ds(pl.multiple_of(kv_head * size, size), size)

    def take(slot, carry):
        wanted = here.source(slot)
        for i, hop in enumerate(reversed(hops)):
            rows = pl.ds(pl.multiple_of((slot * len(hops) + i) * tokens, tokens), tokens)
            seen = (ring - 1 - hop) * tokens >= here.first_key(slot)
            ones[rows] = jnp.full((tokens, HD), jnp.where(seen, 1.0, 0.0), jnp.float32).astype(ones.dtype)
            for kind, held in enumerate((held_key, held_value)):

                @pl.when(jnp.logical_not(seen))
                def _():
                    held[rows] = jnp.zeros((tokens, width), held.dtype)

                for source in range(here.blocks):
                    array, column = places[kind, source, hop]

                    @pl.when(seen & (wanted == source))
                    def _():
                        held[rows] = arrays[array][:, column : column + width]

        return carry

    lax.fori_loop(0, here.slots, take, 0)
    if first:
        own = lax.broadcasted_iota(jnp.int32, (tokens, masked), 0)
        key_row = lax.broadcasted_iota(jnp.int32, (tokens, masked), 1) - (masked - tokens)
        bias[...] = jnp.where(key_row <= own, 0.0, -jnp.inf)
    kept = here.kept()
    out = refs[5] if last else out_all

    def one_kv_head(kv_head, carry):
        least, most = carry
        query = query_all.at[:, heads_of(kv_head, span)]
        column = heads_of(kv_head, HD)
        keys, values = held_key[:, column], jnp.concatenate([held_value[:, column], ones[...]], axis=1)
        sums = heads_of(kv_head, 2 * span)
        for tile in range(group // HEADS_PER_TILE):
            these = range(tile * HEADS_PER_TILE, (tile + 1) * HEADS_PER_TILE)
            query_tile = jnp.concatenate([query[:, h * HD : (h + 1) * HD] for h in these], axis=0)
            scores = matmul_nt(query_tile, keys) * EXP2_SCALE
            if first:
                split = scores.shape[1] - masked
                tail = scores[:, split:].reshape(HEADS_PER_TILE, tokens, masked) + bias[...][None]
                tail = tail.reshape(HEADS_PER_TILE * tokens, masked)
                scores = tail if split == 0 else jnp.concatenate([scores[:, :split], tail], axis=1)
            weights = jnp.exp2(scores).astype(jnp.bfloat16)
            summed = jnp.dot(weights, values, preferred_element_type=jnp.float32)
            for i, h in enumerate(these):
                part = summed[i * tokens : (i + 1) * tokens]
                both = slice(h * 2 * HD, (h + 1) * 2 * HD)
                if not first:
                    part = part + state[0].at[:, sums][:, both]
                if last:
                    total = part[:, HD:]
                    least, most = jnp.minimum(least, total), jnp.maximum(most, total)
                    result = jnp.where(kept, part[:, :HD] / total, 0.0).astype(out.dtype)
                    out.at[:, heads_of(kv_head, span)][:, h * HD : (h + 1) * HD] = result
                else:
                    out.at[:, sums][:, both] = part
        if last:
            out_copy(kv_head).start()
        return least, most

    def out_copy(kv_head):
        columns = heads_of(kv_head, span)
        return pltpu.make_async_copy(out.at[:, columns], out_all.at[:, columns], refs[6].at[kv_head])

    zeros = jnp.zeros((tokens, HD), jnp.float32)
    least, most = lax.fori_loop(0, kv_heads, one_kv_head, (zeros + jnp.inf, zeros))
    if not last:
        return
    safe = (jnp.min(least) > LEAST_TOTAL) & (jnp.max(most) < MOST_TOTAL)
    for kv_head in range(kv_heads):
        out_copy(kv_head).wait()

    @pl.when(jnp.logical_not(safe))
    def _():
        all_key, all_value, sem = refs[7:]

        def fetch(slot, carry):
            wanted = here.source(slot)
            for source in range(here.blocks):

                @pl.when(wanted == source)
                def _():
                    for back in range(ring):
                        first = (slot * ring + ring - 1 - back) * tokens
                        rows = pl.ds(pl.multiple_of(first, tokens), tokens)
                        for kind, held in enumerate((all_key, all_value)):
                            array, column = places[kind, source, back, None]
                            piece = stored[array].at[:, column : column + width]
                            copy = pltpu.make_async_copy(piece, held.at[rows], sem)
                            copy.start()
                            copy.wait()

            return carry

        lax.fori_loop(0, here.slots, fetch, 0)

        def again(kv_head, carry):
            columns, column = heads_of(kv_head, span), heads_of(kv_head, HD)
            exact(here, query_all.at[:, columns], all_key.at[:, column], all_value.at[:, column], out.at[:, columns])
            out_copy(kv_head).start()
            out_copy(kv_head).wait()
            return carry

        lax.fori_loop(0, kv_heads, again, 0)


def fold(placement, lengths, query_rows, arrays, where, sizes, hops, state):
    prompt_count, chips, ring, tokens = sizes
    slots = prompt_count + 1
    last = hops[-1] == ring - 1
    wanted = [(kind, source, hop) for kind in range(2) for source in range(chips * CORES) for hop in hops]
    used = sorted({where[piece][0] for piece in wanted})
    places = {piece: (used.index(where[piece][0]), where[piece][1]) for piece in wanted}
    width = arrays[0].shape[1]
    kv_heads = width // HD
    keys = slots * len(hops) * tokens
    masked = tokens if tokens % HD == 0 else keys
    scalar, whole, near = (pl.BlockSpec(memory_space=x) for x in (pltpu.SMEM, pl.ANY, pltpu.VMEM))
    operands = [arrays[a] for a in used]
    if state is not None:
        operands.append(state)
    scratch = [
        pltpu.VMEM((keys, width), jnp.bfloat16),
        pltpu.VMEM((keys, width), jnp.bfloat16),
        pltpu.VMEM((keys, HD), jnp.bfloat16),
        pltpu.VMEM((tokens, masked), jnp.float32),
    ]
    specs = [scalar, scalar, near] + [near] * len(operands)
    stored = []
    if last:
        stored = arrays
        places |= {(*piece, None): at for piece, at in where.items()}
        scratch += [
            pltpu.VMEM(query_rows.shape, query_rows.dtype),
            pltpu.SemaphoreType.DMA((kv_heads,)),
            pltpu.VMEM((slots * ring * tokens, width), jnp.bfloat16),
            pltpu.VMEM((slots * ring * tokens, width), jnp.bfloat16),
            pltpu.SemaphoreType.DMA,
        ]
        out_shape, out_spec, aliases = query_rows.shape, whole, {}
    else:
        out_shape, out_spec = (tokens, 2 * query_rows.shape[1]), near
        aliases = {} if state is None else {3 + len(used): 0}
    counts = len(used), int(state is not None), len(stored)
    work = tokens * keys * query_rows.shape[1] // HD
    scoped = 2 * (keys + (slots * ring * tokens if last else 0)) * width * 2 + (12 << 20)
    return pl.pallas_call(
        functools.partial(fold_kernel, sizes, places, hops, counts),
        in_specs=specs + [whole] * len(stored),
        out_specs=out_spec,
        scratch_shapes=scratch,
        out_shape=jax.ShapeDtypeStruct(out_shape, query_rows.dtype if last else jnp.float32),
        input_output_aliases=aliases,
        cost_estimate=pl.CostEstimate(flops=6 * work * HD, bytes_accessed=4 << 20, transcendentals=work),
        compiler_params=pltpu.CompilerParams(vmem_limit_bytes=scoped),
    )(placement, lengths, query_rows, *operands, *stored)


def after(x, *others):
    return lax.optimization_barrier((x, *others))[0]


def shards(query_rows, key_rows, value_rows, placement, lengths):
    blocks, ring = lax.axis_size("blk"), lax.axis_size("head")
    chips = blocks // CORES
    sizes = (blocks // 2, chips, ring, query_rows.shape[0])
    width = key_rows.shape[1]
    kv_heads = width // HD

    def next_hop(x):
        return lax.ppermute(x, "head", [(i, (i + 1) % ring) for i in range(ring)])

    def next_chip(x):
        return lax.ppermute(x, "blk", [(i, (i + CORES) % blocks) for i in range(blocks)])

    def other_core(x):
        return lax.ppermute(x, "blk", [(i, i ^ 1) for i in range(blocks)])

    planes = [[[key_rows], [value_rows]]] + [[[], []] for _ in range(chips - 1)]
    arrays, where = [], {}

    def bundle(*items):
        for place, (back, c, hop) in enumerate(items):
            where[c, back * CORES + 1, hop] = len(arrays), place * width
        packed = jnp.concatenate([planes[back][c][hop] for back, c, hop in items], axis=1)
        arrays.append(other_core(after(packed, state) if items[0][2] == ring - 1 and items[0][0] else packed))

    cut, state = ring // 2, None

    for hop in range(ring):
        if hop == ring - 1:
            state = fold(placement, lengths, query_rows, arrays, where, sizes, tuple(range(cut)), None)
        for column, across in zip(planes[0], planes[1]):
            x = after(column[hop], across[hop - 1]) if hop else column[hop]
            across.append(next_chip(x))
            if hop < ring - 1:
                column.append(next_hop(x))
        for back in range(2, chips):
            for c in range(2):
                planes[back][c].append(next_chip(planes[back - 1][c][hop]))
        for back, plane in enumerate(planes):
            for c in range(2):
                where[c, back * CORES, hop] = len(arrays), 0
                arrays.append(plane[c][hop])
        everything = [(back, c, hop) for back in range(chips) for c in range(2)]
        if hop < cut:
            for piece in everything:
                bundle(piece)
        elif hop < ring - 1:
            bundle(*everything)
        else:
            bundle(*everything[:2])
            bundle(*everything[2:])
    return fold(placement, lengths, query_rows, arrays, where, sizes, tuple(range(cut, ring)), state)


def solution(mesh):
    rows = P(("grp", "blk", "head"), None)
    return jax.shard_map(
        shards,
        mesh=mesh,
        in_specs=(rows, rows, rows, P("grp"), P("grp")),
        out_specs=rows,
        check_vma=False,
    )
```

time: 201 us -> 202 us (level)
  waiting for transfers between devices: 42 us -> 34.6 us
  starting transfers between devices: 9.53 us -> 14 us
  Pallas kernels: 149 us -> 153 us
    ppermute x8, waiting for transfers between devices: 18.4 us -> 11.1 us  [next_chip(): lax.ppermute(x, 'blk', [(i, (i + CORES) % blocks) for i in range(blocks)])]
    pallas_call x1 -> x2, Pallas kernels: 149 us -> 153 us  [fold(): pl.pallas_call(functools.partial(fold_kernel, sizes, places, hops, counts...]
    ppermute x6, starting transfers between devices: 3.16 us -> 6 us  [next_hop(): return lax.ppermute(x, 'head', [(i, (i + 1) % ring) for i in range(ring)])]
  transfers between devices with their start and end apart: 21 -> 25, of which waited for: 17 -> 14; matrix products, arithmetic and copies ran while one was open for 0% -> 0% of each run, Pallas kernels for 0% -> 5%
where the time goes in v11:
time: 202 us
  Pallas kernels  153 us (76%)
  waiting for transfers between devices  34.6 us (17%)
  starting transfers between devices  14 us (7%)
    pallas_call x2, Pallas kernels, fold(): pl.pallas_call(functools.partial(fold_kernel, sizes, places, hops, counts...  153 us
    ppermute x6, waiting for transfers between devices, next_hop(): return lax.ppermute(x, 'head', [(i, (i + 1) % ring) for i in range(ring)])  21.6 us
    ppermute x8, waiting for transfers between devices, next_chip(): lax.ppermute(x, 'blk', [(i, (i + CORES) % blocks) for i in range(blocks)])  11.1 us
    ppermute x8, starting transfers between devices, next_chip(): lax.ppermute(x, 'blk', [(i, (i + CORES) % blocks) for i in range(blocks)])  7.37 us
    ppermute x6, starting transfers between devices, next_hop(): return lax.ppermute(x, 'head', [(i, (i + 1) % ring) for i in range(ring)])  6 us
  transfers between devices with their start and end apart: 25, of which 14 were waited for; matrix products, arithmetic and copies ran while one was open for 0% of the time, Pallas kernels for 5%

profile of v11, /device:TPU:0, one launch (start us, length us, event | category | flops | bytes accessed | tf_op | source)
XLA Modules:
  0.0 201.7 jit_solution(1152389761950439800)
XLA Ops:
  0.0 3.0 %collective-permute-start.1 = (bf16[128,1024]{1,0:T(8,128)(2,1)}, bf16[128,1024]{1,0:T(8,128)(2,1)S(1)}, u32[]{:S(2)}, u32[]{:S(2)}) collective-permute-start(bf16[128,1024]{1,0:T(8,128)(2,1)} %refs_12_.1), channel_id=1, source_target_pairs={{0,8},{4,12},{8,0},{12,4},{1,9},{5,13},{9,1},{13,5},{2,10},{6,14},... | collective-permute-start | bytes 786440 | tf_op jit(solution)/shard_map/ppermute | solution.py:280
  3.0 1.6 collective-permute-start
  4.6 0.5 collective-permute-start.4
  5.1 1.6 collective-permute-start.3
  6.7 3.7 %collective-permute-done.1.refs_2_.refs_14_ = bf16[128,1024]{1,0:T(8,128)(2,1)S(1)} collective-permute-done((bf16[128,1024]{1,0:T(8,128)(2,1)}, bf16[128,1024]{1,0:T(8,128)(2,1)S(1)}, u32[]{:S(2)}, u32[]{:S(2)}) %collective-permute-start.1) | collective-permute-done | bytes 262176 | tf_op jit(solution)/shard_map/ppermute | solution.py:280
  10.4 3.9 %collective-permute-done.refs_8_.refs_20_ = bf16[128,1024]{1,0:T(8,128)(2,1)S(1)} collective-permute-done((bf16[128,1024]{1,0:T(8,128)(2,1)}, bf16[128,1024]{1,0:T(8,128)(2,1)S(1)}, u32[]{:S(2)}, u32[]{:S(2)}) %collective-permute-start) | collective-permute-done | bytes 262176 | tf_op jit(solution)/shard_map/ppermute | solution.py:277
  14.3 0.3 collective-permute-start.6
  14.6 1.4 collective-permute-done.4.refs_3_.refs_15_
  16.0 3.9 %collective-permute-done.3.refs_9_.refs_21_ = bf16[128,1024]{1,0:T(8,128)(2,1)S(1)} collective-permute-done((bf16[128,1024]{1,0:T(8,128)(2,1)}, bf16[128,1024]{1,0:T(8,128)(2,1)S(1)}, u32[]{:S(2)}, u32[]{:S(2)}) %collective-permute-start.3) | collective-permute-done | bytes 262176 | tf_op jit(solution)/shard_map/ppermute | solution.py:277
  19.9 0.3 collective-permute-start.8
  20.2 1.4 collective-permute-done.6.refs_10_.refs_22_
  21.6 4.0 %collective-permute-done.2.refs_0_.refs_28_ = bf16[128,1024]{1,0:T(8,128)(2,1)S(1)} collective-permute-done((bf16[128,1024]{1,0:T(8,128)(2,1)S(1)}, bf16[128,1024]{1,0:T(8,128)(2,1)S(1)}, u32[]{:S(2)}, u32[]{:S(2)}) %collective-permute-start.2) | collective-permute-done | bytes 262176 | tf_op jit(solution)/shard_map/ppermute | solution.py:277
  25.6 0.8 collective-permute-done.8.refs_11_.refs_23_
  26.4 1.8 collective-permute-start.11
  28.2 1.5 collective-permute-done.5.refs_1_.refs_29_
  29.8 0.5 collective-permute-start.7
  30.3 1.0 collective-permute-start.12
  31.3 0.6 collective-permute-start.9
  31.9 5.6 %collective-permute-done.11.refs_5_.refs_33_ = bf16[128,1024]{1,0:T(8,128)(2,1)S(1)} collective-permute-done((bf16[128,1024]{1,0:T(8,128)(2,1)S(1)}, bf16[128,1024]{1,0:T(8,128)(2,1)S(1)}, u32[]{:S(2)}, u32[]{:S(2)}) %collective-permute-start.11) | collective-permute-done | bytes 262176 | tf_op jit(solution)/shard_map/ppermute | solution.py:277
  37.4 1.6 collective-permute-done.7.refs_2_.refs_30_
  39.0 2.8 %collective-permute-done.12.refs_6_.refs_34_ = bf16[128,1024]{1,0:T(8,128)(2,1)S(1)} collective-permute-done((bf16[128,1024]{1,0:T(8,128)(2,1)S(1)}, bf16[128,1024]{1,0:T(8,128)(2,1)S(1)}, u32[]{:S(2)}, u32[]{:S(2)}) %collective-permute-start.12) | collective-permute-done | bytes 262176 | tf_op jit(solution)/shard_map/ppermute | solution.py:277
  41.8 0.4 collective-permute-done.9.refs_3_.refs_31_
  42.2 0.1 collective-permute-start.23
  42.3 0.1 pad_maximum_fusion
  42.4 1.1 collective-permute-start.13
  43.5 1.0 collective-permute-start.14
  44.5 0.5 collective-permute-start.10
  45.1 9.9 %shard_map.55.refs_11_ = f32[128,16384]{1,0:T(8,128)S(1)} custom-call(s32[4]{0:T(128)S(1)} %copy-done.3, s32[2]{0:T(128)S(1)} %copy-done.4, bf16[128,8192]{1,0:T(8,128)(2,1)S(1)} %copy-done, bf16[128,1024]{1,0:T(8,128)(2,1)S(1)} %copy-done.1, bf16[128,1024]{1,0:T(8,128)(2,1)S(1)} %copy-done.2, bf16[128,1024]{1,0:T(8,128)(2,1)S(1)} %collective-permute-done.1.refs_2_.refs_14_, ...), custom_call_target="tpu_custom_call" | custom-call | flops 4831838208 | bytes 4194304 | tf_op jit(solution)/shard_map/pallas_call | solution.py:253
  54.9 1.8 collective-permute-done.14.refs_8_.refs_36_
  56.8 0.1 collective-permute-start.24
  56.9 1.9 collective-permute-done.24.refs_10_.refs_38_
  58.8 142.9 %shard_map.56 = bf16[128,8192]{1,0:T(8,128)(2,1)} custom-call(s32[4]{0:T(128)S(1)} %copy-done.3, s32[2]{0:T(128)S(1)} %copy-done.4, bf16[128,8192]{1,0:T(8,128)(2,1)S(1)} %copy-done, bf16[128,1024]{1,0:T(8,128)(2,1)S(1)} %collective-permute-done.2.refs_0_.refs_28_, bf16[128,1024]{1,0:T(8,128)(2,1)S(1)} %collective-permute-done.5.refs_1_.refs_29_, ...), custom_call_target="tpu_custom_call" | custom-call | flops 4831838208 | bytes 4194304 | tf_op jit(solution)/shard_map/pallas_call | solution.py:253
  (33 shorter events, 0.1 us)
Async XLA Ops:
  0.0 45.0 %copy-start.1 = (bf16[128,1024]{1,0:T(8,128)(2,1)S(1)}, bf16[128,1024]{1,0:T(8,128)(2,1)}, u32[]{:S(2)}) copy-start(bf16[128,1024]{1,0:T(8,128)(2,1)} %refs_12_.1) | copy-start | bytes 786436
  0.0 45.0 %copy-start.2 = (bf16[128,1024]{1,0:T(8,128)(2,1)S(1)}, bf16[128,1024]{1,0:T(8,128)(2,1)}, u32[]{:S(2)}) copy-start(bf16[128,1024]{1,0:T(8,128)(2,1)} %refs_13_.1) | copy-start | bytes 786436
  0.0 45.0 %copy-start.4 = (s32[2]{0:T(128)S(1)}, s32[2]{0:T(128)}, u32[]{:S(2)}) copy-start(s32[2]{0:T(128)} %lengths.3) | copy-start | bytes 28
  0.0 45.0 %copy-start.3 = (s32[4]{0:T(128)S(1)}, s32[4]{0:T(128)}, u32[]{:S(2)}) copy-start(s32[4]{0:T(128)} %placement.3) | copy-start | bytes 52
  0.0 45.0 %copy-start = (bf16[128,8192]{1,0:T(8,128)(2,1)S(1)}, bf16[128,8192]{1,0:T(8,128)(2,1)}, u32[]{:S(2)}) copy-start(bf16[128,8192]{1,0:T(8,128)(2,1)} %query_all.3) | copy-start | bytes 6291460
  0.0 10.4 %collective-permute-start.1 = (bf16[128,1024]{1,0:T(8,128)(2,1)}, bf16[128,1024]{1,0:T(8,128)(2,1)S(1)}, u32[]{:S(2)}, u32[]{:S(2)}) collective-permute-start(bf16[128,1024]{1,0:T(8,128)(2,1)} %refs_12_.1), channel_id=1, source_target_pairs={{0,8},{4,12},{8,0},{12,4},{1,9},{5,13},{9,1},{13,5},{2,10},{6,14},... | collective-permute-start | bytes 786440 | tf_op jit(solution)/shard_map/ppermute | solution.py:280
  3.0 11.2 %collective-permute-start = (bf16[128,1024]{1,0:T(8,128)(2,1)}, bf16[128,1024]{1,0:T(8,128)(2,1)S(1)}, u32[]{:S(2)}, u32[]{:S(2)}) collective-permute-start(bf16[128,1024]{1,0:T(8,128)(2,1)} %refs_12_.1), channel_id=1, source_target_pairs={{0,1},{1,2},{2,3},{3,0},{4,5},{5,6},{6,7},{7,4},{8,9},{9,10},{10,1... | collective-permute-start | bytes 786440 | tf_op jit(solution)/shard_map/ppermute | solution.py:277
  4.6 11.4 %collective-permute-start.4 = (bf16[128,1024]{1,0:T(8,128)(2,1)}, bf16[128,1024]{1,0:T(8,128)(2,1)S(1)}, u32[]{:S(2)}, u32[]{:S(2)}) collective-permute-start(bf16[128,1024]{1,0:T(8,128)(2,1)} %refs_13_.1), channel_id=1, source_target_pairs={{0,8},{4,12},{8,0},{12,4},{1,9},{5,13},{9,1},{13,5},{2,10},{6,14},... | collective-permute-start | bytes 786440 | tf_op jit(solution)/shard_map/ppermute | solution.py:280
  5.1 14.7 %collective-permute-start.3 = (bf16[128,1024]{1,0:T(8,128)(2,1)}, bf16[128,1024]{1,0:T(8,128)(2,1)S(1)}, u32[]{:S(2)}, u32[]{:S(2)}) collective-permute-start(bf16[128,1024]{1,0:T(8,128)(2,1)} %refs_13_.1), channel_id=1, source_target_pairs={{0,1},{1,2},{2,3},{3,0},{4,5},{5,6},{6,7},{7,4},{8,9},{9,10},{10,1... | collective-permute-start | bytes 786440 | tf_op jit(solution)/shard_map/ppermute | solution.py:277
  14.3 7.4 %collective-permute-start.6 = (bf16[128,1024]{1,0:T(8,128)(2,1)S(1)}, bf16[128,1024]{1,0:T(8,128)(2,1)S(1)}, u32[]{:S(2)}, u32[]{:S(2)}) collective-permute-start(bf16[128,1024]{1,0:T(8,128)(2,1)S(1)} %collective-permute-done.refs_8_.refs_20_), channel_id=1, source_target_pairs={{0,8},{4,12},{8,0},{12,4},{1,9},{5,13},{9,1},{13,5},{2,10},{6,14},... | collective-permute-start | bytes 786440 | tf_op jit(solution)/shard_map/ppermute | solution.py:280
  14.6 11.0 %collective-permute-start.2 = (bf16[128,1024]{1,0:T(8,128)(2,1)S(1)}, bf16[128,1024]{1,0:T(8,128)(2,1)S(1)}, u32[]{:S(2)}, u32[]{:S(2)}) collective-permute-start(bf16[128,1024]{1,0:T(8,128)(2,1)S(1)} %collective-permute-done.refs_8_.refs_20_), channel_id=1, source_target_pairs={{0,1},{1,2},{2,3},{3,0},{4,5},{5,6},{6,7},{7,4},{8,9},{9,10},{10,1... | collective-permute-start | bytes 786440 | tf_op jit(solution)/shard_map/ppermute | solution.py:277
  19.9 6.5 %collective-permute-start.8 = (bf16[128,1024]{1,0:T(8,128)(2,1)S(1)}, bf16[128,1024]{1,0:T(8,128)(2,1)S(1)}, u32[]{:S(2)}, u32[]{:S(2)}) collective-permute-start(bf16[128,1024]{1,0:T(8,128)(2,1)S(1)} %collective-permute-done.3.refs_9_.refs_21_), channel_id=1, source_target_pairs={{0,8},{4,12},{8,0},{12,4},{1,9},{5,13},{9,1},{13,5},{2,10},{6,14},... | collective-permute-start | bytes 786440 | tf_op jit(solution)/shard_map/ppermute | solution.py:280
  20.2 9.6 %collective-permute-start.5 = (bf16[128,1024]{1,0:T(8,128)(2,1)S(1)}, bf16[128,1024]{1,0:T(8,128)(2,1)S(1)}, u32[]{:S(2)}, u32[]{:S(2)}) collective-permute-start(bf16[128,1024]{1,0:T(8,128)(2,1)S(1)} %collective-permute-done.3.refs_9_.refs_21_), channel_id=1, source_target_pairs={{0,1},{1,2},{2,3},{3,0},{4,5},{5,6},{6,7},{7,4},{8,9},{9,10},{10,1... | collective-permute-start | bytes 786440 | tf_op jit(solution)/shard_map/ppermute | solution.py:277
  20.2 10.1 %collective-permute-start.16 = (bf16[128,1024]{1,0:T(8,128)(2,1)}, bf16[128,1024]{1,0:T(8,128)(2,1)S(1)}, u32[]{:S(2)}, u32[]{:S(2)}) collective-permute-start(bf16[128,1024]{1,0:T(8,128)(2,1)} %refs_12_.1), channel_id=1, source_target_pairs={{0,4},{4,0},{8,12},{12,8},{1,5},{5,1},{9,13},{13,9},{2,6},{6,2},{1... | collective-permute-start | bytes 786440 | tf_op jit(solution)/shard_map/ppermute | solution.py:283
  21.6 9.7 %collective-permute-start.17 = (bf16[128,1024]{1,0:T(8,128)(2,1)}, bf16[128,1024]{1,0:T(8,128)(2,1)S(1)}, u32[]{:S(2)}, u32[]{:S(2)}) collective-permute-start(bf16[128,1024]{1,0:T(8,128)(2,1)} %refs_13_.1), channel_id=1, source_target_pairs={{0,4},{4,0},{8,12},{12,8},{1,5},{5,1},{9,13},{13,9},{2,6},{6,2},{1... | collective-permute-start | bytes 786440 | tf_op jit(solution)/shard_map/ppermute | solution.py:283
  25.6 6.2 %collective-permute-start.18 = (bf16[128,1024]{1,0:T(8,128)(2,1)S(1)}, bf16[128,1024]{1,0:T(8,128)(2,1)S(1)}, u32[]{:S(2)}, u32[]{:S(2)}) collective-permute-start(bf16[128,1024]{1,0:T(8,128)(2,1)S(1)} %collective-permute-done.1.refs_2_.refs_14_), channel_id=1, source_target_pairs={{0,4},{4,0},{8,12},{12,8},{1,5},{5,1},{9,13},{13,9},{2,6},{6,2},{1... | collective-permute-start | bytes 786440 | tf_op jit(solution)/shard_map/ppermute | solution.py:283
  26.4 11.0 %collective-permute-start.11 = (bf16[128,1024]{1,0:T(8,128)(2,1)S(1)}, bf16[128,1024]{1,0:T(8,128)(2,1)S(1)}, u32[]{:S(2)}, u32[]{:S(2)}) collective-permute-start(bf16[128,1024]{1,0:T(8,128)(2,1)S(1)} %collective-permute-done.2.refs_0_.refs_28_), channel_id=1, source_target_pairs={{0,1},{1,2},{2,3},{3,0},{4,5},{5,6},{6,7},{7,4},{8,9},{9,10},{10,1... | collective-permute-start | bytes 786440 | tf_op jit(solution)/shard_map/ppermute | solution.py:277
  29.8 9.2 %collective-permute-start.7 = (bf16[128,1024]{1,0:T(8,128)(2,1)S(1)}, bf16[128,1024]{1,0:T(8,128)(2,1)S(1)}, u32[]{:S(2)}, u32[]{:S(2)}) collective-permute-start(bf16[128,1024]{1,0:T(8,128)(2,1)S(1)} %collective-permute-done.2.refs_0_.refs_28_), channel_id=1, source_target_pairs={{0,8},{4,12},{8,0},{12,4},{1,9},{5,13},{9,1},{13,5},{2,10},{6,14},... | collective-permute-start | bytes 786440 | tf_op jit(solution)/shard_map/ppermute | solution.py:280
  30.3 11.5 %collective-permute-start.12 = (bf16[128,1024]{1,0:T(8,128)(2,1)S(1)}, bf16[128,1024]{1,0:T(8,128)(2,1)S(1)}, u32[]{:S(2)}, u32[]{:S(2)}) collective-permute-start(bf16[128,1024]{1,0:T(8,128)(2,1)S(1)} %collective-permute-done.5.refs_1_.refs_29_), channel_id=1, source_target_pairs={{0,1},{1,2},{2,3},{3,0},{4,5},{5,6},{6,7},{7,4},{8,9},{9,10},{10,1... | collective-permute-start | bytes 786440 | tf_op jit(solution)/shard_map/ppermute | solution.py:277
  31.3 10.9 %collective-permute-start.9 = (bf16[128,1024]{1,0:T(8,128)(2,1)S(1)}, bf16[128,1024]{1,0:T(8,128)(2,1)S(1)}, u32[]{:S(2)}, u32[]{:S(2)}) collective-permute-start(bf16[128,1024]{1,0:T(8,128)(2,1)S(1)} %collective-permute-done.5.refs_1_.refs_29_), channel_id=1, source_target_pairs={{0,8},{4,12},{8,0},{12,4},{1,9},{5,13},{9,1},{13,5},{2,10},{6,14},... | collective-permute-start | bytes 786440 | tf_op jit(solution)/shard_map/ppermute | solution.py:280
  31.9 10.5 %collective-permute-start.20 = (bf16[128,1024]{1,0:T(8,128)(2,1)S(1)}, bf16[128,1024]{1,0:T(8,128)(2,1)S(1)}, u32[]{:S(2)}, u32[]{:S(2)}) collective-permute-start(bf16[128,1024]{1,0:T(8,128)(2,1)S(1)} %collective-permute-done.refs_8_.refs_20_), channel_id=1, source_target_pairs={{0,4},{4,0},{8,12},{12,8},{1,5},{5,1},{9,13},{13,9},{2,6},{6,2},{1... | collective-permute-start | bytes 786440 | tf_op jit(solution)/shard_map/ppermute | solution.py:283
  37.4 6.1 %collective-permute-start.19 = (bf16[128,1024]{1,0:T(8,128)(2,1)S(1)}, bf16[128,1024]{1,0:T(8,128)(2,1)S(1)}, u32[]{:S(2)}, u32[]{:S(2)}) collective-permute-start(bf16[128,1024]{1,0:T(8,128)(2,1)S(1)} %collective-permute-done.4.refs_3_.refs_15_), channel_id=1, source_target_pairs={{0,4},{4,0},{8,12},{12,8},{1,5},{5,1},{9,13},{13,9},{2,6},{6,2},{1... | collective-permute-start | bytes 786440 | tf_op jit(solution)/shard_map/ppermute | solution.py:283
  39.0 5.5 %collective-permute-start.21 = (bf16[128,1024]{1,0:T(8,128)(2,1)S(1)}, bf16[128,1024]{1,0:T(8,128)(2,1)S(1)}, u32[]{:S(2)}, u32[]{:S(2)}) collective-permute-start(bf16[128,1024]{1,0:T(8,128)(2,1)S(1)} %collective-permute-done.3.refs_9_.refs_21_), channel_id=1, source_target_pairs={{0,4},{4,0},{8,12},{12,8},{1,5},{5,1},{9,13},{13,9},{2,6},{6,2},{1... | collective-permute-start | bytes 786440 | tf_op jit(solution)/shard_map/ppermute | solution.py:283
  41.8 2.7 %collective-permute-start.22 = (bf16[128,1024]{1,0:T(8,128)(2,1)S(1)}, bf16[128,1024]{1,0:T(8,128)(2,1)S(1)}, u32[]{:S(2)}, u32[]{:S(2)}) collective-permute-start(bf16[128,1024]{1,0:T(8,128)(2,1)S(1)} %collective-permute-done.6.refs_10_.refs_22_), channel_id=1, source_target_pairs={{0,4},{4,0},{8,12},{12,8},{1,5},{5,1},{9,13},{13,9},{2,6},{6,2},{1... | collective-permute-start | bytes 786440 | tf_op jit(solution)/shard_map/ppermute | solution.py:283
  42.2 2.8 %collective-permute-start.23 = (bf16[128,1024]{1,0:T(8,128)(2,1)S(1)}, bf16[128,1024]{1,0:T(8,128)(2,1)S(1)}, u32[]{:S(2)}, u32[]{:S(2)}) collective-permute-start(bf16[128,1024]{1,0:T(8,128)(2,1)S(1)} %collective-permute-done.8.refs_11_.refs_23_), channel_id=1, source_target_pairs={{0,4},{4,0},{8,12},{12,8},{1,5},{5,1},{9,13},{13,9},{2,6},{6,2},{1... | collective-permute-start | bytes 786440 | tf_op jit(solution)/shard_map/ppermute | solution.py:283
  42.4 12.5 %collective-permute-start.13 = (bf16[128,1024]{1,0:T(8,128)(2,1)S(1)}, bf16[128,1024]{1,0:T(8,128)(2,1)S(1)}, u32[]{:S(2)}, u32[]{:S(2)}) collective-permute-start(bf16[128,1024]{1,0:T(8,128)(2,1)S(1)} %collective-permute-done.11.refs_5_.refs_33_), channel_id=1, source_target_pairs={{0,8},{4,12},{8,0},{12,4},{1,9},{5,13},{9,1},{13,5},{2,10},{6,14},... | collective-permute-start | bytes 786440 | tf_op jit(solution)/shard_map/ppermute | solution.py:280
  43.5 13.2 %collective-permute-start.14 = (bf16[128,1024]{1,0:T(8,128)(2,1)S(1)}, bf16[128,1024]{1,0:T(8,128)(2,1)S(1)}, u32[]{:S(2)}, u32[]{:S(2)}) collective-permute-start(bf16[128,1024]{1,0:T(8,128)(2,1)S(1)} %collective-permute-done.12.refs_6_.refs_34_), channel_id=1, source_target_pairs={{0,8},{4,12},{8,0},{12,4},{1,9},{5,13},{9,1},{13,5},{2,10},{6,14},... | collective-permute-start | bytes 786440 | tf_op jit(solution)/shard_map/ppermute | solution.py:280
  44.5 12.4 %collective-permute-start.15 = (bf16[128,2048]{1,0:T(8,128)(2,1)S(1)}, bf16[128,2048]{1,0:T(8,128)(2,1)S(1)}, u32[]{:S(2)}, u32[]{:S(2)}) collective-permute-start(bf16[128,2048]{1,0:T(8,128)(2,1)S(1)} %pad_maximum_fusion.1), channel_id=1, source_target_pairs={{0,4},{4,0},{8,12},{12,8},{1,5},{5,1},{9,13},{13,9},{2,6},{6,2},{1... | collective-permute-start | bytes 1572872 | tf_op jit(solution)/shard_map/ppermute | solution.py:283
  44.5 14.2 %collective-permute-start.10 = (bf16[128,4096]{1,0:T(8,128)(2,1)S(1)}, bf16[128,4096]{1,0:T(8,128)(2,1)S(1)}, u32[]{:S(2)}, u32[]{:S(2)}) collective-permute-start(bf16[128,4096]{1,0:T(8,128)(2,1)S(1)} %pad_maximum_fusion), channel_id=1, source_target_pairs={{0,4},{4,0},{8,12},{12,8},{1,5},{5,1},{9,13},{13,9},{2,6},{6,2},{1... | collective-permute-start | bytes 3145736 | tf_op jit(solution)/shard_map/ppermute | solution.py:283
  56.8 2.0 collective-permute-start.24

commit v12 on v10

--- a/solution.py
+++ b/solution.py
@@ -10,7 +10,7 @@
 
 HD = 128
 CORES = 2
-HEADS_PER_TILE = 2
+HEADS_PER_TILE = 4
 RESIDENT_BYTES = 16 << 20
 EXP2_SCALE = math.log2(math.e) / math.sqrt(HD)
 LEAST_TOTAL, MOST_TOTAL = 1e-20, 1e30
@@ -218,7 +218,7 @@
         ],
         out_shape=jax.ShapeDtypeStruct(query_rows.shape, query_rows.dtype),
         cost_estimate=pl.CostEstimate(flops=6 * work * HD, bytes_accessed=12 << 20, transcendentals=work),
-        compiler_params=pltpu.CompilerParams(vmem_limit_bytes=2 * keys * width * 2 + (14 << 20)),
+        compiler_params=pltpu.CompilerParams(vmem_limit_bytes=2 * keys * width * 2 + (20 << 20)),
     )(placement, lengths, pltpu.with_memory_space_constraint(query_rows, pltpu.HBM), *arrays)
 
 

time: 201 us -> 200 us (level)
  no operation moved by 1% of the time
where the time goes in v12:
time: 200 us
  Pallas kernels  148 us (74%)
  waiting for transfers between devices  42 us (21%)
  starting transfers between devices  9.53 us (5%)
    pallas_call x1, Pallas kernels, attend(): pl.pallas_call(functools.partial(attend_kernel, sizes, where, resident),...  148 us
    ppermute x6, waiting for transfers between devices, next_hop(): return lax.ppermute(x, 'head', [(i, (i + 1) % ring) for i in range(ring)])  21.2 us
    ppermute x8, waiting for transfers between devices, next_chip(): lax.ppermute(x, 'blk', [(i, (i + CORES) % blocks) for i in range(blocks)])  18.4 us
    ppermute x8, starting transfers between devices, next_chip(): lax.ppermute(x, 'blk', [(i, (i + CORES) % blocks) for i in range(blocks)])  5.63 us
  transfers between devices with their start and end apart: 21, of which 17 were waited for; matrix products, arithmetic and copies ran while one was open for 0% of the time, Pallas kernels for 0%

profile of v12, /device:TPU:0, one launch (start us, length us, event | category | flops | bytes accessed | tf_op | source)
XLA Modules:
  0.0 200.3 jit_solution(2584614003040214081)
XLA Ops:
  0.0 2.9 %collective-permute-start.1 = (bf16[128,1024]{1,0:T(8,128)(2,1)}, bf16[128,1024]{1,0:T(8,128)(2,1)S(1)}, u32[]{:S(2)}, u32[]{:S(2)}) collective-permute-start(bf16[128,1024]{1,0:T(8,128)(2,1)} %refs_0_.1), channel_id=1, source_target_pairs={{0,8},{4,12},{8,0},{12,4},{1,9},{5,13},{9,1},{13,5},{2,10},{6,14},... | collective-permute-start | bytes 786440 | tf_op jit(solution)/shard_map/ppermute | solution.py:240
  2.9 1.6 collective-permute-start
  4.5 0.5 collective-permute-start.6
  5.1 1.6 collective-permute-start.5
  6.6 3.7 %collective-permute-done.1.refs_8_ = bf16[128,1024]{1,0:T(8,128)(2,1)S(1)} collective-permute-done((bf16[128,1024]{1,0:T(8,128)(2,1)}, bf16[128,1024]{1,0:T(8,128)(2,1)S(1)}, u32[]{:S(2)}, u32[]{:S(2)}) %collective-permute-start.1) | collective-permute-done | bytes 262176 | tf_op jit(solution)/shard_map/ppermute | solution.py:240
  10.4 3.8 %collective-permute-done.refs_1_ = bf16[128,1024]{1,0:T(8,128)(2,1)S(1)} collective-permute-done((bf16[128,1024]{1,0:T(8,128)(2,1)}, bf16[128,1024]{1,0:T(8,128)(2,1)S(1)}, u32[]{:S(2)}, u32[]{:S(2)}) %collective-permute-start) | collective-permute-done | bytes 262176 | tf_op jit(solution)/shard_map/ppermute | solution.py:237
  14.2 0.3 collective-permute-start.3
  14.5 1.5 collective-permute-done.6.refs_12_
  16.0 3.8 %collective-permute-done.5.refs_5_ = bf16[128,1024]{1,0:T(8,128)(2,1)S(1)} collective-permute-done((bf16[128,1024]{1,0:T(8,128)(2,1)}, bf16[128,1024]{1,0:T(8,128)(2,1)S(1)}, u32[]{:S(2)}, u32[]{:S(2)}) %collective-permute-start.5) | collective-permute-done | bytes 262176 | tf_op jit(solution)/shard_map/ppermute | solution.py:237
  19.8 0.3 collective-permute-start.8
  20.1 1.6 collective-permute-done.3.refs_9_
  21.7 3.9 %collective-permute-done.2.refs_2_ = bf16[128,1024]{1,0:T(8,128)(2,1)S(1)} collective-permute-done((bf16[128,1024]{1,0:T(8,128)(2,1)S(1)}, bf16[128,1024]{1,0:T(8,128)(2,1)S(1)}, u32[]{:S(2)}, u32[]{:S(2)}) %collective-permute-start.2) | collective-permute-done | bytes 262176 | tf_op jit(solution)/shard_map/ppermute | solution.py:237
  25.5 0.2 collective-permute-start.10
  25.9 0.1 collective-permute-start.15
  26.0 1.5 collective-permute-done.8.refs_13_
  27.4 3.7 %collective-permute-done.7.refs_6_ = bf16[128,1024]{1,0:T(8,128)(2,1)S(1)} collective-permute-done((bf16[128,1024]{1,0:T(8,128)(2,1)S(1)}, bf16[128,1024]{1,0:T(8,128)(2,1)S(1)}, u32[]{:S(2)}, u32[]{:S(2)}) %collective-permute-start.7) | collective-permute-done | bytes 262176 | tf_op jit(solution)/shard_map/ppermute | solution.py:237
  31.2 0.4 collective-permute-start.12
  31.5 1.5 collective-permute-done.10.refs_10_
  33.0 3.7 %collective-permute-done.4.refs_3_ = bf16[128,1024]{1,0:T(8,128)(2,1)S(1)} collective-permute-done((bf16[128,1024]{1,0:T(8,128)(2,1)S(1)}, bf16[128,1024]{1,0:T(8,128)(2,1)S(1)}, u32[]{:S(2)}, u32[]{:S(2)}) %collective-permute-start.4) | collective-permute-done | bytes 262176 | tf_op jit(solution)/shard_map/ppermute | solution.py:237
  36.8 0.4 collective-permute-start.11
  37.2 0.1 collective-permute-start.16
  37.4 1.3 collective-permute-done.12.refs_14_
  38.7 2.2 %collective-permute-done.9.refs_7_ = bf16[128,1024]{1,0:T(8,128)(2,1)S(1)} collective-permute-done((bf16[128,1024]{1,0:T(8,128)(2,1)S(1)}, bf16[128,1024]{1,0:T(8,128)(2,1)S(1)}, u32[]{:S(2)}, u32[]{:S(2)}) %collective-permute-start.9) | collective-permute-done | bytes 262176 | tf_op jit(solution)/shard_map/ppermute | solution.py:237
  40.9 0.5 collective-permute-start.13
  41.4 2.8 %collective-permute-done.11.refs_11_ = bf16[128,1024]{1,0:T(8,128)(2,1)S(1)} collective-permute-done((bf16[128,1024]{1,0:T(8,128)(2,1)S(1)}, bf16[128,1024]{1,0:T(8,128)(2,1)S(1)}, u32[]{:S(2)}, u32[]{:S(2)}) %collective-permute-start.11) | collective-permute-done | bytes 262176 | tf_op jit(solution)/shard_map/ppermute | solution.py:240
  44.4 4.5 %collective-permute-done.13.refs_15_ = bf16[128,1024]{1,0:T(8,128)(2,1)S(1)} collective-permute-done((bf16[128,1024]{1,0:T(8,128)(2,1)S(1)}, bf16[128,1024]{1,0:T(8,128)(2,1)S(1)}, u32[]{:S(2)}, u32[]{:S(2)}) %collective-permute-start.13) | collective-permute-done | bytes 262176 | tf_op jit(solution)/shard_map/ppermute | solution.py:240
  48.9 0.5 collective-permute-start.18
  49.4 0.1 collective-permute-start.20
  49.4 1.3 collective-permute-done.17.refs_19_
  50.8 0.7 collective-permute-done.18.refs_20_
  51.5 0.4 collective-permute-done.20.refs_22_
  51.9 148.4 %shard_map.55 = bf16[128,8192]{1,0:T(8,128)(2,1)} custom-call(s32[4]{0:T(128)S(1)} %copy-done.2, s32[2]{0:T(128)S(1)} %copy-done.3, bf16[128,8192]{1,0:T(8,128)(2,1)} %query_all.1, bf16[128,1024]{1,0:T(8,128)(2,1)S(1)} %copy-done, bf16[128,1024]{1,0:T(8,128)(2,1)S(1)} %collective-permute-done.refs_1_, bf16[128,1024]{1,0:T(8,128)(2,1)S(1)} %collective-permute-done.2.refs_2_, ...), custom_call_target="tpu_custom_call" | custom-call | flops 9663676416 | bytes 12582912 | tf_op jit(solution)/shard_map/pallas_call | solution.py:205
  (24 shorter events, 0.3 us)
Async XLA Ops:
  0.0 37.3 %copy-start = (bf16[128,1024]{1,0:T(8,128)(2,1)S(1)}, bf16[128,1024]{1,0:T(8,128)(2,1)}, u32[]{:S(2)}) copy-start(bf16[128,1024]{1,0:T(8,128)(2,1)} %refs_0_.1) | copy-start | bytes 786436
  0.0 37.3 %copy-start.1 = (bf16[128,1024]{1,0:T(8,128)(2,1)S(1)}, bf16[128,1024]{1,0:T(8,128)(2,1)}, u32[]{:S(2)}) copy-start(bf16[128,1024]{1,0:T(8,128)(2,1)} %refs_4_.1) | copy-start | bytes 786436
  0.0 10.3 %collective-permute-start.1 = (bf16[128,1024]{1,0:T(8,128)(2,1)}, bf16[128,1024]{1,0:T(8,128)(2,1)S(1)}, u32[]{:S(2)}, u32[]{:S(2)}) collective-permute-start(bf16[128,1024]{1,0:T(8,128)(2,1)} %refs_0_.1), channel_id=1, source_target_pairs={{0,8},{4,12},{8,0},{12,4},{1,9},{5,13},{9,1},{13,5},{2,10},{6,14},... | collective-permute-start | bytes 786440 | tf_op jit(solution)/shard_map/ppermute | solution.py:240
  2.9 11.2 %collective-permute-start = (bf16[128,1024]{1,0:T(8,128)(2,1)}, bf16[128,1024]{1,0:T(8,128)(2,1)S(1)}, u32[]{:S(2)}, u32[]{:S(2)}) collective-permute-start(bf16[128,1024]{1,0:T(8,128)(2,1)} %refs_0_.1), channel_id=1, source_target_pairs={{0,1},{1,2},{2,3},{3,0},{4,5},{5,6},{6,7},{7,4},{8,9},{9,10},{10,1... | collective-permute-start | bytes 786440 | tf_op jit(solution)/shard_map/ppermute | solution.py:237
  4.5 11.5 %collective-permute-start.6 = (bf16[128,1024]{1,0:T(8,128)(2,1)}, bf16[128,1024]{1,0:T(8,128)(2,1)S(1)}, u32[]{:S(2)}, u32[]{:S(2)}) collective-permute-start(bf16[128,1024]{1,0:T(8,128)(2,1)} %refs_4_.1), channel_id=1, source_target_pairs={{0,8},{4,12},{8,0},{12,4},{1,9},{5,13},{9,1},{13,5},{2,10},{6,14},... | collective-permute-start | bytes 786440 | tf_op jit(solution)/shard_map/ppermute | solution.py:240
  5.1 14.7 %collective-permute-start.5 = (bf16[128,1024]{1,0:T(8,128)(2,1)}, bf16[128,1024]{1,0:T(8,128)(2,1)S(1)}, u32[]{:S(2)}, u32[]{:S(2)}) collective-permute-start(bf16[128,1024]{1,0:T(8,128)(2,1)} %refs_4_.1), channel_id=1, source_target_pairs={{0,1},{1,2},{2,3},{3,0},{4,5},{5,6},{6,7},{7,4},{8,9},{9,10},{10,1... | collective-permute-start | bytes 786440 | tf_op jit(solution)/shard_map/ppermute | solution.py:237
  14.2 7.5 %collective-permute-start.3 = (bf16[128,1024]{1,0:T(8,128)(2,1)S(1)}, bf16[128,1024]{1,0:T(8,128)(2,1)S(1)}, u32[]{:S(2)}, u32[]{:S(2)}) collective-permute-start(bf16[128,1024]{1,0:T(8,128)(2,1)S(1)} %collective-permute-done.refs_1_), channel_id=1, source_target_pairs={{0,8},{4,12},{8,0},{12,4},{1,9},{5,13},{9,1},{13,5},{2,10},{6,14},... | collective-permute-start | bytes 786440 | tf_op jit(solution)/shard_map/ppermute | solution.py:240
  14.5 11.0 %collective-permute-start.2 = (bf16[128,1024]{1,0:T(8,128)(2,1)S(1)}, bf16[128,1024]{1,0:T(8,128)(2,1)S(1)}, u32[]{:S(2)}, u32[]{:S(2)}) collective-permute-start(bf16[128,1024]{1,0:T(8,128)(2,1)S(1)} %collective-permute-done.refs_1_), channel_id=1, source_target_pairs={{0,1},{1,2},{2,3},{3,0},{4,5},{5,6},{6,7},{7,4},{8,9},{9,10},{10,1... | collective-permute-start | bytes 786440 | tf_op jit(solution)/shard_map/ppermute | solution.py:237
  19.8 7.6 %collective-permute-start.8 = (bf16[128,1024]{1,0:T(8,128)(2,1)S(1)}, bf16[128,1024]{1,0:T(8,128)(2,1)S(1)}, u32[]{:S(2)}, u32[]{:S(2)}) collective-permute-start(bf16[128,1024]{1,0:T(8,128)(2,1)S(1)} %collective-permute-done.5.refs_5_), channel_id=1, source_target_pairs={{0,8},{4,12},{8,0},{12,4},{1,9},{5,13},{9,1},{13,5},{2,10},{6,14},... | collective-permute-start | bytes 786440 | tf_op jit(solution)/shard_map/ppermute | solution.py:240
  20.1 11.0 %collective-permute-start.7 = (bf16[128,1024]{1,0:T(8,128)(2,1)S(1)}, bf16[128,1024]{1,0:T(8,128)(2,1)S(1)}, u32[]{:S(2)}, u32[]{:S(2)}) collective-permute-start(bf16[128,1024]{1,0:T(8,128)(2,1)S(1)} %collective-permute-done.5.refs_5_), channel_id=1, source_target_pairs={{0,1},{1,2},{2,3},{3,0},{4,5},{5,6},{6,7},{7,4},{8,9},{9,10},{10,1... | collective-permute-start | bytes 786440 | tf_op jit(solution)/shard_map/ppermute | solution.py:237
  25.5 7.5 %collective-permute-start.10 = (bf16[128,1024]{1,0:T(8,128)(2,1)S(1)}, bf16[128,1024]{1,0:T(8,128)(2,1)S(1)}, u32[]{:S(2)}, u32[]{:S(2)}) collective-permute-start(bf16[128,1024]{1,0:T(8,128)(2,1)S(1)} %collective-permute-done.2.refs_2_), channel_id=1, source_target_pairs={{0,8},{4,12},{8,0},{12,4},{1,9},{5,13},{9,1},{13,5},{2,10},{6,14},... | collective-permute-start | bytes 786440 | tf_op jit(solution)/shard_map/ppermute | solution.py:240
  25.8 11.0 %collective-permute-start.4 = (bf16[128,1024]{1,0:T(8,128)(2,1)S(1)}, bf16[128,1024]{1,0:T(8,128)(2,1)S(1)}, u32[]{:S(2)}, u32[]{:S(2)}) collective-permute-start(bf16[128,1024]{1,0:T(8,128)(2,1)S(1)} %collective-permute-done.2.refs_2_), channel_id=1, source_target_pairs={{0,1},{1,2},{2,3},{3,0},{4,5},{5,6},{6,7},{7,4},{8,9},{9,10},{10,1... | collective-permute-start | bytes 786440 | tf_op jit(solution)/shard_map/ppermute | solution.py:237
  25.9 26.0 %copy-start.2 = (s32[4]{0:T(128)S(1)}, s32[4]{0:T(128)}, u32[]{:S(2)}) copy-start(s32[4]{0:T(128)} %placement.1) | copy-start | bytes 52
  25.9 26.0 %copy-start.3 = (s32[2]{0:T(128)S(1)}, s32[2]{0:T(128)}, u32[]{:S(2)}) copy-start(s32[2]{0:T(128)} %lengths.1) | copy-start | bytes 28
  25.9 23.6 %collective-permute-start.15 = (bf16[128,4096]{1,0:T(8,128)(2,1)S(1)}, bf16[128,4096]{1,0:T(8,128)(2,1)S(1)}, u32[]{:S(2)}, u32[]{:S(2)}) collective-permute-start(bf16[128,4096]{1,0:T(8,128)(2,1)S(1)} %pad_maximum_fusion), channel_id=1, source_target_pairs={{0,4},{4,0},{8,12},{12,8},{1,5},{5,1},{9,13},{13,9},{2,6},{6,2},{1... | collective-permute-start | bytes 3145736 | tf_op jit(solution)/shard_map/ppermute | solution.py:243
  31.2 7.5 %collective-permute-start.12 = (bf16[128,1024]{1,0:T(8,128)(2,1)S(1)}, bf16[128,1024]{1,0:T(8,128)(2,1)S(1)}, u32[]{:S(2)}, u32[]{:S(2)}) collective-permute-start(bf16[128,1024]{1,0:T(8,128)(2,1)S(1)} %collective-permute-done.7.refs_6_), channel_id=1, source_target_pairs={{0,8},{4,12},{8,0},{12,4},{1,9},{5,13},{9,1},{13,5},{2,10},{6,14},... | collective-permute-start | bytes 786440 | tf_op jit(solution)/shard_map/ppermute | solution.py:240
  31.5 9.4 %collective-permute-start.9 = (bf16[128,1024]{1,0:T(8,128)(2,1)S(1)}, bf16[128,1024]{1,0:T(8,128)(2,1)S(1)}, u32[]{:S(2)}, u32[]{:S(2)}) collective-permute-start(bf16[128,1024]{1,0:T(8,128)(2,1)S(1)} %collective-permute-done.7.refs_6_), channel_id=1, source_target_pairs={{0,1},{1,2},{2,3},{3,0},{4,5},{5,6},{6,7},{7,4},{8,9},{9,10},{10,1... | collective-permute-start | bytes 786440 | tf_op jit(solution)/shard_map/ppermute | solution.py:237
  36.8 7.5 %collective-permute-start.11 = (bf16[128,1024]{1,0:T(8,128)(2,1)S(1)}, bf16[128,1024]{1,0:T(8,128)(2,1)S(1)}, u32[]{:S(2)}, u32[]{:S(2)}) collective-permute-start(bf16[128,1024]{1,0:T(8,128)(2,1)S(1)} %collective-permute-done.4.refs_3_), channel_id=1, source_target_pairs={{0,8},{4,12},{8,0},{12,4},{1,9},{5,13},{9,1},{13,5},{2,10},{6,14},... | collective-permute-start | bytes 786440 | tf_op jit(solution)/shard_map/ppermute | solution.py:240
  37.2 14.3 %collective-permute-start.16 = (bf16[128,4096]{1,0:T(8,128)(2,1)S(1)}, bf16[128,4096]{1,0:T(8,128)(2,1)S(1)}, u32[]{:S(2)}, u32[]{:S(2)}) collective-permute-start(bf16[128,4096]{1,0:T(8,128)(2,1)S(1)} %pad_maximum_fusion.1), channel_id=1, source_target_pairs={{0,4},{4,0},{8,12},{12,8},{1,5},{5,1},{9,13},{13,9},{2,6},{6,2},{1... | collective-permute-start | bytes 3145736 | tf_op jit(solution)/shard_map/ppermute | solution.py:243
  38.7 10.7 %collective-permute-start.14 = (bf16[128,2048]{1,0:T(8,128)(2,1)S(1)}, bf16[128,2048]{1,0:T(8,128)(2,1)S(1)}, u32[]{:S(2)}, u32[]{:S(2)}) collective-permute-start(bf16[128,2048]{1,0:T(8,128)(2,1)S(1)} %pad_maximum_fusion.2), channel_id=1, source_target_pairs={{0,4},{4,0},{8,12},{12,8},{1,5},{5,1},{9,13},{13,9},{2,6},{6,2},{1... | collective-permute-start | bytes 1572872 | tf_op jit(solution)/shard_map/ppermute | solution.py:243
  40.9 7.9 %collective-permute-start.13 = (bf16[128,1024]{1,0:T(8,128)(2,1)S(1)}, bf16[128,1024]{1,0:T(8,128)(2,1)S(1)}, u32[]{:S(2)}, u32[]{:S(2)}) collective-permute-start(bf16[128,1024]{1,0:T(8,128)(2,1)S(1)} %collective-permute-done.9.refs_7_), channel_id=1, source_target_pairs={{0,8},{4,12},{8,0},{12,4},{1,9},{5,13},{9,1},{13,5},{2,10},{6,14},... | collective-permute-start | bytes 786440 | tf_op jit(solution)/shard_map/ppermute | solution.py:240
  44.3 4.6 %collective-permute-start.19 = (bf16[128,1024]{1,0:T(8,128)(2,1)S(1)}, bf16[128,1024]{1,0:T(8,128)(2,1)S(1)}, u32[]{:S(2)}, u32[]{:S(2)}) collective-permute-start(bf16[128,1024]{1,0:T(8,128)(2,1)S(1)} %collective-permute-done.11.refs_11_), channel_id=1, source_target_pairs={{0,4},{4,0},{8,12},{12,8},{1,5},{5,1},{9,13},{13,9},{2,6},{6,2},{1... | collective-permute-start | bytes 786440 | tf_op jit(solution)/shard_map/ppermute | solution.py:243
  48.8 1.9 collective-permute-start.17
  48.9 2.7 %collective-permute-start.18 = (bf16[128,2048]{1,0:T(8,128)(2,1)S(1)}, bf16[128,2048]{1,0:T(8,128)(2,1)S(1)}, u32[]{:S(2)}, u32[]{:S(2)}) collective-permute-start(bf16[128,2048]{1,0:T(8,128)(2,1)S(1)} %pad_maximum_fusion.4), channel_id=1, source_target_pairs={{0,4},{4,0},{8,12},{12,8},{1,5},{5,1},{9,13},{13,9},{2,6},{6,2},{1... | collective-permute-start | bytes 1572872 | tf_op jit(solution)/shard_map/ppermute | solution.py:243
  49.4 2.5 %collective-permute-start.20 = (bf16[128,1024]{1,0:T(8,128)(2,1)S(1)}, bf16[128,1024]{1,0:T(8,128)(2,1)S(1)}, u32[]{:S(2)}, u32[]{:S(2)}) collective-permute-start(bf16[128,1024]{1,0:T(8,128)(2,1)S(1)} %collective-permute-done.13.refs_15_), channel_id=1, source_target_pairs={{0,4},{4,0},{8,12},{12,8},{1,5},{5,1},{9,13},{13,9},{2,6},{6,2},{1... | collective-permute-start | bytes 786440 | tf_op jit(solution)/shard_map/ppermute | solution.py:243
